TPU v7x, 128 devices: a whole 4x4x4 slice. The times are simulated.
128 devices in a mesh: row: 8 (over y, x_hi), col: 16 (over x_lo, z, core).
Axes of the slice: x: 4 (x_hi: 2, x_lo: 2; x = x_hi * 2 + x_lo), y: 4, z: 4, core: 2. Of those that a mesh axis runs over, the one named last changes fastest.
Arguments:
- features: float32 [32768, 256], P(('row', 'col')), may hold values from -6 to 6
- weight: float32 [256, 256], replicated, may hold values from -0.375 to 0.375
- tile_vals: float32 [16, 8, 256, 128, 128], P('col', 'row'), may hold values from 0 to 0.022097087
- tile_index: int32 [16, 8, 2, 256], P('col', 'row'), may hold values from 0 to 31, as said below
- tile_count: int32 [16, 8], P('col', 'row'), may hold values from 1 to 256, as said below
- out_grad: float32 [32768, 256], P(('col', 'row')), may hold values from -6 to 6
Outputs:
- hidden: float32 [32768, 256], P(('col', 'row'))
- grad_x: float32 [32768, 256], P(('row', 'col'))
- grad_w: float32 [256, 256], replicated
Inputs may be any that keep to these rules, and one draw needn't show every extreme that they name: For each device the first tile_count slots name distinct tiles; tile_index[c, r, 0, s] is below 16 and tile_index[c, r, 1, s] below 32. `tile_count`: exactly one device holds 256 tiles in every draw.
All inputs are finite; a program needn't handle non-finite values.
Results may differ from a plain program's by a relative error of at most 0.0003.
Values sent between devices are 32-bit elements; how exact they have to be, the bound alone decides.
No kernel may reach another device: no remote copies, remote signals or barrier semaphores. Data moves between devices by JAX's collectives and lax.ppermute only.
A program may use at most 128 MiB of HBM per device.

v0:
```python
import jax
import jax.numpy as jnp
from jax import lax
from jax.sharding import PartitionSpec as P

highest = lax.Precision.HIGHEST


def silu_slope(value):
    sigma = jax.nn.sigmoid(value)
    return sigma * (1.0 + value * (1.0 - sigma))


def aggregate(
    slot_tiles, take_idx, put_idx, live_count, source, out_tiles, flipped, rounds, slot_group
):
    tile_edge = slot_tiles.shape[-1]
    feat_width = source.shape[-1]
    src_count = source.shape[0] // tile_edge
    src_flat = source.reshape(src_count, tile_edge * feat_width)
    einsum_form = "sji,sjf->sif" if flipped else "sij,sjf->sif"
    src_range = jnp.arange(src_count, dtype=jnp.int32)
    out_range = jnp.arange(out_tiles, dtype=jnp.int32)
    group_range = jnp.arange(slot_group, dtype=jnp.int32)

    def one_group(turn_index, summed):
        first_slot = turn_index * slot_group
        slot_piece = lax.dynamic_slice_in_dim(slot_tiles, first_slot, slot_group, 0)
        take_piece = lax.dynamic_slice_in_dim(take_idx, first_slot, slot_group, 0)
        put_piece = lax.dynamic_slice_in_dim(put_idx, first_slot, slot_group, 0)
        live_mask = (first_slot + group_range < live_count).astype(jnp.float32)
        take_hot = (take_piece[:, None] == src_range[None, :]).astype(jnp.float32)
        picked = jnp.dot(take_hot, src_flat, precision=highest, preferred_element_type=jnp.float32)
        picked = picked.reshape(slot_group, tile_edge, feat_width)
        products = jnp.einsum(
            einsum_form, slot_piece, picked, precision=highest, preferred_element_type=jnp.float32
        )
        put_hot = (out_range[:, None] == put_piece[None, :]).astype(jnp.float32) * live_mask[
            None, :
        ]
        placed = jnp.dot(
            put_hot,
            products.reshape(slot_group, tile_edge * feat_width),
            precision=highest,
            preferred_element_type=jnp.float32,
        )
        return summed + placed

    summed = jnp.zeros((out_tiles, tile_edge * feat_width), jnp.float32)
    summed = lax.fori_loop(0, rounds, one_group, summed)
    return summed.reshape(out_tiles * tile_edge, feat_width)


def body(features, weight, tile_vals, tile_index, tile_count, out_grad):
    slot_tiles = tile_vals[0, 0]
    dest_idx = tile_index[0, 0, 0]
    src_idx = tile_index[0, 0, 1]
    live_count = tile_count[0, 0]
    tile_edge = slot_tiles.shape[-1]
    rows_here = features.shape[0]
    dest_tiles = rows_here * lax.axis_size("row") // tile_edge
    src_tiles = rows_here * lax.axis_size("col") // tile_edge
    node_total = rows_here * lax.axis_size("row") * lax.axis_size("col")
    slot_group = min(slot_tiles.shape[0], 32)
    rounds = slot_tiles.shape[0] // slot_group
    projected = jnp.dot(features, weight, precision=highest, preferred_element_type=jnp.float32)
    source = lax.all_gather(projected, "col", axis=0, tiled=True)
    partial_value = aggregate(
        slot_tiles, src_idx, dest_idx, live_count, source, dest_tiles, False, rounds, slot_group
    )
    pre_act = lax.psum_scatter(partial_value, "row", scatter_dimension=0, tiled=True)
    hidden = pre_act * jax.nn.sigmoid(pre_act)
    grad_pre = out_grad * silu_slope(pre_act)
    grad_block = lax.all_gather(grad_pre, "row", axis=0, tiled=True)
    proj_terms = aggregate(
        slot_tiles, dest_idx, src_idx, live_count, grad_block, src_tiles, True, rounds, slot_group
    )
    grad_proj = lax.psum_scatter(proj_terms, "col", scatter_dimension=0, tiled=True)
    grad_x = jnp.dot(grad_proj, weight.T, precision=highest, preferred_element_type=jnp.float32)
    weight_term = jnp.dot(
        features.T, grad_proj, precision=highest, preferred_element_type=jnp.float32
    )
    grad_w = lax.psum(weight_term, ("row", "col"))
    grad_w = grad_w * node_total ** (-0.5)
    return (hidden, grad_x, grad_w)


def solution(mesh):
    placed = (
        P(("row", "col"), None),
        P(),
        P("col", "row", None, None, None),
        P("col", "row", None, None),
        P("col", "row"),
        P(("col", "row"), None),
    )
    return jax.shard_map(
        body,
        mesh=mesh,
        in_specs=placed,
        out_specs=(P(("col", "row"), None), P(("row", "col"), None), P()),
        check_vma=False,
    )
```

profile of v0, /device:TPU:0, one launch (start us, length us, event | category | flops | bytes accessed | tf_op | source)
XLA Modules:
  0.0 758.9 jit_solution(6811864648708813243)
XLA Ops:
  11.0 39.2 %all-gather.3.cloned.1.call-done = f32[4096,256]{1,0:T(8,128)} async-done(((f32[256,256]{1,0:T(8,128)}), f32[4096,256]{1,0:T(8,128)}) %all-gather.3.cloned.1.call-update) | async-done | bytes 4194320 | tf_op jit(solution)/shard_map/all_gather | solution.py:67
  55.2 162.7 %while.32 = (s32[]{:T(128)}, f32[16,32768]{1,0:T(8,128)S(1)}, s32[256]{0:T(256)S(1)}, s32[]{:T(128)}, f32[256,128,128]{2,1,0:T(8,128)}, /*index=5*/s32[256]{0:T(...) while((s32[]{:T(128)}, f32[16,32768]{1,0:T(8,128)S(1)}, ...), condition=%wide.region_1.0_spmd.clone.clone, body=%wide.region_0.0_spmd.clone.clone.sunk | while | flops 2215643136 | bytes 44041404 | solution.py:50
  60.9 5.4 fusion.64
  81.2 5.4 fusion.64
  101.6 5.4 fusion.64
  121.9 5.4 fusion.64
  142.2 5.4 fusion.64
  162.6 5.4 fusion.64
  182.9 5.4 fusion.64
  203.3 5.4 fusion.64
  219.5 75.0 %reduce-scatter.3.cloned.1.call-done = f32[256,256]{1,0:T(8,128)} async-done(((f32[2048,256]{1,0:T(8,128)}), f32[256,256]{1,0:T(8,128)}) %reduce-scatter.3.cloned.1.call-update) | async-done | bytes 262160 | tf_op jit(solution)/shard_map/reduce_scatter | solution.py:71
  296.5 17.5 %copy.9 = f32[1,1,256,128,128]{3,4,2,1,0:T(8,128)} copy(f32[1,1,256,128,128]{4,3,2,1,0:T(8,128)} %bitcast.64) | data formatting | bytes 33554432 | tf_op args[2]
  313.9 36.3 %all-gather.5.cloned.1.call-done = f32[2048,256]{1,0:T(8,128)} async-done(((f32[256,256]{1,0:T(8,128)}), f32[2048,256]{1,0:T(8,128)}) %all-gather.5.cloned.1.call-update) | async-done | bytes 2097168 | tf_op jit(solution)/shard_map/all_gather | solution.py:74
  352.0 183.0 %while.33 = (s32[]{:T(128)}, f32[32,32768]{1,0:T(8,128)}, s32[256]{0:T(256)S(1)}, s32[]{:T(128)}, f32[256,128,128]{1,2,0:T(8,128)}, /*index=5*/s32[256]{0:T(256)...) while((s32[]{:T(128)}, f32[32,32768]{1,0:T(8,128)}, ...), condition=%wide.region_4.0_spmd.clone.clone, body=%wide.region_3.0_spmd.clone.clone.sunk | while | flops 2216692224 | bytes 46138556 | solution.py:50
  355.4 5.4 fusion.71
  366.0 7.9 %convolution_add_fusion.5 = f32[32,32768]{1,0:T(8,128)} fusion(f32[32,32768]{1,0:T(8,128)} %bitcast.56, f32[32,32768]{1,0:T(8,128)} %get-tuple-element.644, pred[]{:T(512)S(6)} %compare.7, f32[32]{0:T(128)S(1)} %compare_convert_fusion.5, s32[32]{0:T(128)S(1)} %dynamic_slice.75), kind=kOutput, calls=%fused_computation.19.clone.1 | convolution fusion | flops 404752384 | bytes 12583169 | tf_op jit(solution)/shard_map/while/body/eval_jaxpr/dot_general | solution.py:41
  377.1 5.4 fusion.71
  387.7 9.2 %convolution_add_fusion.5 = f32[32,32768]{1,0:T(8,128)} fusion(f32[32,32768]{1,0:T(8,128)} %bitcast.56, f32[32,32768]{1,0:T(8,128)} %get-tuple-element.644, pred[]{:T(512)S(6)} %compare.7, f32[32]{0:T(128)S(1)} %compare_convert_fusion.5, s32[32]{0:T(128)S(1)} %dynamic_slice.75), kind=kOutput, calls=%fused_computation.19.clone.1 | convolution fusion | flops 404752384 | bytes 12583169 | tf_op jit(solution)/shard_map/while/body/eval_jaxpr/dot_general | solution.py:41
  400.1 5.4 fusion.71
  410.7 9.2 %convolution_add_fusion.5 = f32[32,32768]{1,0:T(8,128)} fusion(f32[32,32768]{1,0:T(8,128)} %bitcast.56, f32[32,32768]{1,0:T(8,128)} %get-tuple-element.644, pred[]{:T(512)S(6)} %compare.7, f32[32]{0:T(128)S(1)} %compare_convert_fusion.5, s32[32]{0:T(128)S(1)} %dynamic_slice.75), kind=kOutput, calls=%fused_computation.19.clone.1 | convolution fusion | flops 404752384 | bytes 12583169 | tf_op jit(solution)/shard_map/while/body/eval_jaxpr/dot_general | solution.py:41
  423.1 5.4 fusion.71
  433.7 9.2 %convolution_add_fusion.5 = f32[32,32768]{1,0:T(8,128)} fusion(f32[32,32768]{1,0:T(8,128)} %bitcast.56, f32[32,32768]{1,0:T(8,128)} %get-tuple-element.644, pred[]{:T(512)S(6)} %compare.7, f32[32]{0:T(128)S(1)} %compare_convert_fusion.5, s32[32]{0:T(128)S(1)} %dynamic_slice.75), kind=kOutput, calls=%fused_computation.19.clone.1 | convolution fusion | flops 404752384 | bytes 12583169 | tf_op jit(solution)/shard_map/while/body/eval_jaxpr/dot_general | solution.py:41
  446.1 5.4 fusion.71
  456.7 9.2 %convolution_add_fusion.5 = f32[32,32768]{1,0:T(8,128)} fusion(f32[32,32768]{1,0:T(8,128)} %bitcast.56, f32[32,32768]{1,0:T(8,128)} %get-tuple-element.644, pred[]{:T(512)S(6)} %compare.7, f32[32]{0:T(128)S(1)} %compare_convert_fusion.5, s32[32]{0:T(128)S(1)} %dynamic_slice.75), kind=kOutput, calls=%fused_computation.19.clone.1 | convolution fusion | flops 404752384 | bytes 12583169 | tf_op jit(solution)/shard_map/while/body/eval_jaxpr/dot_general | solution.py:41
  469.1 5.4 fusion.71
  479.7 9.2 %convolution_add_fusion.5 = f32[32,32768]{1,0:T(8,128)} fusion(f32[32,32768]{1,0:T(8,128)} %bitcast.56, f32[32,32768]{1,0:T(8,128)} %get-tuple-element.644, pred[]{:T(512)S(6)} %compare.7, f32[32]{0:T(128)S(1)} %compare_convert_fusion.5, s32[32]{0:T(128)S(1)} %dynamic_slice.75), kind=kOutput, calls=%fused_computation.19.clone.1 | convolution fusion | flops 404752384 | bytes 12583169 | tf_op jit(solution)/shard_map/while/body/eval_jaxpr/dot_general | solution.py:41
  492.1 5.4 fusion.71
  502.7 9.2 %convolution_add_fusion.5 = f32[32,32768]{1,0:T(8,128)} fusion(f32[32,32768]{1,0:T(8,128)} %bitcast.56, f32[32,32768]{1,0:T(8,128)} %get-tuple-element.644, pred[]{:T(512)S(6)} %compare.7, f32[32]{0:T(128)S(1)} %compare_convert_fusion.5, s32[32]{0:T(128)S(1)} %dynamic_slice.75), kind=kOutput, calls=%fused_computation.19.clone.1 | convolution fusion | flops 404752384 | bytes 12583169 | tf_op jit(solution)/shard_map/while/body/eval_jaxpr/dot_general | solution.py:41
  515.1 5.4 fusion.71
  525.7 9.2 %convolution_add_fusion.5 = f32[32,32768]{1,0:T(8,128)} fusion(f32[32,32768]{1,0:T(8,128)} %bitcast.56, f32[32,32768]{1,0:T(8,128)} %get-tuple-element.644, pred[]{:T(512)S(6)} %compare.7, f32[32]{0:T(128)S(1)} %compare_convert_fusion.5, s32[32]{0:T(128)S(1)} %dynamic_slice.75), kind=kOutput, calls=%fused_computation.19.clone.1 | convolution fusion | flops 404752384 | bytes 12583169 | tf_op jit(solution)/shard_map/while/body/eval_jaxpr/dot_general | solution.py:41
  539.9 65.1 %reduce-scatter.5.cloned.1.call-done = f32[256,256]{1,0:T(8,128)} async-done(((f32[4096,256]{1,0:T(8,128)}), f32[256,256]{1,0:T(8,128)}) %reduce-scatter.5.cloned.1.call-update) | async-done | bytes 262160 | tf_op jit(solution)/shard_map/reduce_scatter | solution.py:78
  609.3 141.2 %all-reduce.2.cloned.1.call-done = f32[256,256]{0,1:T(8,128)} async-done(((f32[256,256]{0,1:T(8,128)}), f32[256,256]{0,1:T(8,128)}) %all-reduce.2.cloned.1.call-update) | async-done | bytes 262160 | tf_op jit(solution)/shard_map/psum | solution.py:83
  (133 shorter events, 210.5 us)
Async XLA Ops:
  7.2 1.0 copy-start
  7.2 43.0 %all-gather.3.cloned.1.call-start = ((), (), s32[]{:S(2)}) async-start(), calls=%async_computation.2 | async-start | bytes 4456448 | tf_op jit(solution)/shard_map/all_gather | solution.py:67
  10.2 284.3 %reduce-scatter.3.cloned.1.call-start = ((), (), s32[]{:S(2)}) async-start(), calls=%async_computation.3 | async-start | bytes 2359296 | tf_op jit(solution)/shard_map/reduce_scatter | solution.py:71
  217.9 76.6 %copy-start.2 = (f32[256,256]{1,0:T(8,128)S(1)}, f32[256,256]{1,0:T(8,128)}, u32[]{:S(2)}) copy-start(f32[256,256]{1,0:T(8,128)} %param.15) | copy-start | bytes 786436
  219.5 130.7 %all-gather.5.cloned.1.call-start = ((), (), s32[]{:S(2)}) async-start(), calls=%async_computation.4 | async-start | bytes 2359296 | tf_op jit(solution)/shard_map/all_gather | solution.py:74
  296.4 308.6 %reduce-scatter.5.cloned.1.call-start = ((), (), s32[]{:S(2)}) async-start(), calls=%async_computation.5 | async-start | bytes 4456448 | tf_op jit(solution)/shard_map/reduce_scatter | solution.py:78
  539.8 67.4 %copy-start.1 = (f32[256,256]{1,0:T(8,128)S(1)}, f32[256,256]{1,0:T(8,128)}, u32[]{:S(2)}) copy-start(f32[256,256]{1,0:T(8,128)} %param.11) | copy-start | bytes 786436
  539.8 210.7 %all-reduce.2.cloned.1.call-start = ((), (), s32[]{:S(2)}) async-start(), calls=%async_computation.6 | async-start | bytes 524288 | tf_op jit(solution)/shard_map/psum | solution.py:83
Sparse Core Ops, SparseCore 0:
  10.3 39.8 all-gather.2
  219.6 74.8 reduce-scatter.2
  297.4 52.7 all-gather.4
  540.0 64.9 reduce-scatter.4
  610.1 140.3 all-reduce.1
where the time goes:
time: 761 us; the launch traced here: 759 us
  waiting for transfers between devices  357 us (47%)
  matrix products  247 us (32%)
  local copies, waits for them, and re-layouts  127 us (17%)
  between operations  13.8 us (2%)
  other arithmetic  13.2 us (2%)
    psum x1, waiting for transfers between devices, body(): grad_w = lax.psum(weight_term, ('row', 'col'))  141 us
    dot_general x16, matrix products, one_group(): jnp.dot(put_hot, products.reshape(slot_group, tile_edge * feat_width), pr...  105 us
    while x32, local copies, waits for them, and re-layouts  91 us
    dot_general x16, matrix products, one_group(): jnp.einsum(einsum_form, slot_piece, picked, precision=highest, preferred_...  87 us
    reduce_scatter x1, waiting for transfers between devices, body(): lax.psum_scatter(partial_value, 'row', scatter_dimension=0, tiled=True)  75 us
    reduce_scatter x1, waiting for transfers between devices, body(): lax.psum_scatter(proj_terms, 'col', scatter_dimension=0, tiled=True)  65.1 us
    dot_general x16, matrix products, one_group(): jnp.dot(take_hot, src_flat, precision=highest, preferred_element_type=jnp...  49.3 us
    all_gather x1, waiting for transfers between devices, body(): source = lax.all_gather(projected, 'col', axis=0, tiled=True)  39.2 us
  transfers between devices with their start and end apart: 5, of which 5 were waited for; matrix products, arithmetic and copies ran while one was open for 3% of the time, Pallas kernels for 0%

commit v1 on v0

v1 whole, which is shorter than its diff:
```python
import functools

import jax
import jax.numpy as jnp
from jax import lax
from jax.experimental import pallas as pl
from jax.experimental.pallas import tpu as pltpu
from jax.sharding import Mesh
from jax.sharding import PartitionSpec as P

EDGE = 128
GROUP = 64
UNROLL = 32
ROW_AXES = ("y", "xh")
COL_AXES = ("xl", "z", "core")
PLANE_AXES = ("xl", "z")
VMEM_LIMIT = 48 << 20


def split(value):
    high = value.astype(jnp.bfloat16)
    low = (value - high.astype(jnp.float32)).astype(jnp.bfloat16)
    return high, low


def dot3(left, right, dims=((1,), (0,))):
    dot = functools.partial(
        lax.dot_general, dimension_numbers=(dims, ((), ())), preferred_element_type=jnp.float32
    )
    left_high, left_low = split(left)
    right_high, right_low = split(right)
    return dot(left_high, right_high) + (dot(left_high, right_low) + dot(left_low, right_high))


def spread_body(flipped, n_src, take, put, count, tiles, *refs):
    sources, (outs, (paired, total)) = refs[:n_src], (refs[n_src:-2], refs[-2:])
    step = pl.program_id(0)

    @pl.when(step == 0)
    def _():
        total[...] = jnp.zeros_like(total)
        place = 0
        for source in sources:

            def pair(index, carry, source=source, place=place):
                high, low = split(source[index])
                paired[place + index, :EDGE, :EDGE] = high
                paired[place + index, :EDGE, EDGE:] = low
                paired[place + index, EDGE:, :EDGE] = high
                paired[place + index, EDGE:, EDGE:] = jnp.zeros_like(low)
                return carry

            lax.fori_loop(0, source.shape[0], pair, 0)
            place += source.shape[0]

    first = step * GROUP

    def one(slot):
        tile = tiles[slot]
        high, low = split(tile.T if flipped else tile)
        both = jnp.dot(
            jnp.concatenate([high, low], axis=1),
            paired[take[first + slot]],
            preferred_element_type=jnp.float32,
        )
        where = put[first + slot]
        total[where] += both[:, :EDGE] + both[:, EDGE:]

    live = jnp.clip(count[0] - first, 0, GROUP)
    blocks = live // UNROLL

    def block(index, carry):
        for offset in range(UNROLL):
            one(index * UNROLL + offset)
        return carry

    def rest(slot, carry):
        one(slot)
        return carry

    lax.fori_loop(0, blocks, block, 0)
    lax.fori_loop(blocks * UNROLL, live, rest, 0)

    @pl.when(step == pl.num_programs(0) - 1)
    def _():
        place = 0
        for out in outs:
            out[...] = total[place : place + out.shape[0]]
            place += out.shape[0]


def spread(tiles, take, put, count, sources, out_counts, flipped, name):
    slots = tiles.shape[0]
    src_count = sum(source.shape[0] for source in sources)
    whole = lambda *unused: (0, 0, 0)
    return pl.pallas_call(
        functools.partial(spread_body, flipped, len(sources)),
        grid_spec=pltpu.PrefetchScalarGridSpec(
            num_scalar_prefetch=3,
            grid=(slots // GROUP,),
            in_specs=[
                pl.BlockSpec(
                    (GROUP, EDGE, EDGE),
                    lambda g, take, put, count: (jnp.minimum(g, (count[0] - 1) // GROUP), 0, 0),
                )
            ]
            + [pl.BlockSpec(source.shape, whole) for source in sources],
            out_specs=[pl.BlockSpec((n, EDGE, EDGE), whole) for n in out_counts],
            scratch_shapes=[
                pltpu.VMEM((src_count, 2 * EDGE, 2 * EDGE), jnp.bfloat16),
                pltpu.VMEM((sum(out_counts), EDGE, EDGE), jnp.float32),
            ],
        ),
        out_shape=[jax.ShapeDtypeStruct((n, EDGE, EDGE), jnp.float32) for n in out_counts],
        compiler_params=pltpu.CompilerParams(vmem_limit_bytes=VMEM_LIMIT),
        cost_estimate=pl.CostEstimate(
            flops=2 * slots * EDGE * 4 * EDGE * EDGE,
            bytes_accessed=slots * EDGE * EDGE * 4,
            transcendentals=0,
        ),
        name=name,
    )(take, put, count, tiles, *sources)


def middle_body(terms0, terms1, weight, out_grad, hidden, grad0, grad1, gathered, grad_pre):
    parts = [jnp.sum(terms[...], axis=0) for terms in (terms0, terms1)]
    mixed = jnp.concatenate(parts, axis=1)
    gathered[...] = mixed
    pre_act = dot3(mixed, weight[...])
    sigma = jax.nn.sigmoid(pre_act)
    hidden[...] = pre_act * sigma
    slope = sigma * (1.0 + pre_act * (1.0 - sigma))
    local = out_grad[...] * slope
    grad_pre[...] = local
    back = dot3(local, weight[...], ((1,), (1,)))
    grad0[...] = back[:, :EDGE]
    grad1[...] = back[:, EDGE:]


def middle(terms0, terms1, weight, out_grad):
    rows, width = out_grad.shape
    full = jax.ShapeDtypeStruct((rows, width), jnp.float32)
    half = jax.ShapeDtypeStruct((rows, EDGE), jnp.float32)
    return pl.pallas_call(
        middle_body,
        out_shape=[full, half, half, full, full],
        compiler_params=pltpu.CompilerParams(vmem_limit_bytes=VMEM_LIMIT),
        name="middle",
    )(terms0, terms1, weight, out_grad)


def weight_body(gathered, grad_pre, out):
    out[...] = dot3(gathered[...], grad_pre[...], ((0,), (0,)))


def exchange(value, axes):
    return lax.all_to_all(value, axes, 0, 0, tiled=True)


def copies(value, count):
    return jnp.broadcast_to(value[None], (count, *value.shape))


def swap_core(value):
    return lax.ppermute(value, "core", [(0, 1), (1, 0)])


def body(features, weight, tile_vals, tile_index, tile_count, out_grad):
    tiles = tile_vals[0, 0]
    dest = tile_index[0, 0, 0]
    src = tile_index[0, 0, 1]
    count = tile_count[0]
    n_row = lax.axis_size(ROW_AXES)
    n_col = lax.axis_size(COL_AXES)
    n_plane = lax.axis_size(PLANE_AXES)
    rows, width = features.shape
    per = rows // EDGE
    half_tiles = n_plane * per
    src = (
        (((src // per) % 2) ^ lax.axis_index("core")) * half_tiles
        + (src // (2 * per)) * per
        + src % per
    ).astype(jnp.int32)

    def tiled(value):
        return value.reshape(-1, EDGE, EDGE)

    received = []
    for chunk in range(2):
        part = features[:, chunk * EDGE : (chunk + 1) * EDGE]
        received.append(exchange(copies(part, n_plane), PLANE_AXES))
    terms = []
    for chunk in range(2):
        mine = received[chunk]
        other = swap_core(mine)
        (partial,) = spread(
            tiles, src, dest, count, [tiled(mine), tiled(other)], [n_row * per], False, f"forward{chunk}"
        )
        terms.append(exchange(partial.reshape(n_row, rows, EDGE), ROW_AXES))
    hidden, grad0, grad1, gathered, grad_pre = middle(terms[0], terms[1], weight, out_grad)

    received = [exchange(copies(grad, n_row), ROW_AXES) for grad in (grad0, grad1)]
    weight_term = pl.pallas_call(
        weight_body,
        out_shape=jax.ShapeDtypeStruct((width, width), jnp.float32),
        name="weight_term",
    )(gathered, grad_pre)
    pieces = exchange(weight_term.reshape(n_row, width // n_row, width), ROW_AXES)
    piece = jnp.sum(pieces, axis=0)
    pieces = exchange(copies(piece, n_col), COL_AXES)
    piece = jnp.sum(pieces, axis=0)
    grad_w = exchange(copies(piece, n_row), ROW_AXES).reshape(width, width)
    nodes = rows * n_row * n_col
    grad_w = grad_w * nodes ** (-0.5)

    grads = []
    for chunk in range(2):
        mine, other = spread(
            tiles,
            dest,
            src,
            count,
            [tiled(received[chunk])],
            [half_tiles, half_tiles],
            True,
            f"backward{chunk}",
        )
        share = mine + swap_core(other)
        arrived = exchange(share.reshape(n_plane, rows, EDGE), PLANE_AXES)
        grads.append(jnp.sum(arrived, axis=0))
    grad_x = jnp.concatenate(grads, axis=1)
    return hidden, grad_x, grad_w


def solution(mesh):
    chips = Mesh(mesh.devices.reshape(4, 2, 2, 4, 2), ROW_AXES + COL_AXES)
    placed = (
        P(ROW_AXES + COL_AXES, None),
        P(),
        P(COL_AXES, ROW_AXES, None, None, None),
        P(COL_AXES, ROW_AXES, None, None),
        P(COL_AXES, ROW_AXES),
        P(COL_AXES + ROW_AXES, None),
    )
    return jax.shard_map(
        body,
        mesh=chips,
        in_specs=placed,
        out_specs=(P(COL_AXES + ROW_AXES, None), P(ROW_AXES + COL_AXES, None), P()),
        check_vma=False,
    )
```

time: 761 us -> 229 us (0.30)
  waiting for transfers between devices: 357 us -> 58.5 us
  matrix products: 247 us -> 0 us
  local copies, waits for them, and re-layouts: 127 us -> 7.09 us
  blocking collectives: 0 us -> 89.3 us
  Pallas kernels: 0 us -> 31.9 us
  starting transfers between devices: 0.21 us -> 31.9 us
  between operations: 13.8 us -> 1.39 us
    dot_general x51 -> x0, matrix products: 247 us -> none  [the longest x16 105 us: one_group(): jnp.dot(put_hot, products.reshape(slot_group, tile_edge * feat_width), pr...]
    psum x1 -> x0, waiting for transfers between devices: 141 us -> none  [body(): grad_w = lax.psum(weight_term, ('row', 'col'))]
    reduce_scatter x2 -> x0, waiting for transfers between devices: 140 us -> none  [the longest x1 75 us: body(): lax.psum_scatter(partial_value, 'row', scatter_dimension=0, tiled=True)]
    while x32 -> x0, local copies, waits for them, and re-layouts: 91 us -> none
    all_to_all x0 -> x5, blocking collectives: none -> 89.3 us  [exchange(): return lax.all_to_all(value, axes, 0, 0, tiled=True)]
    all_gather x2 -> x0, waiting for transfers between devices: 75.5 us -> none  [the longest x1 39.2 us: body(): source = lax.all_gather(projected, 'col', axis=0, tiled=True)]
    all_to_all x0 -> x6, waiting for transfers between devices: none -> 58.5 us  [exchange(): return lax.all_to_all(value, axes, 0, 0, tiled=True)]
    pallas_call x0 -> x6, Pallas kernels: none -> 31.9 us  [the longest x4 28.7 us: spread(): pl.pallas_call(functools.partial(spread_body, flipped, len(sources)), gri...]
  transfers between devices with their start and end apart: 5 -> 10, of which waited for: 5 -> 5; matrix products, arithmetic and copies ran while one was open for 3% -> 3% of each run, Pallas kernels for 0% -> 13%
where the time goes in v1:
time: 229 us; the launch traced here: 226 us
  blocking collectives  89.3 us (39%)
  waiting for transfers between devices  58.5 us (26%)
  starting transfers between devices  31.9 us (14%)
  Pallas kernels  31.9 us (14%)
  local copies, waits for them, and re-layouts  7.09 us (3%)
  other arithmetic  6.14 us (3%)
    all_to_all x5, blocking collectives, exchange(): return lax.all_to_all(value, axes, 0, 0, tiled=True)  89.3 us
    all_to_all x6, waiting for transfers between devices, exchange(): return lax.all_to_all(value, axes, 0, 0, tiled=True)  58.5 us
    all_to_all x6, starting transfers between devices, exchange(): return lax.all_to_all(value, axes, 0, 0, tiled=True)  31.4 us
    pallas_call x4, Pallas kernels, spread(): pl.pallas_call(functools.partial(spread_body, flipped, len(sources)), gri...  28.7 us
  transfers between devices with their start and end apart: 10, of which 5 were waited for; matrix products, arithmetic and copies ran while one was open for 3% of the time, Pallas kernels for 13%

profile of v1, /device:TPU:0, one launch (start us, length us, event | category | flops | bytes accessed | tf_op | source)
XLA Modules:
  0.0 226.3 jit_solution(9686789256395556124)
XLA Ops:
  0.6 1.0 fusion.5
  1.7 21.9 %all_to_all.55 = f32[8,256,128]{2,1,0:T(8,128)S(1)} all-to-all(f32[8,256,128]{2,1,0:T(8,128)S(1)} %broadcast_in_dim.13), channel_id=1, replica_groups=mesh['y'=4,'xh'=2,'xl'=2,'z'=4,'core'=2] {'xl','z'}, dimensions={0} | all-to-all | bytes 2097152 | tf_op jit(solution)/shard_map/all_to_all | solution.py:157
  23.6 1.0 broadcast_in_dim.12
  24.6 3.6 %all-to-all-start = ((f32[8,256,128]{2,1,0:T(8,128)}), f32[8,256,128]{2,1,0:T(8,128)S(1)}, u32[]{:S(2)}, u32[]{:S(2)}) async-start(f32[8,256,128]{2,1,0:T(8,128)} %broadcast_in_dim.12), calls=%async_computation | async-start | bytes 2097152 | tf_op jit(solution)/shard_map/all_to_all | solution.py:157
  28.9 0.8 fusion.6
  29.7 11.7 %all-to-all-done = f32[8,256,128]{2,1,0:T(8,128)S(1)} async-done(((f32[8,256,128]{2,1,0:T(8,128)}), f32[8,256,128]{2,1,0:T(8,128)S(1)}, u32[]{:S(2)}, u32[]{:S(2)}) %all-to-all-start) | async-done | bytes 1048608 | tf_op jit(solution)/shard_map/all_to_all | solution.py:157
  41.5 7.1 %forward1.1 = f32[16,128,128]{2,1,0:T(8,128)} custom-call(s32[256]{0:T(256)S(1)} %fusion.3.take.put, s32[256]{0:T(256)S(1)} %bitcast.26, s32[1]{0:T(128)} %bitcast.17.count, f32[256,128,128]{2,1,0:T(8,128)} %bitcast.30, f32[16,128,128]{2,1,0:T(8,128)S(1)} %bitcast.21, f32[16,128,128]{2,1,0:T(8,128)S(1)} %bitcast.25), custom_call_target="tpu_custom_call" | custom-call | flops 4294967296 | bytes 16777216 | tf_op jit(solution)/shard_map/forward1/pallas_call | solution.py:96
  48.6 8.4 %all-to-all-start.3 = ((f32[8,256,128]{2,1,0:T(8,128)}), f32[8,256,128]{2,1,0:T(8,128)S(1)}, u32[]{:S(2)}, u32[]{:S(2)}) async-start(f32[8,256,128]{2,1,0:T(8,128)} %bitcast.9), calls=%async_computation.3 | async-start | bytes 2097152 | tf_op jit(solution)/shard_map/all_to_all | solution.py:157
  57.0 6.4 %forward0.1 = f32[16,128,128]{2,1,0:T(8,128)S(1)} custom-call(s32[256]{0:T(256)S(1)} %fusion.3.take.put, s32[256]{0:T(256)S(1)} %bitcast.27, s32[1]{0:T(128)} %bitcast.16.count, f32[256,128,128]{2,1,0:T(8,128)} %bitcast.31, f32[16,128,128]{2,1,0:T(8,128)S(1)} %bitcast.20, f32[16,128,128]{2,1,0:T(8,128)} %bitcast.5.refs_1_), custom_call_target="tpu_custom_call" | custom-call | flops 4294967296 | bytes 16777216 | tf_op jit(solution)/shard_map/forward0/pallas_call | solution.py:96
  63.5 11.6 %all-to-all-done.3.terms1 = f32[8,256,128]{2,1,0:T(8,128)S(1)} async-done(((f32[8,256,128]{2,1,0:T(8,128)}), f32[8,256,128]{2,1,0:T(8,128)S(1)}, u32[]{:S(2)}, u32[]{:S(2)}) %all-to-all-start.3) | async-done | bytes 1048608 | tf_op jit(solution)/shard_map/all_to_all | solution.py:157
  75.1 20.5 %all_to_all.56.terms0 = f32[8,256,128]{2,1,0:T(8,128)S(1)} all-to-all(f32[8,256,128]{2,1,0:T(8,128)S(1)} %bitcast.24), channel_id=1, replica_groups=mesh['y'=4,'xh'=2,'xl'=2,'z'=4,'core'=2] {'y','xh'}, dimensions={0} | all-to-all | bytes 2097152 | tf_op jit(solution)/shard_map/all_to_all | solution.py:157
  95.6 0.9 copy-done.1
  96.5 1.2 middle.1
  99.1 2.0 weight_term.1
  101.1 12.1 %all_to_all.57 = f32[8,32,256]{2,1,0:T(8,128)S(1)} all-to-all(f32[8,32,256]{2,1,0:T(8,128)} %bitcast.34), channel_id=1, replica_groups=mesh['y'=4,'xh'=2,'xl'=2,'z'=4,'core'=2] {'y','xh'}, dimensions={0} | all-to-all | bytes 524288 | tf_op jit(solution)/shard_map/all_to_all | solution.py:157
  113.3 15.3 %all_to_all.58 = f32[16,32,256]{2,1,0:T(8,128)} all-to-all(f32[16,32,256]{2,1,0:T(8,128)S(1)} %broadcast_in_dim.16), channel_id=1, replica_groups=mesh['y'=4,'xh'=2,'xl'=2,'z'=4,'core'=2] {'xl','z','core'}, dimensions={0} | all-to-all | bytes 1048576 | tf_op jit(solution)/shard_map/all_to_all | solution.py:157
  128.7 19.5 %all_to_all.59 = f32[8,256,128]{2,1,0:T(8,128)S(1)} all-to-all(f32[8,256,128]{2,1,0:T(8,128)S(1)} %broadcast_in_dim.14), channel_id=1, replica_groups=mesh['y'=4,'xh'=2,'xl'=2,'z'=4,'core'=2] {'y','xh'}, dimensions={0} | all-to-all | bytes 2097152 | tf_op jit(solution)/shard_map/all_to_all | solution.py:157
  148.3 1.0 broadcast_in_dim.15
  149.3 3.6 %all-to-all-start.6 = ((f32[8,256,128]{2,1,0:T(8,128)}), f32[8,256,128]{2,1,0:T(8,128)S(1)}, u32[]{:S(2)}, u32[]{:S(2)}) async-start(f32[8,256,128]{2,1,0:T(8,128)} %broadcast_in_dim.15), calls=%async_computation.6 | async-start | bytes 2097152 | tf_op jit(solution)/shard_map/all_to_all | solution.py:157
  152.9 7.6 %backward0.1 = (f32[16,128,128]{2,1,0:T(8,128)S(1)}, f32[16,128,128]{2,1,0:T(8,128)}) custom-call(s32[256]{0:T(256)S(1)} %bitcast.28, s32[256]{0:T(256)S(1)} %fusion.3.take.put, s32[1]{0:T(128)} %bitcast.18.count, f32[256,128,128]{2,1,0:T(8,128)} %bitcast.32, f32[16,128,128]{2,1,0:T(8,128)S(1)} %bitcast.23), custom_call_target="tpu_custom_call" | custom-call | flops 4294967296 | bytes 16777216 | tf_op jit(solution)/shard_map/backward0/pallas_call | solution.py:96
  160.5 1.1 reduce_sum.39
  161.5 7.0 %all-to-all-done.6 = f32[8,256,128]{2,1,0:T(8,128)S(1)} async-done(((f32[8,256,128]{2,1,0:T(8,128)}), f32[8,256,128]{2,1,0:T(8,128)S(1)}, u32[]{:S(2)}, u32[]{:S(2)}) %all-to-all-start.6) | async-done | bytes 1048608 | tf_op jit(solution)/shard_map/all_to_all | solution.py:157
  168.6 0.7 broadcast_in_dim.17
  169.3 3.4 %all-to-all-start.10 = ((f32[8,32,256]{2,1,0:T(8,128)}), f32[8,32,256]{2,1,0:T(8,128)S(1)}, u32[]{:S(2)}, u32[]{:S(2)}) async-start(f32[8,32,256]{2,1,0:T(8,128)} %broadcast_in_dim.17), calls=%async_computation.10 | async-start | bytes 524288 | tf_op jit(solution)/shard_map/all_to_all | solution.py:157
  172.7 7.6 %backward1.1 = (f32[16,128,128]{2,1,0:T(8,128)S(1)}, f32[16,128,128]{2,1,0:T(8,128)}) custom-call(s32[256]{0:T(256)S(1)} %bitcast.29, s32[256]{0:T(256)S(1)} %fusion.3.take.put, s32[1]{0:T(128)} %bitcast.19.count, f32[256,128,128]{2,1,0:T(8,128)} %bitcast.33, f32[16,128,128]{2,1,0:T(8,128)S(1)} %bitcast.22), custom_call_target="tpu_custom_call" | custom-call | flops 4294967296 | bytes 16777216 | tf_op jit(solution)/shard_map/backward1/pallas_call | solution.py:96
  180.7 2.4 %add.28 = f32[16,128,128]{2,1,0:T(8,128)} add(f32[16,128,128]{2,1,0:T(8,128)S(1)} %get-tuple-element.14, f32[16,128,128]{2,1,0:T(8,128)} %collective-permute-done.2) | non-fusion elementwise | flops 262144 | bytes 3145728 | tf_op jit(solution)/shard_map/add | solution.py:228
  183.1 8.8 %all-to-all-start.5 = ((f32[8,256,128]{2,1,0:T(8,128)}), f32[8,256,128]{2,1,0:T(8,128)S(1)}, u32[]{:S(2)}, u32[]{:S(2)}) async-start(f32[8,256,128]{2,1,0:T(8,128)} %bitcast.11), calls=%async_computation.5 | async-start | bytes 2097152 | tf_op jit(solution)/shard_map/all_to_all | solution.py:157
  191.9 1.1 add.29
  193.0 13.9 %all-to-all-done.5 = f32[8,256,128]{2,1,0:T(8,128)S(1)} async-done(((f32[8,256,128]{2,1,0:T(8,128)}), f32[8,256,128]{2,1,0:T(8,128)S(1)}, u32[]{:S(2)}, u32[]{:S(2)}) %all-to-all-start.5) | async-done | bytes 1048608 | tf_op jit(solution)/shard_map/all_to_all | solution.py:157
  206.9 3.6 %all-to-all-start.7 = ((f32[8,256,128]{2,1,0:T(8,128)}), f32[8,256,128]{2,1,0:T(8,128)S(1)}, u32[]{:S(2)}, u32[]{:S(2)}) async-start(f32[8,256,128]{2,1,0:T(8,128)} %bitcast.13), calls=%async_computation.7 | async-start | bytes 2097152 | tf_op jit(solution)/shard_map/all_to_all | solution.py:157
  210.5 0.7 broadcast_multiply_fusion
  211.3 14.2 %all-to-all-done.7 = f32[8,256,128]{2,1,0:T(8,128)S(1)} async-done(((f32[8,256,128]{2,1,0:T(8,128)}), f32[8,256,128]{2,1,0:T(8,128)S(1)}, u32[]{:S(2)}, u32[]{:S(2)}) %all-to-all-start.7) | async-done | bytes 1048608 | tf_op jit(solution)/shard_map/all_to_all | solution.py:157
  (24 shorter events, 3.0 us)
Async XLA Ops:
  24.6 16.8 %all-to-all-start = ((f32[8,256,128]{2,1,0:T(8,128)}), f32[8,256,128]{2,1,0:T(8,128)S(1)}, u32[]{:S(2)}, u32[]{:S(2)}) async-start(f32[8,256,128]{2,1,0:T(8,128)} %broadcast_in_dim.12), calls=%async_computation | async-start | bytes 2097152 | tf_op jit(solution)/shard_map/all_to_all | solution.py:157
  28.2 13.3 %collective-permute-start.1 = (f32[8,256,128]{2,1,0:T(8,128)S(1)}, f32[8,256,128]{2,1,0:T(8,128)S(1)}, u32[]{:S(2)}, u32[]{:S(2)}) collective-permute-start(f32[8,256,128]{2,1,0:T(8,128)S(1)} %all_to_all.55), channel_id=1, source_target_pairs={{0,1},{1,0},{2,3},{3,2},{4,5},{5,4},{6,7},{7,6},{8,9},{9,8},{10,11... | collective-permute-start | bytes 3145736 | tf_op jit(solution)/shard_map/ppermute | solution.py:165
  41.4 15.6 %collective-permute-start = (f32[8,256,128]{2,1,0:T(8,128)S(1)}, f32[8,256,128]{2,1,0:T(8,128)}, u32[]{:S(2)}, u32[]{:S(2)}) collective-permute-start(f32[8,256,128]{2,1,0:T(8,128)S(1)} %all-to-all-done), channel_id=1, source_target_pairs={{0,1},{1,0},{2,3},{3,2},{4,5},{5,4},{6,7},{7,6},{8,9},{9,8},{10,11... | collective-permute-start | bytes 3145736 | tf_op jit(solution)/shard_map/ppermute | solution.py:165
  48.6 47.0 %copy-start = (f32[256,256]{1,0:T(8,128)S(1)}, f32[256,256]{1,0:T(8,128)}, u32[]{:S(2)}) copy-start(f32[256,256]{1,0:T(8,128)} %weight.1) | copy-start | bytes 786436
  48.6 26.5 %all-to-all-start.3 = ((f32[8,256,128]{2,1,0:T(8,128)}), f32[8,256,128]{2,1,0:T(8,128)S(1)}, u32[]{:S(2)}, u32[]{:S(2)}) async-start(f32[8,256,128]{2,1,0:T(8,128)} %bitcast.9), calls=%async_computation.3 | async-start | bytes 2097152 | tf_op jit(solution)/shard_map/all_to_all | solution.py:157
  95.6 1.0 copy-start.1
  97.7 0.7 copy-start.2
  98.4 0.7 copy-start.3
  149.3 19.3 %all-to-all-start.6 = ((f32[8,256,128]{2,1,0:T(8,128)}), f32[8,256,128]{2,1,0:T(8,128)S(1)}, u32[]{:S(2)}, u32[]{:S(2)}) async-start(f32[8,256,128]{2,1,0:T(8,128)} %broadcast_in_dim.15), calls=%async_computation.6 | async-start | bytes 2097152 | tf_op jit(solution)/shard_map/all_to_all | solution.py:157
  160.5 20.3 %collective-permute-start.2 = (f32[16,128,128]{2,1,0:T(8,128)}, f32[16,128,128]{2,1,0:T(8,128)}, u32[]{:S(2)}, u32[]{:S(2)}) collective-permute-start(f32[16,128,128]{2,1,0:T(8,128)} %get-tuple-element.15), channel_id=1, source_target_pairs={{0,1},{1,0},{2,3},{3,2},{4,5},{5,4},{6,7},{7,6},{8,9},{9,8},{10,11... | collective-permute-start | bytes 3145736 | tf_op jit(solution)/shard_map/ppermute | solution.py:165
  169.3 13.8 %all-to-all-start.10 = ((f32[8,32,256]{2,1,0:T(8,128)}), f32[8,32,256]{2,1,0:T(8,128)S(1)}, u32[]{:S(2)}, u32[]{:S(2)}) async-start(f32[8,32,256]{2,1,0:T(8,128)} %broadcast_in_dim.17), calls=%async_computation.10 | async-start | bytes 524288 | tf_op jit(solution)/shard_map/all_to_all | solution.py:157
  180.3 11.6 %collective-permute-start.3 = (f32[16,128,128]{2,1,0:T(8,128)}, f32[16,128,128]{2,1,0:T(8,128)S(1)}, u32[]{:S(2)}, u32[]{:S(2)}) collective-permute-start(f32[16,128,128]{2,1,0:T(8,128)} %get-tuple-element.18), channel_id=1, source_target_pairs={{0,1},{1,0},{2,3},{3,2},{4,5},{5,4},{6,7},{7,6},{8,9},{9,8},{10,11... | collective-permute-start | bytes 3145736 | tf_op jit(solution)/shard_map/ppermute | solution.py:165
  183.1 23.8 %all-to-all-start.5 = ((f32[8,256,128]{2,1,0:T(8,128)}), f32[8,256,128]{2,1,0:T(8,128)S(1)}, u32[]{:S(2)}, u32[]{:S(2)}) async-start(f32[8,256,128]{2,1,0:T(8,128)} %bitcast.11), calls=%async_computation.5 | async-start | bytes 2097152 | tf_op jit(solution)/shard_map/all_to_all | solution.py:157
  206.9 18.6 %all-to-all-start.7 = ((f32[8,256,128]{2,1,0:T(8,128)}), f32[8,256,128]{2,1,0:T(8,128)S(1)}, u32[]{:S(2)}, u32[]{:S(2)}) async-start(f32[8,256,128]{2,1,0:T(8,128)} %bitcast.13), calls=%async_computation.7 | async-start | bytes 2097152 | tf_op jit(solution)/shard_map/all_to_all | solution.py:157

commit v2 on v1

--- a/solution.py
+++ b/solution.py
@@ -43,15 +43,15 @@
         for source in sources:
 
             def pair(index, carry, source=source, place=place):
-                high, low = split(source[index])
+                high, low = split(source[pl.ds(pl.multiple_of(index * EDGE, EDGE), EDGE), :])
                 paired[place + index, :EDGE, :EDGE] = high
                 paired[place + index, :EDGE, EDGE:] = low
                 paired[place + index, EDGE:, :EDGE] = high
                 paired[place + index, EDGE:, EDGE:] = jnp.zeros_like(low)
                 return carry
 
-            lax.fori_loop(0, source.shape[0], pair, 0)
-            place += source.shape[0]
+            lax.fori_loop(0, source.shape[0] // EDGE, pair, 0)
+            place += source.shape[0] // EDGE
 
     first = step * GROUP
 
@@ -89,9 +89,9 @@
             place += out.shape[0]
 
 
-def spread(tiles, take, put, count, sources, out_counts, flipped, name):
+def spread(tiles, take, put, count, sources, rows, out_counts, flipped, name):
     slots = tiles.shape[0]
-    src_count = sum(source.shape[0] for source in sources)
+    src_count = len(sources) * rows // EDGE
     whole = lambda *unused: (0, 0, 0)
     return pl.pallas_call(
         functools.partial(spread_body, flipped, len(sources)),
@@ -104,7 +104,7 @@
                     lambda g, take, put, count: (jnp.minimum(g, (count[0] - 1) // GROUP), 0, 0),
                 )
             ]
-            + [pl.BlockSpec(source.shape, whole) for source in sources],
+            + [pl.BlockSpec((rows, EDGE), lambda *unused: (0, 0)) for source in sources],
             out_specs=[pl.BlockSpec((n, EDGE, EDGE), whole) for n in out_counts],
             scratch_shapes=[
                 pltpu.VMEM((src_count, 2 * EDGE, 2 * EDGE), jnp.bfloat16),
@@ -122,6 +122,18 @@
     )(take, put, count, tiles, *sources)
 
 
+def whole_call(kernel, outs, *args, skipped=0, name):
+    here, there = pl.BlockSpec(memory_space=pltpu.VMEM), pl.BlockSpec(memory_space=pl.ANY)
+    return pl.pallas_call(
+        kernel,
+        in_specs=[here] * (len(args) - skipped) + [there] * skipped,
+        out_specs=[here] * len(outs),
+        out_shape=[jax.ShapeDtypeStruct(shape, jnp.float32) for shape in outs],
+        compiler_params=pltpu.CompilerParams(vmem_limit_bytes=VMEM_LIMIT),
+        name=name,
+    )(*args)
+
+
 def middle_body(terms0, terms1, weight, out_grad, hidden, grad0, grad1, gathered, grad_pre):
     parts = [jnp.sum(terms[...], axis=0) for terms in (terms0, terms1)]
     mixed = jnp.concatenate(parts, axis=1)
@@ -137,32 +149,79 @@
     grad1[...] = back[:, EDGE:]
 
 
-def middle(terms0, terms1, weight, out_grad):
-    rows, width = out_grad.shape
-    full = jax.ShapeDtypeStruct((rows, width), jnp.float32)
-    half = jax.ShapeDtypeStruct((rows, EDGE), jnp.float32)
-    return pl.pallas_call(
-        middle_body,
-        out_shape=[full, half, half, full, full],
-        compiler_params=pltpu.CompilerParams(vmem_limit_bytes=VMEM_LIMIT),
-        name="middle",
-    )(terms0, terms1, weight, out_grad)
-
-
 def weight_body(gathered, grad_pre, out):
-    out[...] = dot3(gathered[...], grad_pre[...], ((0,), (0,)))
+    term = dot3(gathered[...], grad_pre[...], ((0,), (0,)))
+    me = lax.axis_index("xh")
+    n_y, piece = out.shape[1], out.shape[2] // 2
+    for place in range(n_y):
+        for half in range(2):
+            first = (place * 2 + half) * piece
+            for side in range(2):
+                out[half ^ me, place, side * piece : (side + 1) * piece, :] = term[
+                    first : first + piece, side * EDGE : (side + 1) * EDGE
+                ]
+
+
+def pair_body(mine, other, *refs):
+    out = refs[-1]
+    rows = mine.shape[0]
+    out[:rows] = mine[...]
+    out[rows:] = other[...]
+
+
+def ring_body(n_ring, grad, other, weight_part, *refs):
+    outs = refs[-n_ring:]
+    me = lax.axis_index("y")
+    rows = grad.shape[0]
+    piece = weight_part.shape[1]
+    for step, out in enumerate(outs):
+        out[:rows] = grad[...]
+        out[rows : 2 * rows] = other[:rows]
+        place = lax.rem(me + step, n_ring)
+        out[2 * rows :] = weight_part[place] + other[pl.ds(rows + place * piece, piece), :]
+
+
+def share_body(mine, other, piece, other_piece, out):
+    rows = out.shape[1] - piece.shape[0]
+    both = piece[...] + other_piece[...]
+    for place in range(out.shape[0]):
+        here = pl.ds(place * rows, rows)
+        out[place, :rows] = mine[here, :] + other[here, :]
+        out[place, rows:] = both
+
+
+def add_body(mine, other, out):
+    out[...] = mine[...] + other[...]
+
+
+def sum_body(terms, grad, piece):
+    total = jnp.sum(terms[...], axis=0)
+    rows = grad.shape[0]
+    grad[...] = total[:rows]
+    piece[...] = total[rows:]
+
+
+def finish_body(grad0, terms1, out):
+    out[:, :EDGE] = grad0[...]
+    out[:, EDGE:] = jnp.sum(terms1[...], axis=0)
 
 
 def exchange(value, axes):
     return lax.all_to_all(value, axes, 0, 0, tiled=True)
 
 
-def copies(value, count):
-    return jnp.broadcast_to(value[None], (count, *value.shape))
-
-
-def swap_core(value):
-    return lax.ppermute(value, "core", [(0, 1), (1, 0)])
+def swap(value, axis):
+    return lax.ppermute(value, axis, [(0, 1), (1, 0)])
+
+
+def ring_send(value, axis, step):
+    size = lax.axis_size(axis)
+    return lax.ppermute(value, axis, [(place, (place + step) % size) for place in range(size)])
+
+
+def offset_of(ring_index, pair_index, ring, pair):
+    step = (lax.axis_index(ring) - ring_index) % lax.axis_size(ring)
+    return step * 2 + (pair_index ^ lax.axis_index(pair))
 
 
 def body(features, weight, tile_vals, tile_index, tile_count, out_grad):
@@ -173,62 +232,104 @@
     n_row = lax.axis_size(ROW_AXES)
     n_col = lax.axis_size(COL_AXES)
     n_plane = lax.axis_size(PLANE_AXES)
+    n_z = lax.axis_size("z")
+    n_y = lax.axis_size("y")
     rows, width = features.shape
     per = rows // EDGE
     half_tiles = n_plane * per
-    src = (
-        (((src // per) % 2) ^ lax.axis_index("core")) * half_tiles
-        + (src // (2 * per)) * per
-        + src % per
+    src_home, src_tile = src // per, src % per
+    src_core = (src_home % 2) ^ lax.axis_index("core")
+    src_plane = src_home // 2
+    src_take = (
+        src_core * half_tiles + offset_of(src_plane % n_z, src_plane // n_z, "z", "xl") * per + src_tile
     ).astype(jnp.int32)
-
-    def tiled(value):
-        return value.reshape(-1, EDGE, EDGE)
-
-    received = []
+    src_put = (src_core * half_tiles + src_plane * per + src_tile).astype(jnp.int32)
+    dest_home, dest_tile = dest // per, dest % per
+    dest_take = (offset_of(dest_home // 2, dest_home % 2, "y", "xh") * per + dest_tile).astype(jnp.int32)
+
+    terms = []
+    before = []
     for chunk in range(2):
         part = features[:, chunk * EDGE : (chunk + 1) * EDGE]
-        received.append(exchange(copies(part, n_plane), PLANE_AXES))
-    terms = []
-    for chunk in range(2):
-        mine = received[chunk]
-        other = swap_core(mine)
+        (both,) = whole_call(
+            pair_body,
+            [(2 * rows, EDGE)],
+            part,
+            swap(part, "xl"),
+            *before,
+            skipped=len(before),
+            name=f"pair{chunk}",
+        )
+        mine = [both] + [ring_send(both, "z", step) for step in (1, 3, 2)]
+        before = mine[1:]
+        mine = [mine[0], mine[1], mine[3], mine[2]]
+        other = [swap(value, "core") for value in mine]
         (partial,) = spread(
-            tiles, src, dest, count, [tiled(mine), tiled(other)], [n_row * per], False, f"forward{chunk}"
+            tiles, src_take, dest, count, mine + other, 2 * rows, [n_row * per], False, f"forward{chunk}"
         )
         terms.append(exchange(partial.reshape(n_row, rows, EDGE), ROW_AXES))
-    hidden, grad0, grad1, gathered, grad_pre = middle(terms[0], terms[1], weight, out_grad)
-
-    received = [exchange(copies(grad, n_row), ROW_AXES) for grad in (grad0, grad1)]
-    weight_term = pl.pallas_call(
-        weight_body,
-        out_shape=jax.ShapeDtypeStruct((width, width), jnp.float32),
-        name="weight_term",
-    )(gathered, grad_pre)
-    pieces = exchange(weight_term.reshape(n_row, width // n_row, width), ROW_AXES)
-    piece = jnp.sum(pieces, axis=0)
-    pieces = exchange(copies(piece, n_col), COL_AXES)
-    piece = jnp.sum(pieces, axis=0)
-    grad_w = exchange(copies(piece, n_row), ROW_AXES).reshape(width, width)
-    nodes = rows * n_row * n_col
-    grad_w = grad_w * nodes ** (-0.5)
-
-    grads = []
-    for chunk in range(2):
+    half = (rows, EDGE)
+    full = (rows, width)
+    hidden, grad0, grad1, gathered, grad_pre = whole_call(
+        middle_body, [full, half, half, full, full], *terms, weight, out_grad, name="middle"
+    )
+
+    (both,) = whole_call(pair_body, [(2 * rows, EDGE)], grad0, swap(grad0, "xh"), name="pair2")
+    received = [both] + [ring_send(both, "y", step) for step in (1, 3, 2)]
+    before = received[1:]
+    received0 = [received[0], received[1], received[3], received[2]]
+    piece_rows = 2 * width // n_row
+    (weight_part,) = whole_call(
+        weight_body, [(2, n_y, piece_rows, EDGE)], gathered, grad_pre, name="weight_term"
+    )
+    other = swap(jnp.concatenate([grad1, weight_part[1].reshape(-1, EDGE)], axis=0), "xh")
+    sends = whole_call(
+        functools.partial(ring_body, n_y),
+        [(2 * rows + piece_rows, EDGE)] * n_y,
+        grad1,
+        other,
+        weight_part[0],
+        *before,
+        skipped=len(before),
+        name="ring",
+    )
+    received1 = [sends[0]] + [ring_send(sends[step], "y", step) for step in range(1, n_y)]
+    piece = sum(value[2 * rows :] for value in received1)
+
+    shares = []
+    for chunk, received in enumerate((received0, received1)):
         mine, other = spread(
             tiles,
-            dest,
-            src,
+            dest_take,
+            src_put,
             count,
-            [tiled(received[chunk])],
+            received,
+            2 * rows,
             [half_tiles, half_tiles],
             True,
             f"backward{chunk}",
         )
-        share = mine + swap_core(other)
-        arrived = exchange(share.reshape(n_plane, rows, EDGE), PLANE_AXES)
-        grads.append(jnp.sum(arrived, axis=0))
-    grad_x = jnp.concatenate(grads, axis=1)
+        mine = mine.reshape(-1, EDGE)
+        other = swap(other.reshape(-1, EDGE), "core")
+        if chunk == 0:
+            (share,) = whole_call(
+                share_body,
+                [(n_plane, rows + piece_rows, EDGE)],
+                mine,
+                other,
+                piece,
+                swap(piece, "core"),
+                name="share0",
+            )
+        else:
+            (share,) = whole_call(add_body, [(n_plane * rows, EDGE)], mine, other, name="share1")
+            share = share.reshape(n_plane, rows, EDGE)
+        shares.append(exchange(share, PLANE_AXES))
+    grad_x0, piece = whole_call(sum_body, [half, (piece_rows, EDGE)], shares[0], name="sum0")
+    pieces = lax.all_gather(piece, ROW_AXES, axis=0, tiled=False)
+    grad_w = pieces.reshape(n_row, 2, piece_rows // 2, EDGE).transpose(0, 2, 1, 3).reshape(width, width)
+    grad_w = grad_w * (rows * n_row * n_col) ** (-0.5)
+    (grad_x,) = whole_call(finish_body, [full], grad_x0, shares[1], name="finish")
     return hidden, grad_x, grad_w
 
 

time: 229 us -> 216 us (0.943)
  blocking collectives: 89.3 us -> 61.4 us
  Pallas kernels: 31.9 us -> 42.2 us
  starting transfers between devices: 31.9 us -> 40 us
  waiting for transfers between devices: 58.5 us -> 65.5 us
  other arithmetic: 6.14 us -> 0.12 us
  local copies, waits for them, and re-layouts: 7.09 us -> 2.71 us
    all_to_all x5 -> x1, blocking collectives: 89.3 us -> 19.4 us  [exchange(): return lax.all_to_all(value, axes, 0, 0, tiled=True)]
    ppermute x4 -> x27, waiting for transfers between devices: 0.01 us -> 55.7 us  [the longest x12 31.3 us: ring_send(): lax.ppermute(value, axis, [(place, (place + step) % size) for place in ra...]
    all_to_all x6 -> x3, waiting for transfers between devices: 58.5 us -> 9.84 us  [exchange(): return lax.all_to_all(value, axes, 0, 0, tiled=True)]
    all_gather x0 -> x1, blocking collectives: none -> 42 us  [body(): pieces = lax.all_gather(piece, ROW_AXES, axis=0, tiled=False)]
    ppermute x4 -> x27, starting transfers between devices: 0.54 us -> 23.6 us  [the longest x12 17.3 us: ring_send(): lax.ppermute(value, axis, [(place, (place + step) % size) for place in ra...]
    all_to_all x6 -> x3, starting transfers between devices: 31.4 us -> 16.3 us  [exchange(): return lax.all_to_all(value, axes, 0, 0, tiled=True)]
    pallas_call x4, Pallas kernels: 28.7 us -> 37.4 us  [spread(): pl.pallas_call(functools.partial(spread_body, flipped, len(sources)), gri...]
    add x3, other arithmetic: 3.48 us -> 0.08 us  [the longest x1 0.04 us: body(): src_core * half_tiles + src_plane * per + src_tile]
  transfers between devices with their start and end apart: 10 -> 30, of which waited for: 5 -> 18; matrix products, arithmetic and copies ran while one was open for 3% -> 1% of each run, Pallas kernels for 13% -> 14%
where the time goes in v2:
time: 216 us; the launch traced here: 213 us
  waiting for transfers between devices  65.5 us (30%)
  blocking collectives  61.4 us (28%)
  Pallas kernels  42.2 us (20%)
  starting transfers between devices  40 us (19%)
  local copies, waits for them, and re-layouts  2.71 us (1%)
    all_gather x1, blocking collectives, body(): pieces = lax.all_gather(piece, ROW_AXES, axis=0, tiled=False)  42 us
    pallas_call x4, Pallas kernels, spread(): pl.pallas_call(functools.partial(spread_body, flipped, len(sources)), gri...  37.4 us
    ppermute x12, waiting for transfers between devices, ring_send(): lax.ppermute(value, axis, [(place, (place + step) % size) for place in ra...  31.3 us
    ppermute x15, waiting for transfers between devices, swap(): return lax.ppermute(value, axis, [(0, 1), (1, 0)])  24.4 us
    all_to_all x1, blocking collectives, exchange(): return lax.all_to_all(value, axes, 0, 0, tiled=True)  19.4 us
    ppermute x12, starting transfers between devices, ring_send(): lax.ppermute(value, axis, [(place, (place + step) % size) for place in ra...  17.3 us
    all_to_all x3, starting transfers between devices, exchange(): return lax.all_to_all(value, axes, 0, 0, tiled=True)  16.3 us
    all_to_all x3, waiting for transfers between devices, exchange(): return lax.all_to_all(value, axes, 0, 0, tiled=True)  9.84 us
  transfers between devices with their start and end apart: 30, of which 18 were waited for; matrix products, arithmetic and copies ran while one was open for 1% of the time, Pallas kernels for 14%

profile of v2, /device:TPU:0, one launch (start us, length us, event | category | flops | bytes accessed | tf_op | source)
XLA Modules:
  0.0 213.3 jit_solution(15750339555137915333)
XLA Ops:
  1.6 1.7 collective-permute-start
  3.3 3.5 %collective-permute-done.other = f32[256,128]{1,0:T(8,128)S(1)} collective-permute-done((f32[256,128]{1,0:T(8,128)S(1)}, f32[256,128]{1,0:T(8,128)S(1)}, u32[]{:S(2)}, u32[]{:S(2)}) %collective-permute-start) | collective-permute-done | bytes 131104 | tf_op jit(solution)/shard_map/ppermute | solution.py:214
  6.8 2.2 %collective-permute-start.1 = (f32[512,128]{1,0:T(8,128)S(1)}, f32[512,128]{1,0:T(8,128)S(1)}, u32[]{:S(2)}, u32[]{:S(2)}) collective-permute-start(f32[512,128]{1,0:T(8,128)S(1)} %pair0.1.refs_0_), channel_id=1, source_target_pairs={{0,2},{2,4},{4,6},{6,0},{1,3},{3,5},{5,7},{7,1},{8,10},{10,12},{12... | collective-permute-start | bytes 786440 | tf_op jit(solution)/shard_map/ppermute | solution.py:219
  9.0 3.6 %collective-permute-start.2 = (f32[512,128]{1,0:T(8,128)S(1)}, f32[512,128]{1,0:T(8,128)S(1)}, u32[]{:S(2)}, u32[]{:S(2)}) collective-permute-start(f32[512,128]{1,0:T(8,128)S(1)} %pair0.1.refs_0_), channel_id=1, source_target_pairs={{0,4},{2,6},{4,0},{6,2},{1,5},{3,7},{5,1},{7,3},{8,12},{10,14},{12... | collective-permute-start | bytes 786440 | tf_op jit(solution)/shard_map/ppermute | solution.py:219
  13.6 1.5 collective-permute-start.8
  15.1 2.4 %collective-permute-done.1.refs_1_.refs_0_ = f32[512,128]{1,0:T(8,128)S(1)} collective-permute-done((f32[512,128]{1,0:T(8,128)S(1)}, f32[512,128]{1,0:T(8,128)S(1)}, u32[]{:S(2)}, u32[]{:S(2)}) %collective-permute-start.1) | collective-permute-done | bytes 262176 | tf_op jit(solution)/shard_map/ppermute | solution.py:219
  17.5 5.9 %collective-permute-done.2.refs_2_ = f32[512,128]{1,0:T(8,128)S(1)} collective-permute-done((f32[512,128]{1,0:T(8,128)S(1)}, f32[512,128]{1,0:T(8,128)S(1)}, u32[]{:S(2)}, u32[]{:S(2)}) %collective-permute-start.2) | collective-permute-done | bytes 262176 | tf_op jit(solution)/shard_map/ppermute | solution.py:219
  26.2 2.4 %collective-permute-start.10 = (f32[512,128]{1,0:T(8,128)S(1)}, f32[512,128]{1,0:T(8,128)S(1)}, u32[]{:S(2)}, u32[]{:S(2)}) collective-permute-start(f32[512,128]{1,0:T(8,128)S(1)} %pair1.1.refs_0_), channel_id=1, source_target_pairs={{0,4},{2,6},{4,0},{6,2},{1,5},{3,7},{5,1},{7,3},{8,12},{10,14},{12... | collective-permute-start | bytes 786440 | tf_op jit(solution)/shard_map/ppermute | solution.py:219
  28.6 1.2 collective-permute-start.11
  29.8 9.4 %forward0.1 = f32[16,128,128]{2,1,0:T(8,128)} custom-call(s32[256]{0:T(256)S(1)} %get-tuple-element.40.take, s32[256]{0:T(256)S(1)} %bitcast.29, s32[1]{0:T(128)} %bitcast.22.count, f32[256,128,128]{2,1,0:T(8,128)} %bitcast.34, f32[512,128]{1,0:T(8,128)S(1)} %pair0.1.refs_0_, f32[512,128]{1,0:T(8,128)S(1)} %collective-permute-done.1.refs_1_.refs_0_, ...), custom_call_target="tpu_custom_call" | custom-call | flops 4294967296 | bytes 16777216 | tf_op jit(solution)/shard_map/forward0/pallas_call | solution.py:96
  39.3 4.9 %all-to-all-start = ((f32[8,256,128]{2,1,0:T(8,128)}), f32[8,256,128]{2,1,0:T(8,128)S(1)}, u32[]{:S(2)}, u32[]{:S(2)}) async-start(f32[8,256,128]{2,1,0:T(8,128)} %bitcast.4), calls=%async_computation | async-start | bytes 2097152 | tf_op jit(solution)/shard_map/all_to_all | solution.py:210
  46.8 8.5 %forward1.1 = f32[16,128,128]{2,1,0:T(8,128)S(1)} custom-call(s32[256]{0:T(256)S(1)} %get-tuple-element.40.take, s32[256]{0:T(256)S(1)} %bitcast.30, s32[1]{0:T(128)} %bitcast.23.count, f32[256,128,128]{2,1,0:T(8,128)} %bitcast.35, f32[512,128]{1,0:T(8,128)S(1)} %pair1.1.refs_0_, f32[512,128]{1,0:T(8,128)S(1)} %collective-permute-done.9.refs_1_, ...), custom_call_target="tpu_custom_call" | custom-call | flops 4294967296 | bytes 16777216 | tf_op jit(solution)/shard_map/forward1/pallas_call | solution.py:96
  55.3 5.5 %all-to-all-done.terms0 = f32[8,256,128]{2,1,0:T(8,128)S(1)} async-done(((f32[8,256,128]{2,1,0:T(8,128)}), f32[8,256,128]{2,1,0:T(8,128)S(1)}, u32[]{:S(2)}, u32[]{:S(2)}) %all-to-all-start) | async-done | bytes 1048608 | tf_op jit(solution)/shard_map/all_to_all | solution.py:210
  60.9 19.4 %all_to_all.20.terms1 = f32[8,256,128]{2,1,0:T(8,128)S(1)} all-to-all(f32[8,256,128]{2,1,0:T(8,128)S(1)} %bitcast.26), channel_id=1, replica_groups=mesh['y'=4,'xh'=2,'xl'=2,'z'=4,'core'=2] {'y','xh'}, dimensions={0} | all-to-all | bytes 2097152 | tf_op jit(solution)/shard_map/all_to_all | solution.py:210
  82.3 5.6 %collective-permute-done.16.other = f32[256,128]{1,0:T(8,128)S(1)} collective-permute-done((f32[256,128]{1,0:T(8,128)S(1)}, f32[256,128]{1,0:T(8,128)S(1)}, u32[]{:S(2)}, u32[]{:S(2)}) %collective-permute-start.16) | collective-permute-done | bytes 131104 | tf_op jit(solution)/shard_map/ppermute | solution.py:214
  88.2 2.1 collective-permute-start.18
  90.3 1.4 collective-permute-start.19
  92.1 7.8 %collective-permute-done.17.refs_1_.refs_0_ = f32[512,128]{1,0:T(8,128)S(1)} collective-permute-done((f32[512,128]{1,0:T(8,128)S(1)}, f32[512,128]{1,0:T(8,128)S(1)}, u32[]{:S(2)}, u32[]{:S(2)}) %collective-permute-start.17) | collective-permute-done | bytes 262176 | tf_op jit(solution)/shard_map/ppermute | solution.py:219
  100.6 9.8 %backward0.1 = (f32[16,128,128]{2,1,0:T(8,128)S(1)}, f32[16,128,128]{2,1,0:T(8,128)S(1)}) custom-call(s32[256]{0:T(256)S(1)} %fusion.7.take, s32[256]{0:T(256)S(1)} %get-tuple-element.39.put, s32[1]{0:T(128)} %bitcast.24.count, f32[256,128,128]{2,1,0:T(8,128)} %bitcast.36, f32[512,128]{1,0:T(8,128)S(1)} %pair2.1.refs_0_, ...), custom_call_target="tpu_custom_call" | custom-call | flops 4294967296 | bytes 16777216 | tf_op jit(solution)/shard_map/backward0/pallas_call | solution.py:96
  111.0 9.8 %collective-permute-done.21.other = f32[512,128]{1,0:T(8,128)S(1)} collective-permute-done((f32[512,128]{1,0:T(8,128)S(1)}, f32[512,128]{1,0:T(8,128)S(1)}, u32[]{:S(2)}, u32[]{:S(2)}) %collective-permute-start.21) | collective-permute-done | bytes 262176 | tf_op jit(solution)/shard_map/ppermute | solution.py:214
  121.4 1.8 collective-permute-start.22
  123.1 7.9 %collective-permute-done.24.refs_3_ = f32[576,128]{1,0:T(8,128)S(1)} collective-permute-done((f32[576,128]{1,0:T(8,128)S(1)}, f32[576,128]{1,0:T(8,128)S(1)}, u32[]{:S(2)}, u32[]{:S(2)}) %collective-permute-start.24) | collective-permute-done | bytes 294944 | tf_op jit(solution)/shard_map/ppermute | solution.py:219
  131.0 1.6 collective-permute-done.23.refs_2_
  132.7 5.0 %collective-permute-done.22.refs_1_ = f32[576,128]{1,0:T(8,128)S(1)} collective-permute-done((f32[576,128]{1,0:T(8,128)S(1)}, f32[576,128]{1,0:T(8,128)S(1)}, u32[]{:S(2)}, u32[]{:S(2)}) %collective-permute-start.22) | collective-permute-done | bytes 294944 | tf_op jit(solution)/shard_map/ppermute | solution.py:219
  137.8 1.2 collective-permute-done.25.other_piece
  138.9 1.2 share0.1
  140.2 7.8 %all-to-all-start.2 = ((f32[8,320,128]{2,1,0:T(8,128)}), f32[8,320,128]{2,1,0:T(8,128)S(1)}, u32[]{:S(2)}, u32[]{:S(2)}) async-start(f32[8,320,128]{2,1,0:T(8,128)} %share0.1), calls=%async_computation.2 | async-start | bytes 2621440 | tf_op jit(solution)/shard_map/all_to_all | solution.py:210
  148.0 9.8 %backward1.1 = (f32[16,128,128]{2,1,0:T(8,128)S(1)}, f32[16,128,128]{2,1,0:T(8,128)S(1)}) custom-call(s32[256]{0:T(256)S(1)} %fusion.7.take, s32[256]{0:T(256)S(1)} %get-tuple-element.39.put, s32[1]{0:T(128)} %bitcast.25.count, f32[256,128,128]{2,1,0:T(8,128)} %bitcast.37, f32[576,128]{1,0:T(8,128)S(1)} %get-tuple-element.25.refs_0_, ...), custom_call_target="tpu_custom_call" | custom-call | flops 4294967296 | bytes 16777216 | tf_op jit(solution)/shard_map/backward1/pallas_call | solution.py:96
  157.8 2.6 %collective-permute-done.26.other = f32[2048,128]{1,0:T(8,128)S(1)} collective-permute-done((f32[2048,128]{1,0:T(8,128)S(1)}, f32[2048,128]{1,0:T(8,128)S(1)}, u32[]{:S(2)}, u32[]{:S(2)}) %collective-permute-start.26) | collective-permute-done | bytes 1048608 | tf_op jit(solution)/shard_map/ppermute | solution.py:214
  161.6 4.3 %all-to-all-done.2.terms = f32[8,320,128]{2,1,0:T(8,128)S(1)} async-done(((f32[8,320,128]{2,1,0:T(8,128)}), f32[8,320,128]{2,1,0:T(8,128)S(1)}, u32[]{:S(2)}, u32[]{:S(2)}) %all-to-all-start.2) | async-done | bytes 1310752 | tf_op jit(solution)/shard_map/all_to_all | solution.py:210
  165.9 3.6 %all-to-all-start.3 = ((f32[8,256,128]{2,1,0:T(8,128)}), f32[8,256,128]{2,1,0:T(8,128)S(1)}, u32[]{:S(2)}, u32[]{:S(2)}) async-start(f32[8,256,128]{2,1,0:T(8,128)} %bitcast.12), calls=%async_computation.3 | async-start | bytes 2097152 | tf_op jit(solution)/shard_map/all_to_all | solution.py:210
  169.6 42.0 %all-gather = f32[512,128]{1,0:T(8,128)S(1)} all-gather(f32[64,128]{1,0:T(8,128)S(1)} %get-tuple-element.32), channel_id=2, replica_groups=mesh['y'=4,'xh'=2,'xl'=2,'z'=4,'core'=2] {'y','xh'}, dimensions={0}, use_global_device_ids=true | all-gather | bytes 294912 | tf_op jit(solution)/shard_map/all_gather | solution.py:329
  (58 shorter events, 14.4 us)
Async XLA Ops:
  1.6 5.2 %collective-permute-start = (f32[256,128]{1,0:T(8,128)S(1)}, f32[256,128]{1,0:T(8,128)S(1)}, u32[]{:S(2)}, u32[]{:S(2)}) collective-permute-start(f32[256,128]{1,0:T(8,128)S(1)} %get-tuple-element.36.mine), channel_id=1, source_target_pairs={{0,8},{8,0},{1,9},{9,1},{2,10},{10,2},{3,11},{11,3},{4,12},{12,4},... | collective-permute-start | bytes 393224 | tf_op jit(solution)/shard_map/ppermute | solution.py:214
  6.8 10.7 %collective-permute-start.1 = (f32[512,128]{1,0:T(8,128)S(1)}, f32[512,128]{1,0:T(8,128)S(1)}, u32[]{:S(2)}, u32[]{:S(2)}) collective-permute-start(f32[512,128]{1,0:T(8,128)S(1)} %pair0.1.refs_0_), channel_id=1, source_target_pairs={{0,2},{2,4},{4,6},{6,0},{1,3},{3,5},{5,7},{7,1},{8,10},{10,12},{12... | collective-permute-start | bytes 786440 | tf_op jit(solution)/shard_map/ppermute | solution.py:219
  9.0 14.3 %collective-permute-start.2 = (f32[512,128]{1,0:T(8,128)S(1)}, f32[512,128]{1,0:T(8,128)S(1)}, u32[]{:S(2)}, u32[]{:S(2)}) collective-permute-start(f32[512,128]{1,0:T(8,128)S(1)} %pair0.1.refs_0_), channel_id=1, source_target_pairs={{0,4},{2,6},{4,0},{6,2},{1,5},{3,7},{5,1},{7,3},{8,12},{10,14},{12... | collective-permute-start | bytes 786440 | tf_op jit(solution)/shard_map/ppermute | solution.py:219
  12.6 10.8 %collective-permute-start.3 = (f32[512,128]{1,0:T(8,128)S(1)}, f32[512,128]{1,0:T(8,128)S(1)}, u32[]{:S(2)}, u32[]{:S(2)}) collective-permute-start(f32[512,128]{1,0:T(8,128)S(1)} %pair0.1.refs_0_), channel_id=1, source_target_pairs={{0,6},{2,0},{4,2},{6,4},{1,7},{3,1},{5,3},{7,5},{8,14},{10,8},{12,... | collective-permute-start | bytes 786440 | tf_op jit(solution)/shard_map/ppermute | solution.py:219
  13.6 11.7 %collective-permute-start.8 = (f32[256,128]{1,0:T(8,128)S(1)}, f32[256,128]{1,0:T(8,128)S(1)}, u32[]{:S(2)}, u32[]{:S(2)}) collective-permute-start(f32[256,128]{1,0:T(8,128)S(1)} %get-tuple-element.35.mine), channel_id=1, source_target_pairs={{0,8},{8,0},{1,9},{9,1},{2,10},{10,2},{3,11},{11,3},{4,12},{12,4},... | collective-permute-start | bytes 393224 | tf_op jit(solution)/shard_map/ppermute | solution.py:214
  15.1 11.1 %collective-permute-start.4 = (f32[512,128]{1,0:T(8,128)S(1)}, f32[512,128]{1,0:T(8,128)S(1)}, u32[]{:S(2)}, u32[]{:S(2)}) collective-permute-start(f32[512,128]{1,0:T(8,128)S(1)} %pair0.1.refs_0_), channel_id=1, source_target_pairs={{0,1},{1,0},{2,3},{3,2},{4,5},{5,4},{6,7},{7,6},{8,9},{9,8},{10,11... | collective-permute-start | bytes 786440 | tf_op jit(solution)/shard_map/ppermute | solution.py:214
  17.5 11.1 %collective-permute-start.5 = (f32[512,128]{1,0:T(8,128)S(1)}, f32[512,128]{1,0:T(8,128)S(1)}, u32[]{:S(2)}, u32[]{:S(2)}) collective-permute-start(f32[512,128]{1,0:T(8,128)S(1)} %collective-permute-done.1.refs_1_.refs_0_), channel_id=1, source_target_pairs={{0,1},{1,0},{2,3},{3,2},{4,5},{5,4},{6,7},{7,6},{8,9},{9,8},{10,11... | collective-permute-start | bytes 786440 | tf_op jit(solution)/shard_map/ppermute | solution.py:214
  23.4 6.4 %collective-permute-start.6 = (f32[512,128]{1,0:T(8,128)S(1)}, f32[512,128]{1,0:T(8,128)S(1)}, u32[]{:S(2)}, u32[]{:S(2)}) collective-permute-start(f32[512,128]{1,0:T(8,128)S(1)} %collective-permute-done.2.refs_2_), channel_id=1, source_target_pairs={{0,1},{1,0},{2,3},{3,2},{4,5},{5,4},{6,7},{7,6},{8,9},{9,8},{10,11... | collective-permute-start | bytes 786440 | tf_op jit(solution)/shard_map/ppermute | solution.py:214
  23.4 6.4 %collective-permute-start.7 = (f32[512,128]{1,0:T(8,128)S(1)}, f32[512,128]{1,0:T(8,128)S(1)}, u32[]{:S(2)}, u32[]{:S(2)}) collective-permute-start(f32[512,128]{1,0:T(8,128)S(1)} %collective-permute-done.3.refs_3_.refs_1_), channel_id=1, source_target_pairs={{0,1},{1,0},{2,3},{3,2},{4,5},{5,4},{6,7},{7,6},{8,9},{9,8},{10,11... | collective-permute-start | bytes 786440 | tf_op jit(solution)/shard_map/ppermute | solution.py:214
  25.4 18.8 %collective-permute-start.9 = (f32[512,128]{1,0:T(8,128)S(1)}, f32[512,128]{1,0:T(8,128)S(1)}, u32[]{:S(2)}, u32[]{:S(2)}) collective-permute-start(f32[512,128]{1,0:T(8,128)S(1)} %pair1.1.refs_0_), channel_id=1, source_target_pairs={{0,2},{2,4},{4,6},{6,0},{1,3},{3,5},{5,7},{7,1},{8,10},{10,12},{12... | collective-permute-start | bytes 786440 | tf_op jit(solution)/shard_map/ppermute | solution.py:219
  26.2 18.5 %collective-permute-start.10 = (f32[512,128]{1,0:T(8,128)S(1)}, f32[512,128]{1,0:T(8,128)S(1)}, u32[]{:S(2)}, u32[]{:S(2)}) collective-permute-start(f32[512,128]{1,0:T(8,128)S(1)} %pair1.1.refs_0_), channel_id=1, source_target_pairs={{0,4},{2,6},{4,0},{6,2},{1,5},{3,7},{5,1},{7,3},{8,12},{10,14},{12... | collective-permute-start | bytes 786440 | tf_op jit(solution)/shard_map/ppermute | solution.py:219
  28.6 16.2 %collective-permute-start.11 = (f32[512,128]{1,0:T(8,128)S(1)}, f32[512,128]{1,0:T(8,128)S(1)}, u32[]{:S(2)}, u32[]{:S(2)}) collective-permute-start(f32[512,128]{1,0:T(8,128)S(1)} %pair1.1.refs_0_), channel_id=1, source_target_pairs={{0,6},{2,0},{4,2},{6,4},{1,7},{3,1},{5,3},{7,5},{8,14},{10,8},{12,... | collective-permute-start | bytes 786440 | tf_op jit(solution)/shard_map/ppermute | solution.py:219
  39.3 21.6 %all-to-all-start = ((f32[8,256,128]{2,1,0:T(8,128)}), f32[8,256,128]{2,1,0:T(8,128)S(1)}, u32[]{:S(2)}, u32[]{:S(2)}) async-start(f32[8,256,128]{2,1,0:T(8,128)} %bitcast.4), calls=%async_computation | async-start | bytes 2097152 | tf_op jit(solution)/shard_map/all_to_all | solution.py:210
  44.2 1.5 collective-permute-start.12
  44.2 1.9 collective-permute-start.13
  44.7 1.8 collective-permute-start.14
  44.8 2.0 collective-permute-start.15
  55.3 25.0 %copy-start = (f32[256,256]{1,0:T(8,128)S(1)}, f32[256,256]{1,0:T(8,128)}, u32[]{:S(2)}) copy-start(f32[256,256]{1,0:T(8,128)} %weight.1) | copy-start | bytes 786436
  55.3 25.0 %copy-start.1 = (f32[256,256]{1,0:T(8,128)S(1)}, f32[256,256]{1,0:T(8,128)}, u32[]{:S(2)}) copy-start(f32[256,256]{1,0:T(8,128)} %out_grad.1) | copy-start | bytes 786436
  81.4 6.5 %collective-permute-start.16 = (f32[256,128]{1,0:T(8,128)S(1)}, f32[256,128]{1,0:T(8,128)S(1)}, u32[]{:S(2)}, u32[]{:S(2)}) collective-permute-start(f32[256,128]{1,0:T(8,128)S(1)} %get-tuple-element.19.mine), channel_id=1, source_target_pairs={{0,16},{16,0},{1,17},{17,1},{2,18},{18,2},{3,19},{19,3},{4,20},{20... | collective-permute-start | bytes 393224 | tf_op jit(solution)/shard_map/ppermute | solution.py:214
  87.9 12.0 %collective-permute-start.17 = (f32[512,128]{1,0:T(8,128)S(1)}, f32[512,128]{1,0:T(8,128)S(1)}, u32[]{:S(2)}, u32[]{:S(2)}) collective-permute-start(f32[512,128]{1,0:T(8,128)S(1)} %pair2.1.refs_0_), channel_id=1, source_target_pairs={{0,32},{32,64},{64,96},{96,0},{1,33},{33,65},{65,97},{97,1},{2,34}... | collective-permute-start | bytes 786440 | tf_op jit(solution)/shard_map/ppermute | solution.py:219
  88.2 11.7 %collective-permute-start.18 = (f32[512,128]{1,0:T(8,128)S(1)}, f32[512,128]{1,0:T(8,128)S(1)}, u32[]{:S(2)}, u32[]{:S(2)}) collective-permute-start(f32[512,128]{1,0:T(8,128)S(1)} %pair2.1.refs_0_), channel_id=1, source_target_pairs={{0,64},{32,96},{64,0},{96,32},{1,65},{33,97},{65,1},{97,33},{2,66}... | collective-permute-start | bytes 786440 | tf_op jit(solution)/shard_map/ppermute | solution.py:219
  90.3 10.3 %collective-permute-start.19 = (f32[512,128]{1,0:T(8,128)S(1)}, f32[512,128]{1,0:T(8,128)S(1)}, u32[]{:S(2)}, u32[]{:S(2)}) collective-permute-start(f32[512,128]{1,0:T(8,128)S(1)} %pair2.1.refs_0_), channel_id=1, source_target_pairs={{0,96},{32,0},{64,32},{96,64},{1,97},{33,1},{65,33},{97,65},{2,98}... | collective-permute-start | bytes 786440 | tf_op jit(solution)/shard_map/ppermute | solution.py:219
  110.3 28.6 %collective-permute-start.20 = (f32[2048,128]{1,0:T(8,128)S(1)}, f32[2048,128]{1,0:T(8,128)S(1)}, u32[]{:S(2)}, u32[]{:S(2)}) collective-permute-start(f32[2048,128]{1,0:T(8,128)S(1)} %bitcast.32), channel_id=1, source_target_pairs={{0,1},{1,0},{2,3},{3,2},{4,5},{5,4},{6,7},{7,6},{8,9},{9,8},{10,11... | collective-permute-start | bytes 3145736 | tf_op jit(solution)/shard_map/ppermute | solution.py:214
  110.5 10.3 %collective-permute-start.21 = (f32[512,128]{1,0:T(8,128)S(1)}, f32[512,128]{1,0:T(8,128)S(1)}, u32[]{:S(2)}, u32[]{:S(2)}) collective-permute-start(f32[512,128]{1,0:T(8,128)S(1)} %pad_maximum_fusion), channel_id=1, source_target_pairs={{0,16},{16,0},{1,17},{17,1},{2,18},{18,2},{3,19},{19,3},{4,20},{20... | collective-permute-start | bytes 786440 | tf_op jit(solution)/shard_map/ppermute | solution.py:214
  120.9 10.2 %collective-permute-start.24 = (f32[576,128]{1,0:T(8,128)S(1)}, f32[576,128]{1,0:T(8,128)S(1)}, u32[]{:S(2)}, u32[]{:S(2)}) collective-permute-start(f32[576,128]{1,0:T(8,128)S(1)} %get-tuple-element.28), channel_id=1, source_target_pairs={{0,96},{32,0},{64,32},{96,64},{1,97},{33,1},{65,33},{97,65},{2,98}... | collective-permute-start | bytes 884744 | tf_op jit(solution)/shard_map/ppermute | solution.py:219
  121.1 11.5 %collective-permute-start.23 = (f32[576,128]{1,0:T(8,128)S(1)}, f32[576,128]{1,0:T(8,128)S(1)}, u32[]{:S(2)}, u32[]{:S(2)}) collective-permute-start(f32[576,128]{1,0:T(8,128)S(1)} %get-tuple-element.27), channel_id=1, source_target_pairs={{0,64},{32,96},{64,0},{96,32},{1,65},{33,97},{65,1},{97,33},{2,66}... | collective-permute-start | bytes 884744 | tf_op jit(solution)/shard_map/ppermute | solution.py:219
  121.4 16.3 %collective-permute-start.22 = (f32[576,128]{1,0:T(8,128)S(1)}, f32[576,128]{1,0:T(8,128)S(1)}, u32[]{:S(2)}, u32[]{:S(2)}) collective-permute-start(f32[576,128]{1,0:T(8,128)S(1)} %get-tuple-element.26), channel_id=1, source_target_pairs={{0,32},{32,64},{64,96},{96,0},{1,33},{33,65},{65,97},{97,1},{2,34}... | collective-permute-start | bytes 884744 | tf_op jit(solution)/shard_map/ppermute | solution.py:219
  137.7 1.3 collective-permute-start.25
  140.2 25.7 %all-to-all-start.2 = ((f32[8,320,128]{2,1,0:T(8,128)}), f32[8,320,128]{2,1,0:T(8,128)S(1)}, u32[]{:S(2)}, u32[]{:S(2)}) async-start(f32[8,320,128]{2,1,0:T(8,128)} %share0.1), calls=%async_computation.2 | async-start | bytes 2621440 | tf_op jit(solution)/shard_map/all_to_all | solution.py:210
  157.7 2.7 %collective-permute-start.26 = (f32[2048,128]{1,0:T(8,128)S(1)}, f32[2048,128]{1,0:T(8,128)S(1)}, u32[]{:S(2)}, u32[]{:S(2)}) collective-permute-start(f32[2048,128]{1,0:T(8,128)S(1)} %bitcast.33), channel_id=1, source_target_pairs={{0,1},{1,0},{2,3},{3,2},{4,5},{5,4},{6,7},{7,6},{8,9},{9,8},{10,11... | collective-permute-start | bytes 3145736 | tf_op jit(solution)/shard_map/ppermute | solution.py:214
  165.9 46.6 %all-to-all-start.3 = ((f32[8,256,128]{2,1,0:T(8,128)}), f32[8,256,128]{2,1,0:T(8,128)S(1)}, u32[]{:S(2)}, u32[]{:S(2)}) async-start(f32[8,256,128]{2,1,0:T(8,128)} %bitcast.12), calls=%async_computation.3 | async-start | bytes 2097152 | tf_op jit(solution)/shard_map/all_to_all | solution.py:210

commit v3 on v2

v3 whole, which is shorter than its diff:
```python
import functools

import jax
import jax.numpy as jnp
from jax import lax
from jax.experimental import pallas as pl
from jax.experimental.pallas import tpu as pltpu
from jax.sharding import Mesh
from jax.sharding import PartitionSpec as P

EDGE = 128
BLOCK = 32
ROW_AXES = ("y", "xh")
COL_AXES = ("xl", "z", "core")
PLANE_AXES = ("xl", "z")
VMEM_LIMIT = 40 << 20


def split(value):
    high = value.astype(jnp.bfloat16)
    low = (value - high.astype(jnp.float32)).astype(jnp.bfloat16)
    return high, low


def dot3(left, right, dims=((1,), (0,))):
    dot = functools.partial(
        lax.dot_general, dimension_numbers=(dims, ((), ())), preferred_element_type=jnp.float32
    )
    left_high, left_low = split(left)
    right_high, right_low = split(right)
    return dot(left_high, right_high) + (dot(left_high, right_low) + dot(left_low, right_high))


def spread_body(flipped, n_src, n_out, take, put, count, tiles, *refs):
    sources, outs = refs[:n_src], refs[-4 - n_out : -4]
    paired, total, held, arrived = refs[-4:]
    slots = held.shape[0]

    def fetch(index):
        here = pl.ds(index * BLOCK, BLOCK)
        return pltpu.make_async_copy(tiles.at[here], held.at[here], arrived.at[index])

    for index in range(slots // BLOCK):

        @pl.when(index * BLOCK < count[0])
        def _(index=index):
            fetch(index).start()

    total[...] = jnp.zeros_like(total)
    rows = paired.shape[0] // n_src
    for place, source in enumerate(sources):

        def pair(index, carry, source=source, first=place * rows):
            high, low = split(source[pl.ds(pl.multiple_of(index * EDGE, EDGE), EDGE), :])
            paired[first + index, :EDGE, :EDGE] = high
            paired[first + index, :EDGE, EDGE:] = low
            paired[first + index, EDGE:, :EDGE] = high
            paired[first + index, EDGE:, EDGE:] = jnp.zeros_like(low)
            return carry

        lax.fori_loop(0, rows, pair, 0)

    def block(index, masked):
        for offset in range(BLOCK):
            slot = index * BLOCK + offset
            tile = held[slot]
            if masked:
                tile = jnp.where(slot < count[0], tile, 0.0)
            high, low = split(tile.T if flipped else tile)
            both = jnp.dot(
                jnp.concatenate([high, low], axis=1),
                paired[take[slot]],
                preferred_element_type=jnp.float32,
            )
            total[put[slot]] += both[:, :EDGE] + both[:, EDGE:]

    def whole_block(index, carry):
        fetch(index).wait()
        block(index, False)
        return carry

    blocks = count[0] // BLOCK
    lax.fori_loop(0, blocks, whole_block, 0)

    @pl.when(blocks * BLOCK < count[0])
    def _():
        fetch(blocks).wait()
        block(blocks, True)

    place = 0
    for out in outs:
        for index in range(out.shape[0] // EDGE):
            out[index * EDGE : (index + 1) * EDGE] = total[place + index]
        place += out.shape[0] // EDGE


def spread(tiles, take, put, count, sources, rows, out_rows, flipped, after, name):
    slots = tiles.shape[0]
    src_count = len(sources) * rows // EDGE
    scalars, here = pl.BlockSpec(memory_space=pltpu.SMEM), pl.BlockSpec(memory_space=pltpu.VMEM)
    there = pl.BlockSpec(memory_space=pl.ANY)
    return pl.pallas_call(
        functools.partial(spread_body, flipped, len(sources), len(out_rows)),
        in_specs=[scalars] * 3 + [there] + [here] * len(sources) + [there] * len(after),
        out_specs=[here] * len(out_rows),
        scratch_shapes=[
            pltpu.VMEM((src_count, 2 * EDGE, 2 * EDGE), jnp.bfloat16),
            pltpu.VMEM((sum(out_rows) // EDGE, EDGE, EDGE), jnp.float32),
            pltpu.VMEM(tiles.shape, jnp.float32),
            pltpu.SemaphoreType.DMA((slots // BLOCK,)),
        ],
        out_shape=[jax.ShapeDtypeStruct((n, EDGE), jnp.float32) for n in out_rows],
        compiler_params=pltpu.CompilerParams(vmem_limit_bytes=VMEM_LIMIT),
        cost_estimate=pl.CostEstimate(
            flops=2 * slots * EDGE * 4 * EDGE * EDGE,
            bytes_accessed=slots * EDGE * EDGE * 4,
            transcendentals=0,
        ),
        name=name,
    )(take, put, count, tiles, *sources, *after)


def whole_call(kernel, outs, *args, skipped=0, name):
    here, there = pl.BlockSpec(memory_space=pltpu.VMEM), pl.BlockSpec(memory_space=pl.ANY)
    return pl.pallas_call(
        kernel,
        in_specs=[here] * (len(args) - skipped) + [there] * skipped,
        out_specs=[here] * len(outs),
        out_shape=[jax.ShapeDtypeStruct(shape, jnp.float32) for shape in outs],
        compiler_params=pltpu.CompilerParams(vmem_limit_bytes=VMEM_LIMIT),
        name=name,
    )(*args)


def added(terms):
    values = [term[...] for term in terms]
    while len(values) > 1:
        if len(values) % 2:
            values = [values[0] + values[1]] + values[2:]
        half = len(values) // 2
        values = [left + right for left, right in zip(values[:half], values[half:])] if half else values
    return values[0]


def middle_body(n_first, n_second, *refs):
    firsts, seconds, rest = refs[:n_first], refs[n_first : n_first + n_second], refs[n_first + n_second :]
    weight, out_grad, hidden, grad0, grad1, gathered, grad_pre = rest
    mixed = jnp.concatenate([added(firsts), added(seconds)], axis=1)
    gathered[...] = mixed
    pre_act = dot3(mixed, weight[...])
    sigma = jax.nn.sigmoid(pre_act)
    hidden[...] = pre_act * sigma
    slope = sigma * (1.0 + pre_act * (1.0 - sigma))
    local = out_grad[...] * slope
    grad_pre[...] = local
    back = dot3(local, weight[...], ((1,), (1,)))
    grad0[...] = back[:, :EDGE]
    grad1[...] = back[:, EDGE:]


def weight_body(gathered, grad_pre, out):
    term = dot3(gathered[...], grad_pre[...], ((0,), (0,)))
    me = lax.axis_index("xh")
    n_y, piece = out.shape[1], out.shape[2] // 2
    for place in range(n_y):
        for half in range(2):
            first = (place * 2 + half) * piece
            for side in range(2):
                out[half ^ me, place, side * piece : (side + 1) * piece, :] = term[
                    first : first + piece, side * EDGE : (side + 1) * EDGE
                ]


def pair_body(mine, other, *refs):
    out = refs[-1]
    rows = mine.shape[0]
    out[:rows] = mine[...]
    out[rows:] = other[...]


def ring_body(n_ring, grad, other, weight_part, *refs):
    outs = refs[-n_ring:]
    me = lax.axis_index("y")
    rows = grad.shape[0]
    piece = weight_part.shape[1]
    for step, out in enumerate(outs):
        out[:rows] = grad[...]
        out[rows : 2 * rows] = other[:rows]
        place = lax.rem(me + step, n_ring)
        out[2 * rows :] = weight_part[place] + other[pl.ds(rows + place * piece, piece), :]


def fold_body(n_terms, *refs):
    terms, (own, other) = refs[:n_terms], refs[n_terms:]
    total = added(terms)
    rows = own.shape[0]
    own[...] = total[:rows]
    other[...] = total[rows : 2 * rows]


def share_body(mine, other, piece, other_piece, *outs):
    rows = mine.shape[0] // len(outs)
    both = piece[...] + other_piece[...]
    for step, out in enumerate(outs):
        here = pl.ds(step * rows, rows)
        out[:rows] = mine[here, :] + other[here, :]
        out[rows:] = both


def fold_share_body(n_terms, *refs):
    terms, (own, other) = refs[:n_terms], refs[n_terms:]
    total = added(terms)
    rows = own.shape[0]
    own[...] = total[:rows]
    other[...] = total[rows:]


def add_body(mine, other, *outs):
    rows = mine.shape[0] // len(outs)
    for step, out in enumerate(outs):
        here = pl.ds(step * rows, rows)
        out[...] = mine[here, :] + other[here, :]


def finish_body(grad0, other0, *refs):
    terms, out = refs[:-1], refs[-1]
    out[:, :EDGE] = grad0[...] + other0[: grad0.shape[0]]
    out[:, EDGE:] = added(terms)


def assemble_body(scale, n_ring, own, other, out):
    count = own.shape[0] // (2 * n_ring)
    for step in range(n_ring):
        ring = lax.rem(lax.axis_index("y") + n_ring - step, n_ring)
        for half, pieces in enumerate((own, other)):
            first = (ring * 2 + (lax.axis_index("xh") ^ half)) * count
            here = pl.ds(pl.multiple_of(first, count), count)
            for side in range(2):
                place = (step * 2 + side) * count
                out[here, side * EDGE : (side + 1) * EDGE] = pieces[place : place + count, :] * scale


def swap(value, axis):
    return lax.ppermute(value, axis, [(0, 1), (1, 0)])


def ring_send(value, axis, step):
    size = lax.axis_size(axis)
    return lax.ppermute(value, axis, [(place, (place + step) % size) for place in range(size)])


def offset_send(value, axes, ring, offset):
    sizes = [lax.axis_size(axis) for axis in axes]
    hops = []
    for a in range(sizes[0]):
        for b in range(sizes[1]):
            if axes[0] == ring:
                to = (a + offset // 2) % sizes[0], b ^ (offset % 2)
            else:
                to = a ^ (offset % 2), (b + offset // 2) % sizes[1]
            hops.append((a * sizes[1] + b, to[0] * sizes[1] + to[1]))
    return lax.ppermute(value, axes, hops)


def offset_of(ring_index, pair_index, ring, pair, sign):
    step = (sign * (lax.axis_index(ring) - ring_index)) % lax.axis_size(ring)
    return step * 2 + (pair_index ^ lax.axis_index(pair))


def body(features, weight, tile_vals, tile_index, tile_count, out_grad):
    tiles = tile_vals[0, 0]
    dest = tile_index[0, 0, 0]
    src = tile_index[0, 0, 1]
    count = tile_count[0]
    n_row = lax.axis_size(ROW_AXES)
    n_col = lax.axis_size(COL_AXES)
    n_plane = lax.axis_size(PLANE_AXES)
    n_z = lax.axis_size("z")
    n_y = lax.axis_size("y")
    rows, width = features.shape
    per = rows // EDGE
    half_tiles = n_plane * per
    src_home, src_tile = src // per, src % per
    src_half = ((src_home % 2) ^ lax.axis_index("core")) * half_tiles + src_tile
    dest_home, dest_tile = dest // per, dest % per

    def src_place(sign):
        plane = src_home // 2
        return src_half + per * offset_of(plane % n_z, plane // n_z, "z", "xl", sign)

    def dest_place(sign):
        return dest_tile + per * offset_of(dest_home // 2, dest_home % 2, "y", "xh", sign)

    live = jnp.arange(tiles.shape[0], dtype=jnp.int32) < count[0]
    src_take, dest_put, dest_take, src_put = [
        jnp.where(live, index, 0).astype(jnp.int32)
        for index in (src_place(1), dest_place(-1), dest_place(1), src_place(-1))
    ]

    half = (rows, EDGE)
    full = (rows, width)
    terms = []
    before = []
    for chunk in range(2):
        part = features[:, chunk * EDGE : (chunk + 1) * EDGE]
        (both,) = whole_call(
            pair_body,
            [(2 * rows, EDGE)],
            part,
            swap(part, "xl"),
            *before,
            skipped=len(before),
            name=f"pair{chunk}",
        )
        mine = [both] + [ring_send(both, "z", step) for step in range(1, 4)]
        before = mine[1:]
        other = [swap(value, "core") for value in mine]
        partials = spread(
            tiles,
            src_take,
            dest_put,
            count,
            mine + other,
            2 * rows,
            [2 * rows] * n_y if chunk == 0 else [rows] * n_row,
            False,
            [],
            f"forward{chunk}",
        )
        if chunk == 0:
            arrived = [ring_send(partials[step], "y", step) for step in range(1, 4)]
            own, other = whole_call(
                functools.partial(fold_body, n_y), [half, half], partials[0], *arrived, name="fold0"
            )
            terms.append([own, swap(other, "xh")])
        else:
            terms.append(
                [partials[0]]
                + [offset_send(partials[offset], ROW_AXES, "y", offset) for offset in range(1, n_row)]
            )
    hidden, grad0, grad1, gathered, grad_pre = whole_call(
        functools.partial(middle_body, len(terms[0]), len(terms[1])),
        [full, half, half, full, full],
        *terms[0],
        *terms[1],
        weight,
        out_grad,
        name="middle",
    )

    (both,) = whole_call(pair_body, [(2 * rows, EDGE)], grad0, swap(grad0, "xh"), name="pair2")
    received = [both] + [ring_send(both, "y", step) for step in range(1, 4)]
    received0 = received
    piece_rows = 2 * width // n_row
    (weight_part,) = whole_call(
        weight_body, [(2, n_y, piece_rows, EDGE)], gathered, grad_pre, name="weight_term"
    )
    other = swap(jnp.concatenate([grad1, weight_part[1].reshape(-1, EDGE)], axis=0), "xh")
    sends = whole_call(
        functools.partial(ring_body, n_y),
        [(2 * rows + piece_rows, EDGE)] * n_y,
        grad1,
        other,
        weight_part[0],
        name="ring",
    )
    received1 = [sends[0]] + [ring_send(sends[step], "y", step) for step in range(1, n_y)]
    piece = sum(value[2 * rows :] for value in received1)

    for chunk, received in enumerate((received0, received1)):
        mine, other = spread(
            tiles,
            dest_take,
            src_put,
            count,
            received,
            2 * rows,
            [half_tiles * EDGE] * 2,
            True,
            sends[1:2] if chunk == 0 else [],
            f"backward{chunk}",
        )
        other = swap(other, "core")
        if chunk == 0:
            shares = whole_call(
                share_body,
                [(2 * rows + piece_rows, EDGE)] * n_z,
                mine,
                other,
                piece,
                swap(piece, "core"),
                name="share0",
            )
            arrived = [ring_send(shares[step], "z", step) for step in range(1, 4)]
            grad_x0, other0 = whole_call(
                functools.partial(fold_share_body, n_z),
                [half, (rows + piece_rows, EDGE)],
                shares[0],
                *arrived,
                name="fold1",
            )
            arrived0 = swap(other0, "xl")
        else:
            shares = whole_call(add_body, [half] * n_plane, mine, other, name="share1")
            arrived = [
                offset_send(shares[offset], PLANE_AXES, "z", offset) for offset in range(1, n_plane)
            ]
            (grad_x,) = whole_call(
                finish_body, [full], grad_x0, arrived0, shares[0], *arrived, name="finish"
            )
    piece = other0[rows:] + arrived0[rows:]
    pieces = [piece] + [ring_send(piece, "y", step) for step in range(1, 4)]
    pieces = jnp.concatenate(pieces, axis=0)
    scale = (rows * n_row * n_col) ** (-0.5)
    (grad_w,) = whole_call(
        functools.partial(assemble_body, scale, n_y),
        [(width, width)],
        pieces,
        swap(pieces, "xh"),
        name="assemble",
    )
    return hidden, grad_x, grad_w


def solution(mesh):
    chips = Mesh(mesh.devices.reshape(4, 2, 2, 4, 2), ROW_AXES + COL_AXES)
    placed = (
        P(ROW_AXES + COL_AXES, None),
        P(),
        P(COL_AXES, ROW_AXES, None, None, None),
        P(COL_AXES, ROW_AXES, None, None),
        P(COL_AXES, ROW_AXES),
        P(COL_AXES + ROW_AXES, None),
    )
    return jax.shard_map(
        body,
        mesh=chips,
        in_specs=placed,
        out_specs=(P(COL_AXES + ROW_AXES, None), P(ROW_AXES + COL_AXES, None), P()),
        check_vma=False,
    )
```

time: 216 us -> 169 us (0.78)
  blocking collectives: 61.4 us -> 0 us
  starting transfers between devices: 40 us -> 82.6 us
  Pallas kernels: 42.2 us -> 18.9 us
  waiting for transfers between devices: 65.5 us -> 63.2 us
    all_gather x1 -> x0, blocking collectives: 42 us -> none  [body(): pieces = lax.all_gather(piece, ROW_AXES, axis=0, tiled=False)]
    ppermute x0 -> x14, starting transfers between devices: none -> 30.7 us  [offset_send(): return lax.ppermute(value, axes, hops)]
    pallas_call x4, Pallas kernels: 37.4 us -> 15.5 us  [spread(): pl.pallas_call(functools.partial(spread_body, flipped, len(sources), len(...]
    ppermute x12 -> x21, starting transfers between devices: 17.3 us -> 39.3 us  [ring_send(): lax.ppermute(value, axis, [(place, (place + step) % size) for place in ra...]
    all_to_all x1 -> x0, blocking collectives: 19.4 us -> none  [exchange(): return lax.all_to_all(value, axes, 0, 0, tiled=True)]
    all_to_all x3 -> x0, starting transfers between devices: 16.3 us -> none  [exchange(): return lax.all_to_all(value, axes, 0, 0, tiled=True)]
    ppermute x12 -> x21, waiting for transfers between devices: 31.3 us -> 42.3 us  [ring_send(): lax.ppermute(value, axis, [(place, (place + step) % size) for place in ra...]
    all_to_all x3 -> x0, waiting for transfers between devices: 9.84 us -> none  [exchange(): return lax.all_to_all(value, axes, 0, 0, tiled=True)]
  transfers between devices with their start and end apart: 30 -> 53, of which waited for: 18 -> 21; matrix products, arithmetic and copies ran while one was open for 1% -> 1% of each run, Pallas kernels for 14% -> 10%
where the time goes in v3:
time: 169 us; the launch traced here: 168 us
  starting transfers between devices  82.6 us (49%)
  waiting for transfers between devices  63.2 us (37%)
  Pallas kernels  18.9 us (11%)
  local copies, waits for them, and re-layouts  1.78 us (1%)
    ppermute x21, waiting for transfers between devices, ring_send(): lax.ppermute(value, axis, [(place, (place + step) % size) for place in ra...  42.3 us
    ppermute x21, starting transfers between devices, ring_send(): lax.ppermute(value, axis, [(place, (place + step) % size) for place in ra...  39.3 us
    ppermute x14, starting transfers between devices, offset_send(): return lax.ppermute(value, axes, hops)  30.7 us
    ppermute x18, waiting for transfers between devices, swap(): return lax.ppermute(value, axis, [(0, 1), (1, 0)])  16.7 us
    pallas_call x4, Pallas kernels, spread(): pl.pallas_call(functools.partial(spread_body, flipped, len(sources), len(...  15.5 us
    ppermute x18, starting transfers between devices, swap(): return lax.ppermute(value, axis, [(0, 1), (1, 0)])  12.5 us
    ppermute x14, waiting for transfers between devices, offset_send(): return lax.ppermute(value, axes, hops)  4.17 us
    pallas_call x12, Pallas kernels, whole_call(): pl.pallas_call(kernel, in_specs=[here] * (len(args) - skipped) + [there]...  3.4 us
  transfers between devices with their start and end apart: 53, of which 21 were waited for; matrix products, arithmetic and copies ran while one was open for 1% of the time, Pallas kernels for 10%

profile of v3, /device:TPU:0, one launch (start us, length us, event | category | flops | bytes accessed | tf_op | source)
XLA Modules:
  0.0 168.1 jit_solution(7773172066832482821)
XLA Ops:
  3.7 4.4 %collective-permute-done.other = f32[256,128]{1,0:T(8,128)S(1)} collective-permute-done((f32[256,128]{1,0:T(8,128)S(1)}, f32[256,128]{1,0:T(8,128)S(1)}, u32[]{:S(2)}, u32[]{:S(2)}) %collective-permute-start) | collective-permute-done | bytes 131104 | tf_op jit(solution)/shard_map/ppermute | solution.py:244
  10.2 3.6 %collective-permute-start.2 = (f32[512,128]{1,0:T(8,128)S(1)}, f32[512,128]{1,0:T(8,128)S(1)}, u32[]{:S(2)}, u32[]{:S(2)}) collective-permute-start(f32[512,128]{1,0:T(8,128)S(1)} %pair0.1.refs_0_), channel_id=1, source_target_pairs={{0,4},{2,6},{4,0},{6,2},{1,5},{3,7},{5,1},{7,3},{8,12},{10,14},{12... | collective-permute-start | bytes 786440 | tf_op jit(solution)/shard_map/ppermute | solution.py:249
  16.3 2.4 %collective-permute-done.1.refs_1_.refs_0_ = f32[512,128]{1,0:T(8,128)S(1)} collective-permute-done((f32[512,128]{1,0:T(8,128)S(1)}, f32[512,128]{1,0:T(8,128)S(1)}, u32[]{:S(2)}, u32[]{:S(2)}) %collective-permute-start.1) | collective-permute-done | bytes 262176 | tf_op jit(solution)/shard_map/ppermute | solution.py:249
  18.8 4.6 %collective-permute-done.2.refs_2_.refs_1_ = f32[512,128]{1,0:T(8,128)S(1)} collective-permute-done((f32[512,128]{1,0:T(8,128)S(1)}, f32[512,128]{1,0:T(8,128)S(1)}, u32[]{:S(2)}, u32[]{:S(2)}) %collective-permute-start.2) | collective-permute-done | bytes 262176 | tf_op jit(solution)/shard_map/ppermute | solution.py:249
  24.8 2.4 %collective-permute-start.14 = (f32[512,128]{1,0:T(8,128)S(1)}, f32[512,128]{1,0:T(8,128)S(1)}, u32[]{:S(2)}, u32[]{:S(2)}) collective-permute-start(f32[512,128]{1,0:T(8,128)S(1)} %pair1.1.refs_0_), channel_id=1, source_target_pairs={{0,4},{2,6},{4,0},{6,2},{1,5},{3,7},{5,1},{7,3},{8,12},{10,14},{12... | collective-permute-start | bytes 786440 | tf_op jit(solution)/shard_map/ppermute | solution.py:249
  28.4 3.8 %forward0.1 = (f32[512,128]{1,0:T(8,128)S(1)}, f32[512,128]{1,0:T(8,128)S(1)}, f32[512,128]{1,0:T(8,128)S(1)}, f32[512,128]{1,0:T(8,128)S(1)}) custom-call(s32[256]{0:T(256)S(1)} %add_select_fusion.3.take, s32[256]{0:T(256)S(1)} %add_select_fusion.2.put, s32[1]{0:T(128)} %bitcast.11.count, f32[256,128,128]{2,1,0:T(8,128)} %bitcast.15, ...), custom_call_target="tpu_custom_call" | custom-call | flops 4294967296 | bytes 16777216 | tf_op jit(solution)/shard_map/forward0/pallas_call | solution.py:102
  33.9 3.6 %collective-permute-start.9 = (f32[512,128]{1,0:T(8,128)S(1)}, f32[512,128]{1,0:T(8,128)S(1)}, u32[]{:S(2)}, u32[]{:S(2)}) collective-permute-start(f32[512,128]{1,0:T(8,128)S(1)} %get-tuple-element.46), channel_id=1, source_target_pairs={{0,64},{32,96},{64,0},{96,32},{1,65},{33,97},{65,1},{97,33},{2,66}... | collective-permute-start | bytes 786440 | tf_op jit(solution)/shard_map/ppermute | solution.py:249
  40.0 2.4 %collective-permute-done.8.refs_1_ = f32[512,128]{1,0:T(8,128)S(1)} collective-permute-done((f32[512,128]{1,0:T(8,128)S(1)}, f32[512,128]{1,0:T(8,128)S(1)}, u32[]{:S(2)}, u32[]{:S(2)}) %collective-permute-start.8) | collective-permute-done | bytes 262176 | tf_op jit(solution)/shard_map/ppermute | solution.py:249
  42.3 6.6 %collective-permute-done.9.refs_2_ = f32[512,128]{1,0:T(8,128)S(1)} collective-permute-done((f32[512,128]{1,0:T(8,128)S(1)}, f32[512,128]{1,0:T(8,128)S(1)}, u32[]{:S(2)}, u32[]{:S(2)}) %collective-permute-start.9) | collective-permute-done | bytes 262176 | tf_op jit(solution)/shard_map/ppermute | solution.py:249
  49.0 2.5 %collective-permute-start.11 = (f32[256,128]{1,0:T(8,128)S(1)}, f32[256,128]{1,0:T(8,128)S(1)}, u32[]{:S(2)}, u32[]{:S(2)}) collective-permute-start(f32[256,128]{1,0:T(8,128)S(1)} %get-tuple-element.49), channel_id=1, source_target_pairs={{0,16},{16,0},{1,17},{17,1},{2,18},{18,2},{3,19},{19,3},{4,20},{20... | collective-permute-start | bytes 393224 | tf_op jit(solution)/shard_map/ppermute | solution.py:244
  51.6 3.8 %forward1.1 = (f32[256,128]{1,0:T(8,128)S(1)}, f32[256,128]{1,0:T(8,128)S(1)}, f32[256,128]{1,0:T(8,128)S(1)}, f32[256,128]{1,0:T(8,128)S(1)}, f32[256,128]{1,0:...) custom-call(s32[256]{0:T(256)S(1)} %add_select_fusion.3.take, ...), custom_call_target="tpu_custom_call" | custom-call | flops 4294967296 | bytes 16777216 | tf_op jit(solution)/shard_map/forward1/pallas_call | solution.py:102
  58.5 3.0 %collective-permute-start.22 = (f32[256,128]{1,0:T(8,128)S(1)}, f32[256,128]{1,0:T(8,128)S(1)}, u32[]{:S(2)}, u32[]{:S(2)}) collective-permute-start(f32[256,128]{1,0:T(8,128)S(1)} %get-tuple-element.53), channel_id=1, source_target_pairs={{0,48},{16,32},{32,80},{48,64},{64,112},{80,96},{96,16},{112,0},{1... | collective-permute-start | bytes 393224 | tf_op jit(solution)/shard_map/ppermute | solution.py:262
  65.0 2.7 %collective-permute-start.25 = (f32[256,128]{1,0:T(8,128)S(1)}, f32[256,128]{1,0:T(8,128)S(1)}, u32[]{:S(2)}, u32[]{:S(2)}) collective-permute-start(f32[256,128]{1,0:T(8,128)S(1)} %get-tuple-element.56), channel_id=1, source_target_pairs={{0,96},{16,112},{32,0},{48,16},{64,32},{80,48},{96,64},{112,80},{1... | collective-permute-start | bytes 393224 | tf_op jit(solution)/shard_map/ppermute | solution.py:262
  67.7 5.9 %collective-permute-start.26 = (f32[256,128]{1,0:T(8,128)S(1)}, f32[256,128]{1,0:T(8,128)S(1)}, u32[]{:S(2)}, u32[]{:S(2)}) collective-permute-start(f32[256,128]{1,0:T(8,128)S(1)} %get-tuple-element.57), channel_id=1, source_target_pairs={{0,112},{16,96},{32,16},{48,0},{64,48},{80,32},{96,80},{112,64},{1... | collective-permute-start | bytes 393224 | tf_op jit(solution)/shard_map/ppermute | solution.py:262
  78.9 2.3 %collective-permute-start.31 = (f32[512,128]{1,0:T(8,128)S(1)}, f32[512,128]{1,0:T(8,128)S(1)}, u32[]{:S(2)}, u32[]{:S(2)}) collective-permute-start(f32[512,128]{1,0:T(8,128)S(1)} %pad_maximum_fusion), channel_id=1, source_target_pairs={{0,16},{16,0},{1,17},{17,1},{2,18},{18,2},{3,19},{19,3},{4,20},{20... | collective-permute-start | bytes 786440 | tf_op jit(solution)/shard_map/ppermute | solution.py:244
  81.2 3.7 %collective-permute-done.27.other = f32[256,128]{1,0:T(8,128)S(1)} collective-permute-done((f32[256,128]{1,0:T(8,128)S(1)}, f32[256,128]{1,0:T(8,128)S(1)}, u32[]{:S(2)}, u32[]{:S(2)}) %collective-permute-start.27) | collective-permute-done | bytes 131104 | tf_op jit(solution)/shard_map/ppermute | solution.py:244
  86.4 3.4 %collective-permute-start.29 = (f32[512,128]{1,0:T(8,128)S(1)}, f32[512,128]{1,0:T(8,128)S(1)}, u32[]{:S(2)}, u32[]{:S(2)}) collective-permute-start(f32[512,128]{1,0:T(8,128)S(1)} %pair2.1.refs_0_), channel_id=1, source_target_pairs={{0,64},{32,96},{64,0},{96,32},{1,65},{33,97},{65,1},{97,33},{2,66}... | collective-permute-start | bytes 786440 | tf_op jit(solution)/shard_map/ppermute | solution.py:249
  90.1 2.3 %collective-permute-start.35 = (f32[576,128]{1,0:T(8,128)S(1)}, f32[576,128]{1,0:T(8,128)S(1)}, u32[]{:S(2)}, u32[]{:S(2)}) collective-permute-start(f32[576,128]{1,0:T(8,128)S(1)} %get-tuple-element.68), channel_id=1, source_target_pairs={{0,96},{32,0},{64,32},{96,64},{1,97},{33,1},{65,33},{97,65},{2,98}... | collective-permute-start | bytes 884744 | tf_op jit(solution)/shard_map/ppermute | solution.py:249
  94.0 7.8 %collective-permute-done.28.refs_1_ = f32[512,128]{1,0:T(8,128)S(1)} collective-permute-done((f32[512,128]{1,0:T(8,128)S(1)}, f32[512,128]{1,0:T(8,128)S(1)}, u32[]{:S(2)}, u32[]{:S(2)}) %collective-permute-start.28) | collective-permute-done | bytes 262176 | tf_op jit(solution)/shard_map/ppermute | solution.py:249
  102.6 3.9 %backward0.1 = (f32[2048,128]{1,0:T(8,128)S(1)}, f32[2048,128]{1,0:T(8,128)S(1)}) custom-call(s32[256]{0:T(256)S(1)} %get-tuple-element.98.take, s32[256]{0:T(256)S(1)} %get-tuple-element.85.put, s32[1]{0:T(128)} %bitcast.13.count, f32[256,128,128]{2,1,0:T(8,128)} %bitcast.17, f32[512,128]{1,0:T(8,128)S(1)} %pair2.1.refs_0_, ...), custom_call_target="tpu_custom_call" | custom-call | flops 4294967296 | bytes 16777216 | tf_op jit(solution)/shard_map/backward0/pallas_call | solution.py:102
  107.1 3.1 %collective-permute-done.33.refs_1_ = f32[576,128]{1,0:T(8,128)S(1)} collective-permute-done((f32[576,128]{1,0:T(8,128)S(1)}, f32[576,128]{1,0:T(8,128)S(1)}, u32[]{:S(2)}, u32[]{:S(2)}) %collective-permute-start.33) | collective-permute-done | bytes 294944 | tf_op jit(solution)/shard_map/ppermute | solution.py:249
  110.2 3.9 %backward1.1 = (f32[2048,128]{1,0:T(8,128)S(1)}, f32[2048,128]{1,0:T(8,128)S(1)}) custom-call(s32[256]{0:T(256)S(1)} %get-tuple-element.98.take, s32[256]{0:T(256)S(1)} %get-tuple-element.85.put, s32[1]{0:T(128)} %bitcast.14.count, f32[256,128,128]{2,1,0:T(8,128)} %bitcast.18, f32[576,128]{1,0:T(8,128)S(1)} %get-tuple-element.66.refs_0_, ...), custom_call_target="tpu_custom_call" | custom-call | flops 4294967296 | bytes 16777216 | tf_op jit(solution)/shard_map/backward1/pallas_call | solution.py:102
  114.8 2.1 %collective-permute-done.36.other_piece = f32[64,128]{1,0:T(8,128)S(1)} collective-permute-done((f32[64,128]{1,0:T(8,128)S(1)}, f32[64,128]{1,0:T(8,128)S(1)}, u32[]{:S(2)}, u32[]{:S(2)}) %collective-permute-start.36) | collective-permute-done | bytes 32800 | tf_op jit(solution)/shard_map/ppermute | solution.py:244
  119.1 8.6 %collective-permute-start.38 = (f32[576,128]{1,0:T(8,128)S(1)}, f32[576,128]{1,0:T(8,128)S(1)}, u32[]{:S(2)}, u32[]{:S(2)}) collective-permute-start(f32[576,128]{1,0:T(8,128)S(1)} %get-tuple-element.71), channel_id=1, source_target_pairs={{0,4},{2,6},{4,0},{6,2},{1,5},{3,7},{5,1},{7,3},{8,12},{10,14},{12... | collective-permute-start | bytes 884744 | tf_op jit(solution)/shard_map/ppermute | solution.py:249
  127.7 5.8 %collective-permute-done.37.refs_1_ = f32[576,128]{1,0:T(8,128)S(1)} collective-permute-done((f32[576,128]{1,0:T(8,128)S(1)}, f32[576,128]{1,0:T(8,128)S(1)}, u32[]{:S(2)}, u32[]{:S(2)}) %collective-permute-start.37) | collective-permute-done | bytes 294944 | tf_op jit(solution)/shard_map/ppermute | solution.py:249
  133.5 7.5 %collective-permute-done.38.refs_2_ = f32[576,128]{1,0:T(8,128)S(1)} collective-permute-done((f32[576,128]{1,0:T(8,128)S(1)}, f32[576,128]{1,0:T(8,128)S(1)}, u32[]{:S(2)}, u32[]{:S(2)}) %collective-permute-start.38) | collective-permute-done | bytes 294944 | tf_op jit(solution)/shard_map/ppermute | solution.py:249
  141.3 2.1 %collective-permute-start.42 = (f32[256,128]{1,0:T(8,128)S(1)}, f32[256,128]{1,0:T(8,128)S(1)}, u32[]{:S(2)}, u32[]{:S(2)}) collective-permute-start(f32[256,128]{1,0:T(8,128)S(1)} %get-tuple-element.78), channel_id=1, source_target_pairs={{0,8},{2,10},{4,12},{6,14},{8,0},{10,2},{12,4},{14,6},{1,9},{3,11}... | collective-permute-start | bytes 393224 | tf_op jit(solution)/shard_map/ppermute | solution.py:262
  143.4 4.6 %collective-permute-done.40.other0 = f32[320,128]{1,0:T(8,128)S(1)} collective-permute-done((f32[320,128]{1,0:T(8,128)S(1)}, f32[320,128]{1,0:T(8,128)S(1)}, u32[]{:S(2)}, u32[]{:S(2)}) %collective-permute-start.40) | collective-permute-done | bytes 163872 | tf_op jit(solution)/shard_map/ppermute | solution.py:244
  151.9 3.6 %collective-permute-start.45 = (f32[256,128]{1,0:T(8,128)S(1)}, f32[256,128]{1,0:T(8,128)S(1)}, u32[]{:S(2)}, u32[]{:S(2)}) collective-permute-start(f32[256,128]{1,0:T(8,128)S(1)} %get-tuple-element.81), channel_id=1, source_target_pairs={{0,4},{2,6},{4,0},{6,2},{8,12},{10,14},{12,8},{14,10},{1,5},{3,7},... | collective-permute-start | bytes 393224 | tf_op jit(solution)/shard_map/ppermute | solution.py:262
  155.5 2.2 %collective-permute-start.47 = (f32[256,128]{1,0:T(8,128)S(1)}, f32[256,128]{1,0:T(8,128)S(1)}, u32[]{:S(2)}, u32[]{:S(2)}) collective-permute-start(f32[256,128]{1,0:T(8,128)S(1)} %get-tuple-element.83), channel_id=1, source_target_pairs={{0,6},{2,0},{4,2},{6,4},{8,14},{10,8},{12,10},{14,12},{1,7},{3,1},... | collective-permute-start | bytes 393224 | tf_op jit(solution)/shard_map/ppermute | solution.py:262
  157.7 2.8 %collective-permute-start.48 = (f32[256,128]{1,0:T(8,128)S(1)}, f32[256,128]{1,0:T(8,128)S(1)}, u32[]{:S(2)}, u32[]{:S(2)}) collective-permute-start(f32[256,128]{1,0:T(8,128)S(1)} %get-tuple-element.84), channel_id=1, source_target_pairs={{0,14},{2,8},{4,10},{6,12},{8,6},{10,0},{12,2},{14,4},{1,15},{3,9}... | collective-permute-start | bytes 393224 | tf_op jit(solution)/shard_map/ppermute | solution.py:262
  160.5 2.6 %collective-permute-start.52 = (f32[256,128]{1,0:T(8,128)S(1)}, f32[256,128]{1,0:T(8,128)S(1)}, u32[]{:S(2)}, u32[]{:S(2)}) collective-permute-start(f32[256,128]{1,0:T(8,128)S(1)} %pad_maximum_fusion.1.own), channel_id=1, source_target_pairs={{0,16},{16,0},{1,17},{17,1},{2,18},{18,2},{3,19},{19,3},{4,20},{20... | collective-permute-start | bytes 393224 | tf_op jit(solution)/shard_map/ppermute | solution.py:244
  (104 shorter events, 42.4 us)
Async XLA Ops:
  3.3 20.7 %collective-permute-start.12 = (f32[256,128]{1,0:T(8,128)S(1)}, f32[256,128]{1,0:T(8,128)S(1)}, u32[]{:S(2)}, u32[]{:S(2)}) collective-permute-start(f32[256,128]{1,0:T(8,128)S(1)} %get-tuple-element.94.mine), channel_id=1, source_target_pairs={{0,8},{8,0},{1,9},{9,1},{2,10},{10,2},{3,11},{11,3},{4,12},{12,4},... | collective-permute-start | bytes 393224 | tf_op jit(solution)/shard_map/ppermute | solution.py:244
  8.1 10.6 %collective-permute-start.1 = (f32[512,128]{1,0:T(8,128)S(1)}, f32[512,128]{1,0:T(8,128)S(1)}, u32[]{:S(2)}, u32[]{:S(2)}) collective-permute-start(f32[512,128]{1,0:T(8,128)S(1)} %pair0.1.refs_0_), channel_id=1, source_target_pairs={{0,2},{2,4},{4,6},{6,0},{1,3},{3,5},{5,7},{7,1},{8,10},{10,12},{12... | collective-permute-start | bytes 786440 | tf_op jit(solution)/shard_map/ppermute | solution.py:249
  10.2 13.2 %collective-permute-start.2 = (f32[512,128]{1,0:T(8,128)S(1)}, f32[512,128]{1,0:T(8,128)S(1)}, u32[]{:S(2)}, u32[]{:S(2)}) collective-permute-start(f32[512,128]{1,0:T(8,128)S(1)} %pair0.1.refs_0_), channel_id=1, source_target_pairs={{0,4},{2,6},{4,0},{6,2},{1,5},{3,7},{5,1},{7,3},{8,12},{10,14},{12... | collective-permute-start | bytes 786440 | tf_op jit(solution)/shard_map/ppermute | solution.py:249
  13.8 9.6 %collective-permute-start.3 = (f32[512,128]{1,0:T(8,128)S(1)}, f32[512,128]{1,0:T(8,128)S(1)}, u32[]{:S(2)}, u32[]{:S(2)}) collective-permute-start(f32[512,128]{1,0:T(8,128)S(1)} %pair0.1.refs_0_), channel_id=1, source_target_pairs={{0,6},{2,0},{4,2},{6,4},{1,7},{3,1},{5,3},{7,5},{8,14},{10,8},{12,... | collective-permute-start | bytes 786440 | tf_op jit(solution)/shard_map/ppermute | solution.py:249
  24.0 13.5 %collective-permute-start.13 = (f32[512,128]{1,0:T(8,128)S(1)}, f32[512,128]{1,0:T(8,128)S(1)}, u32[]{:S(2)}, u32[]{:S(2)}) collective-permute-start(f32[512,128]{1,0:T(8,128)S(1)} %pair1.1.refs_0_), channel_id=1, source_target_pairs={{0,2},{2,4},{4,6},{6,0},{1,3},{3,5},{5,7},{7,1},{8,10},{10,12},{12... | collective-permute-start | bytes 786440 | tf_op jit(solution)/shard_map/ppermute | solution.py:249
  24.8 14.7 %collective-permute-start.14 = (f32[512,128]{1,0:T(8,128)S(1)}, f32[512,128]{1,0:T(8,128)S(1)}, u32[]{:S(2)}, u32[]{:S(2)}) collective-permute-start(f32[512,128]{1,0:T(8,128)S(1)} %pair1.1.refs_0_), channel_id=1, source_target_pairs={{0,4},{2,6},{4,0},{6,2},{1,5},{3,7},{5,1},{7,3},{8,12},{10,14},{12... | collective-permute-start | bytes 786440 | tf_op jit(solution)/shard_map/ppermute | solution.py:249
  27.2 12.5 %collective-permute-start.15 = (f32[512,128]{1,0:T(8,128)S(1)}, f32[512,128]{1,0:T(8,128)S(1)}, u32[]{:S(2)}, u32[]{:S(2)}) collective-permute-start(f32[512,128]{1,0:T(8,128)S(1)} %pair1.1.refs_0_), channel_id=1, source_target_pairs={{0,6},{2,0},{4,2},{6,4},{1,7},{3,1},{5,3},{7,5},{8,14},{10,8},{12,... | collective-permute-start | bytes 786440 | tf_op jit(solution)/shard_map/ppermute | solution.py:249
  32.2 10.1 %collective-permute-start.8 = (f32[512,128]{1,0:T(8,128)S(1)}, f32[512,128]{1,0:T(8,128)S(1)}, u32[]{:S(2)}, u32[]{:S(2)}) collective-permute-start(f32[512,128]{1,0:T(8,128)S(1)} %get-tuple-element.45), channel_id=1, source_target_pairs={{0,32},{32,64},{64,96},{96,0},{1,33},{33,65},{65,97},{97,1},{2,34}... | collective-permute-start | bytes 786440 | tf_op jit(solution)/shard_map/ppermute | solution.py:249
  33.9 15.1 %collective-permute-start.9 = (f32[512,128]{1,0:T(8,128)S(1)}, f32[512,128]{1,0:T(8,128)S(1)}, u32[]{:S(2)}, u32[]{:S(2)}) collective-permute-start(f32[512,128]{1,0:T(8,128)S(1)} %get-tuple-element.46), channel_id=1, source_target_pairs={{0,64},{32,96},{64,0},{96,32},{1,65},{33,97},{65,1},{97,33},{2,66}... | collective-permute-start | bytes 786440 | tf_op jit(solution)/shard_map/ppermute | solution.py:249
  37.5 11.5 %collective-permute-start.10 = (f32[512,128]{1,0:T(8,128)S(1)}, f32[512,128]{1,0:T(8,128)S(1)}, u32[]{:S(2)}, u32[]{:S(2)}) collective-permute-start(f32[512,128]{1,0:T(8,128)S(1)} %get-tuple-element.47), channel_id=1, source_target_pairs={{0,96},{32,0},{64,32},{96,64},{1,97},{33,1},{65,33},{97,65},{2,98}... | collective-permute-start | bytes 786440 | tf_op jit(solution)/shard_map/ppermute | solution.py:249
  39.5 12.1 %collective-permute-start.16 = (f32[512,128]{1,0:T(8,128)S(1)}, f32[512,128]{1,0:T(8,128)S(1)}, u32[]{:S(2)}, u32[]{:S(2)}) collective-permute-start(f32[512,128]{1,0:T(8,128)S(1)} %pair1.1.refs_0_), channel_id=1, source_target_pairs={{0,1},{1,0},{2,3},{3,2},{4,5},{5,4},{6,7},{7,6},{8,9},{9,8},{10,11... | collective-permute-start | bytes 786440 | tf_op jit(solution)/shard_map/ppermute | solution.py:244
  39.7 11.8 %collective-permute-start.17 = (f32[512,128]{1,0:T(8,128)S(1)}, f32[512,128]{1,0:T(8,128)S(1)}, u32[]{:S(2)}, u32[]{:S(2)}) collective-permute-start(f32[512,128]{1,0:T(8,128)S(1)} %collective-permute-done.13.refs_1_), channel_id=1, source_target_pairs={{0,1},{1,0},{2,3},{3,2},{4,5},{5,4},{6,7},{7,6},{8,9},{9,8},{10,11... | collective-permute-start | bytes 786440 | tf_op jit(solution)/shard_map/ppermute | solution.py:244
  49.0 14.2 %collective-permute-start.11 = (f32[256,128]{1,0:T(8,128)S(1)}, f32[256,128]{1,0:T(8,128)S(1)}, u32[]{:S(2)}, u32[]{:S(2)}) collective-permute-start(f32[256,128]{1,0:T(8,128)S(1)} %get-tuple-element.49), channel_id=1, source_target_pairs={{0,16},{16,0},{1,17},{17,1},{2,18},{18,2},{3,19},{19,3},{4,20},{20... | collective-permute-start | bytes 393224 | tf_op jit(solution)/shard_map/ppermute | solution.py:244
  55.4 9.6 %collective-permute-start.20 = (f32[256,128]{1,0:T(8,128)S(1)}, f32[256,128]{1,0:T(8,128)S(1)}, u32[]{:S(2)}, u32[]{:S(2)}) collective-permute-start(f32[256,128]{1,0:T(8,128)S(1)} %get-tuple-element.51), channel_id=1, source_target_pairs={{0,16},{16,0},{32,48},{48,32},{64,80},{80,64},{96,112},{112,96},{1... | collective-permute-start | bytes 393224 | tf_op jit(solution)/shard_map/ppermute | solution.py:262
  56.7 11.0 %collective-permute-start.21 = (f32[256,128]{1,0:T(8,128)S(1)}, f32[256,128]{1,0:T(8,128)S(1)}, u32[]{:S(2)}, u32[]{:S(2)}) collective-permute-start(f32[256,128]{1,0:T(8,128)S(1)} %get-tuple-element.52), channel_id=1, source_target_pairs={{0,32},{16,48},{32,64},{48,80},{64,96},{80,112},{96,0},{112,16},{1... | collective-permute-start | bytes 393224 | tf_op jit(solution)/shard_map/ppermute | solution.py:262
  58.5 15.1 %collective-permute-start.22 = (f32[256,128]{1,0:T(8,128)S(1)}, f32[256,128]{1,0:T(8,128)S(1)}, u32[]{:S(2)}, u32[]{:S(2)}) collective-permute-start(f32[256,128]{1,0:T(8,128)S(1)} %get-tuple-element.53), channel_id=1, source_target_pairs={{0,48},{16,32},{32,80},{48,64},{64,112},{80,96},{96,16},{112,0},{1... | collective-permute-start | bytes 393224 | tf_op jit(solution)/shard_map/ppermute | solution.py:262
  61.5 12.1 %collective-permute-start.23 = (f32[256,128]{1,0:T(8,128)S(1)}, f32[256,128]{1,0:T(8,128)S(1)}, u32[]{:S(2)}, u32[]{:S(2)}) collective-permute-start(f32[256,128]{1,0:T(8,128)S(1)} %get-tuple-element.54), channel_id=1, source_target_pairs={{0,64},{16,80},{32,96},{48,112},{64,0},{80,16},{96,32},{112,48},{1... | collective-permute-start | bytes 393224 | tf_op jit(solution)/shard_map/ppermute | solution.py:262
  63.2 10.4 %collective-permute-start.24 = (f32[256,128]{1,0:T(8,128)S(1)}, f32[256,128]{1,0:T(8,128)S(1)}, u32[]{:S(2)}, u32[]{:S(2)}) collective-permute-start(f32[256,128]{1,0:T(8,128)S(1)} %get-tuple-element.55), channel_id=1, source_target_pairs={{0,80},{16,64},{32,112},{48,96},{64,16},{80,0},{96,48},{112,32},{1... | collective-permute-start | bytes 393224 | tf_op jit(solution)/shard_map/ppermute | solution.py:262
  65.0 10.6 %collective-permute-start.25 = (f32[256,128]{1,0:T(8,128)S(1)}, f32[256,128]{1,0:T(8,128)S(1)}, u32[]{:S(2)}, u32[]{:S(2)}) collective-permute-start(f32[256,128]{1,0:T(8,128)S(1)} %get-tuple-element.56), channel_id=1, source_target_pairs={{0,96},{16,112},{32,0},{48,16},{64,32},{80,48},{96,64},{112,80},{1... | collective-permute-start | bytes 393224 | tf_op jit(solution)/shard_map/ppermute | solution.py:262
  78.9 11.1 %collective-permute-start.31 = (f32[512,128]{1,0:T(8,128)S(1)}, f32[512,128]{1,0:T(8,128)S(1)}, u32[]{:S(2)}, u32[]{:S(2)}) collective-permute-start(f32[512,128]{1,0:T(8,128)S(1)} %pad_maximum_fusion), channel_id=1, source_target_pairs={{0,16},{16,0},{1,17},{17,1},{2,18},{18,2},{3,19},{19,3},{4,20},{20... | collective-permute-start | bytes 786440 | tf_op jit(solution)/shard_map/ppermute | solution.py:244
  85.0 16.8 %collective-permute-start.28 = (f32[512,128]{1,0:T(8,128)S(1)}, f32[512,128]{1,0:T(8,128)S(1)}, u32[]{:S(2)}, u32[]{:S(2)}) collective-permute-start(f32[512,128]{1,0:T(8,128)S(1)} %pair2.1.refs_0_), channel_id=1, source_target_pairs={{0,32},{32,64},{64,96},{96,0},{1,33},{33,65},{65,97},{97,1},{2,34}... | collective-permute-start | bytes 786440 | tf_op jit(solution)/shard_map/ppermute | solution.py:249
  86.4 16.2 %collective-permute-start.29 = (f32[512,128]{1,0:T(8,128)S(1)}, f32[512,128]{1,0:T(8,128)S(1)}, u32[]{:S(2)}, u32[]{:S(2)}) collective-permute-start(f32[512,128]{1,0:T(8,128)S(1)} %pair2.1.refs_0_), channel_id=1, source_target_pairs={{0,64},{32,96},{64,0},{96,32},{1,65},{33,97},{65,1},{97,33},{2,66}... | collective-permute-start | bytes 786440 | tf_op jit(solution)/shard_map/ppermute | solution.py:249
  89.8 12.8 %collective-permute-start.30 = (f32[512,128]{1,0:T(8,128)S(1)}, f32[512,128]{1,0:T(8,128)S(1)}, u32[]{:S(2)}, u32[]{:S(2)}) collective-permute-start(f32[512,128]{1,0:T(8,128)S(1)} %pair2.1.refs_0_), channel_id=1, source_target_pairs={{0,96},{32,0},{64,32},{96,64},{1,97},{33,1},{65,33},{97,65},{2,98}... | collective-permute-start | bytes 786440 | tf_op jit(solution)/shard_map/ppermute | solution.py:249
  90.1 16.6 %collective-permute-start.35 = (f32[576,128]{1,0:T(8,128)S(1)}, f32[576,128]{1,0:T(8,128)S(1)}, u32[]{:S(2)}, u32[]{:S(2)}) collective-permute-start(f32[576,128]{1,0:T(8,128)S(1)} %get-tuple-element.68), channel_id=1, source_target_pairs={{0,96},{32,0},{64,32},{96,64},{1,97},{33,1},{65,33},{97,65},{2,98}... | collective-permute-start | bytes 884744 | tf_op jit(solution)/shard_map/ppermute | solution.py:249
  92.4 14.7 %collective-permute-start.34 = (f32[576,128]{1,0:T(8,128)S(1)}, f32[576,128]{1,0:T(8,128)S(1)}, u32[]{:S(2)}, u32[]{:S(2)}) collective-permute-start(f32[576,128]{1,0:T(8,128)S(1)} %get-tuple-element.67), channel_id=1, source_target_pairs={{0,64},{32,96},{64,0},{96,32},{1,65},{33,97},{65,1},{97,33},{2,66}... | collective-permute-start | bytes 884744 | tf_op jit(solution)/shard_map/ppermute | solution.py:249
  106.6 10.4 %collective-permute-start.32 = (f32[2048,128]{1,0:T(8,128)S(1)}, f32[2048,128]{1,0:T(8,128)S(1)}, u32[]{:S(2)}, u32[]{:S(2)}) collective-permute-start(f32[2048,128]{1,0:T(8,128)S(1)} %get-tuple-element.65), channel_id=1, source_target_pairs={{0,1},{1,0},{2,3},{3,2},{4,5},{5,4},{6,7},{7,6},{8,9},{9,8},{10,11... | collective-permute-start | bytes 3145736 | tf_op jit(solution)/shard_map/ppermute | solution.py:244
  114.2 27.0 %collective-permute-start.41 = (f32[2048,128]{1,0:T(8,128)S(1)}, f32[2048,128]{1,0:T(8,128)S(1)}, u32[]{:S(2)}, u32[]{:S(2)}) collective-permute-start(f32[2048,128]{1,0:T(8,128)S(1)} %get-tuple-element.76), channel_id=1, source_target_pairs={{0,1},{1,0},{2,3},{3,2},{4,5},{5,4},{6,7},{7,6},{8,9},{9,8},{10,11... | collective-permute-start | bytes 3145736 | tf_op jit(solution)/shard_map/ppermute | solution.py:244
  117.1 16.5 %collective-permute-start.37 = (f32[576,128]{1,0:T(8,128)S(1)}, f32[576,128]{1,0:T(8,128)S(1)}, u32[]{:S(2)}, u32[]{:S(2)}) collective-permute-start(f32[576,128]{1,0:T(8,128)S(1)} %get-tuple-element.70), channel_id=1, source_target_pairs={{0,2},{2,4},{4,6},{6,0},{1,3},{3,5},{5,7},{7,1},{8,10},{10,12},{12... | collective-permute-start | bytes 884744 | tf_op jit(solution)/shard_map/ppermute | solution.py:249
  119.1 22.0 %collective-permute-start.38 = (f32[576,128]{1,0:T(8,128)S(1)}, f32[576,128]{1,0:T(8,128)S(1)}, u32[]{:S(2)}, u32[]{:S(2)}) collective-permute-start(f32[576,128]{1,0:T(8,128)S(1)} %get-tuple-element.71), channel_id=1, source_target_pairs={{0,4},{2,6},{4,0},{6,2},{1,5},{3,7},{5,1},{7,3},{8,12},{10,14},{12... | collective-permute-start | bytes 884744 | tf_op jit(solution)/shard_map/ppermute | solution.py:249
  127.7 13.3 %collective-permute-start.39 = (f32[576,128]{1,0:T(8,128)S(1)}, f32[576,128]{1,0:T(8,128)S(1)}, u32[]{:S(2)}, u32[]{:S(2)}) collective-permute-start(f32[576,128]{1,0:T(8,128)S(1)} %get-tuple-element.72), channel_id=1, source_target_pairs={{0,6},{2,0},{4,2},{6,4},{1,7},{3,1},{5,3},{7,5},{8,14},{10,8},{12,... | collective-permute-start | bytes 884744 | tf_op jit(solution)/shard_map/ppermute | solution.py:249
  150.0 10.5 %collective-permute-start.44 = (f32[256,128]{1,0:T(8,128)S(1)}, f32[256,128]{1,0:T(8,128)S(1)}, u32[]{:S(2)}, u32[]{:S(2)}) collective-permute-start(f32[256,128]{1,0:T(8,128)S(1)} %get-tuple-element.80), channel_id=1, source_target_pairs={{0,10},{2,12},{4,14},{6,8},{8,2},{10,4},{12,6},{14,0},{1,11},{3,13... | collective-permute-start | bytes 393224 | tf_op jit(solution)/shard_map/ppermute | solution.py:262
  151.9 11.2 %collective-permute-start.45 = (f32[256,128]{1,0:T(8,128)S(1)}, f32[256,128]{1,0:T(8,128)S(1)}, u32[]{:S(2)}, u32[]{:S(2)}) collective-permute-start(f32[256,128]{1,0:T(8,128)S(1)} %get-tuple-element.81), channel_id=1, source_target_pairs={{0,4},{2,6},{4,0},{6,2},{8,12},{10,14},{12,8},{14,10},{1,5},{3,7},... | collective-permute-start | bytes 393224 | tf_op jit(solution)/shard_map/ppermute | solution.py:262
  (23 other events, 245.3 us)

commit v4 on v3

v4 whole, which is shorter than its diff:
```python
import functools

import jax
import jax.numpy as jnp
from jax import lax
from jax.experimental import pallas as pl
from jax.experimental.pallas import tpu as pltpu
from jax.sharding import Mesh
from jax.sharding import PartitionSpec as P

EDGE = 128
BLOCK = 32
ROW_AXES = ("y", "xh")
COL_AXES = ("xl", "z", "core")
PLANE_AXES = ("xl", "z")
VMEM_LIMIT = 40 << 20


def split(value):
    high = value.astype(jnp.bfloat16)
    low = (value - high.astype(jnp.float32)).astype(jnp.bfloat16)
    return high, low


def dot3(left, right, dims=((1,), (0,))):
    dot = functools.partial(
        lax.dot_general, dimension_numbers=(dims, ((), ())), preferred_element_type=jnp.float32
    )
    left_high, left_low = split(left)
    right_high, right_low = split(right)
    return dot(left_high, right_high) + (dot(left_high, right_low) + dot(left_low, right_high))


def spread_body(flipped, n_src, n_out, take, put, count, tiles, *refs):
    sources, outs = refs[:n_src], refs[-4 - n_out : -4]
    paired, total, held, arrived = refs[-4:]
    slots = held.shape[0]

    def fetch(index):
        here = pl.ds(index * BLOCK, BLOCK)
        return pltpu.make_async_copy(tiles.at[here], held.at[here], arrived.at[index])

    for index in range(slots // BLOCK):

        @pl.when(index * BLOCK < count[0])
        def _(index=index):
            fetch(index).start()

    total[...] = jnp.zeros_like(total)
    first = 0
    for source in sources:
        rows = source.shape[0] // EDGE

        def pair(index, carry, source=source, first=first):
            high, low = split(source[pl.ds(pl.multiple_of(index * EDGE, EDGE), EDGE), :])
            paired[first + index, :EDGE, :EDGE] = high
            paired[first + index, :EDGE, EDGE:] = low
            paired[first + index, EDGE:, :EDGE] = high
            paired[first + index, EDGE:, EDGE:] = jnp.zeros_like(low)
            return carry

        lax.fori_loop(0, rows, pair, 0)
        first += rows

    def block(index, masked):
        for offset in range(BLOCK):
            slot = index * BLOCK + offset
            tile = held[slot]
            if masked:
                tile = jnp.where(slot < count[0], tile, 0.0)
            high, low = split(tile.T if flipped else tile)
            both = jnp.dot(
                jnp.concatenate([high, low], axis=1),
                paired[take[slot]],
                preferred_element_type=jnp.float32,
            )
            total[put[slot]] += both[:, :EDGE] + both[:, EDGE:]

    def whole_block(index, carry):
        fetch(index).wait()
        block(index, False)
        return carry

    blocks = count[0] // BLOCK
    lax.fori_loop(0, blocks, whole_block, 0)

    @pl.when(blocks * BLOCK < count[0])
    def _():
        fetch(blocks).wait()
        block(blocks, True)

    place = 0
    for out in outs:
        for index in range(out.shape[0] // EDGE):
            out[index * EDGE : (index + 1) * EDGE] = total[place + index]
        place += out.shape[0] // EDGE


def spread(tiles, take, put, count, sources, out_rows, flipped, after, name):
    slots = tiles.shape[0]
    src_count = sum(source.shape[0] // EDGE for source in sources)
    scalars, here = pl.BlockSpec(memory_space=pltpu.SMEM), pl.BlockSpec(memory_space=pltpu.VMEM)
    there = pl.BlockSpec(memory_space=pl.ANY)
    return pl.pallas_call(
        functools.partial(spread_body, flipped, len(sources), len(out_rows)),
        in_specs=[scalars] * 3 + [there] + [here] * len(sources) + [there] * len(after),
        out_specs=[here] * len(out_rows),
        scratch_shapes=[
            pltpu.VMEM((src_count, 2 * EDGE, 2 * EDGE), jnp.bfloat16),
            pltpu.VMEM((sum(out_rows) // EDGE, EDGE, EDGE), jnp.float32),
            pltpu.VMEM(tiles.shape, jnp.float32),
            pltpu.SemaphoreType.DMA((slots // BLOCK,)),
        ],
        out_shape=[jax.ShapeDtypeStruct((n, EDGE), jnp.float32) for n in out_rows],
        compiler_params=pltpu.CompilerParams(vmem_limit_bytes=VMEM_LIMIT),
        cost_estimate=pl.CostEstimate(flops=0, bytes_accessed=0, transcendentals=0),
        name=name,
    )(take, put, count, tiles, *sources, *after)


def whole_call(kernel, outs, *args, skipped=0, name):
    here, there = pl.BlockSpec(memory_space=pltpu.VMEM), pl.BlockSpec(memory_space=pl.ANY)
    return pl.pallas_call(
        kernel,
        in_specs=[here] * (len(args) - skipped) + [there] * skipped,
        out_specs=[here] * len(outs),
        out_shape=[jax.ShapeDtypeStruct(shape, jnp.float32) for shape in outs],
        compiler_params=pltpu.CompilerParams(vmem_limit_bytes=VMEM_LIMIT),
        name=name,
    )(*args)


def added(terms):
    return functools.reduce(lambda left, right: left + right, [term[...] for term in terms])


def middle_body(weight, out_grad, own, other, *refs):
    terms, (hidden, grad0, grad1, weight_part) = refs[:-4], refs[-4:]
    mixed = jnp.concatenate([own[...] + other[...], added(terms)], axis=1)
    pre_act = dot3(mixed, weight[...])
    sigma = jax.nn.sigmoid(pre_act)
    hidden[...] = pre_act * sigma
    slope = sigma * (1.0 + pre_act * (1.0 - sigma))
    local = out_grad[...] * slope
    back = dot3(local, weight[...], ((1,), (1,)))
    grad0[...] = back[:, :EDGE]
    grad1[...] = back[:, EDGE:]
    term = dot3(mixed, local, ((0,), (0,)))
    count = weight_part.shape[1] // 2
    for place in range(weight_part.shape[0]):
        for side in range(2):
            weight_part[place, side * count : (side + 1) * count, :] = term[
                place * count : (place + 1) * count, side * EDGE : (side + 1) * EDGE
            ]


def copies_body(value, *refs):
    out = refs[-1]
    rows = value.shape[0]
    for place in range(out.shape[0]):
        out[place, :rows] = value[...]
        if out.shape[1] > rows:
            out[place, rows:] = refs[0][place]


def unpack_body(arrived, rows_out, piece):
    rows = rows_out.shape[0] // arrived.shape[0]
    for place in range(arrived.shape[0]):
        rows_out[place * rows : (place + 1) * rows] = arrived[place, :rows]
    piece[...] = jnp.sum(arrived[:, rows:], axis=0)


def join_body(*refs):
    blocks, out = refs[:-2], refs[-1]
    rows = blocks[0].shape[0]
    for place, block in enumerate(blocks):
        out[place * rows : (place + 1) * rows] = block[...]


def pair_body(mine, other, *refs):
    out = refs[-1]
    rows = mine.shape[0]
    out[:rows] = mine[...]
    out[rows:] = other[...]


def fold_body(n_terms, *refs):
    terms, outs = refs[:n_terms], refs[n_terms + 1 :]
    total = added(terms)
    first = 0
    for out in outs:
        out[...] = total[first : first + out.shape[0]]
        first += out.shape[0]


def add_body(mine, other, *outs):
    rows = mine.shape[0] // len(outs)
    for step, out in enumerate(outs):
        here = pl.ds(step * rows, rows)
        out[...] = mine[here, :] + other[here, :]


def share_body(mine, other, piece, other_piece, out):
    rows = out.shape[1] - piece.shape[0]
    both = piece[...] + other_piece[...]
    for place in range(out.shape[0]):
        here = pl.ds(place * rows, rows)
        out[place, :rows] = mine[here, :] + other[here, :]
        out[place, rows:] = both


def sum_body(terms, grad, piece):
    total = jnp.sum(terms[...], axis=0)
    rows = grad.shape[0]
    grad[...] = total[:rows]
    piece[...] = total[rows:]


def finish_body(grad0, *refs):
    terms, out = refs[:-1], refs[-1]
    out[:, :EDGE] = grad0[...]
    out[:, EDGE:] = added(terms)


def assemble_body(scale, pieces, out):
    count = pieces.shape[1] // 2
    for place in range(pieces.shape[0]):
        for side in range(2):
            out[place * count : (place + 1) * count, side * EDGE : (side + 1) * EDGE] = (
                pieces[place, side * count : (side + 1) * count, :] * scale
            )


def swap(value, axis):
    return lax.ppermute(value, axis, [(0, 1), (1, 0)])


def ring_send(value, axis, step):
    size = lax.axis_size(axis)
    return lax.ppermute(value, axis, [(place, (place + step) % size) for place in range(size)])


def offset_send(value, axes, ring, offset):
    sizes = [lax.axis_size(axis) for axis in axes]
    hops = []
    for a in range(sizes[0]):
        for b in range(sizes[1]):
            if axes[0] == ring:
                to = (a + offset // 2) % sizes[0], b ^ (offset % 2)
            else:
                to = a ^ (offset % 2), (b + offset // 2) % sizes[1]
            hops.append((a * sizes[1] + b, to[0] * sizes[1] + to[1]))
    return lax.ppermute(value, axes, hops)


def exchange(value, axes):
    return lax.all_to_all(value, axes, 0, 0, tiled=True)


def offset_of(ring_index, pair_index, ring, pair, sign):
    step = (sign * (lax.axis_index(ring) - ring_index)) % lax.axis_size(ring)
    return step * 2 + (pair_index ^ lax.axis_index(pair))


def body(features, weight, tile_vals, tile_index, tile_count, out_grad):
    tiles = tile_vals[0, 0]
    dest = tile_index[0, 0, 0]
    src = tile_index[0, 0, 1]
    count = tile_count[0]
    n_row = lax.axis_size(ROW_AXES)
    n_col = lax.axis_size(COL_AXES)
    n_plane = lax.axis_size(PLANE_AXES)
    n_z = lax.axis_size("z")
    n_y = lax.axis_size("y")
    rows, width = features.shape
    per = rows // EDGE
    half_tiles = n_plane * per
    src_home, src_tile = src // per, src % per
    src_half = ((src_home % 2) ^ lax.axis_index("core")) * half_tiles + src_tile
    dest_home, dest_tile = dest // per, dest % per

    plane = src_home // 2

    def src_place(sign):
        return src_half + per * offset_of(plane % n_z, plane // n_z, "z", "xl", sign)

    def dest_place(sign):
        return dest_tile + per * offset_of(dest_home // 2, dest_home % 2, "y", "xh", sign)

    live = jnp.arange(tiles.shape[0], dtype=jnp.int32) < count[0]
    src_take, dest_put, dest_take0, dest_take1, src_put0, src_put1 = [
        jnp.where(live, index, 0).astype(jnp.int32)
        for index in (
            src_place(1),
            dest_place(-1),
            dest_place(1),
            dest,
            src_half + per * plane,
            src_place(-1),
        )
    ]

    half = (rows, EDGE)
    full = (rows, width)
    gathered = []
    for chunk in range(2):
        part = features[:, chunk * EDGE : (chunk + 1) * EDGE]
        after = gathered[0][1:] if chunk else []
        (both,) = whole_call(
            pair_body,
            [(2 * rows, EDGE)],
            part,
            swap(part, "xl"),
            *after,
            skipped=len(after),
            name=f"pair{chunk}",
        )
        gathered.append([both] + [ring_send(both, "z", step) for step in range(1, n_z)])
    partial0 = spread(
        tiles,
        src_take,
        dest_put,
        count,
        gathered[0] + [swap(block, "core") for block in gathered[0]],
        [2 * rows] * n_y,
        False,
        [],
        "forward0",
    )
    (joined,) = whole_call(
        join_body, [(half_tiles * EDGE, EDGE)], *gathered[1], partial0[0], skipped=1, name="join"
    )
    partial1 = spread(
        tiles,
        src_take,
        dest_put,
        count,
        [joined, swap(joined, "core")],
        [rows] * n_row,
        False,
        [],
        "forward1",
    )
    arrived = [offset_send(partial1[offset], ROW_AXES, "y", offset) for offset in range(1, n_row)]
    arrived0 = [ring_send(partial0[step], "y", step) for step in range(1, n_y)]
    own, other = whole_call(
        functools.partial(fold_body, n_y),
        [half, half],
        partial0[0],
        *arrived0,
        arrived[0],
        skipped=1,
        name="fold0",
    )
    piece_rows = 2 * width // n_row
    hidden, grad0, grad1, weight_part = whole_call(
        middle_body,
        [full, half, half, (n_row, piece_rows, EDGE)],
        weight,
        out_grad,
        own,
        swap(other, "xh"),
        partial1[0],
        *arrived,
        name="middle",
    )

    (both,) = whole_call(pair_body, [(2 * rows, EDGE)], grad0, swap(grad0, "xh"), name="pair2")
    sources0 = [both] + [ring_send(both, "y", step) for step in range(1, n_y)]
    (copied,) = whole_call(
        copies_body, [(n_row, rows + piece_rows, EDGE)], grad1, weight_part, both, skipped=1, name="copies"
    )
    arrived = exchange(copied, ROW_AXES)
    sources1, piece = whole_call(
        unpack_body, [(n_row * rows, EDGE), (piece_rows, EDGE)], arrived, name="unpack"
    )
    mine, other = spread(
        tiles,
        dest_take0,
        src_put0,
        count,
        sources0,
        [half_tiles * EDGE] * 2,
        True,
        [copied],
        "backward0",
    )
    (share,) = whole_call(
        share_body,
        [(n_plane, rows + piece_rows, EDGE)],
        mine,
        swap(other, "core"),
        piece,
        swap(piece, "core"),
        name="share0",
    )
    terms = exchange(share, PLANE_AXES)
    mine, other = spread(
        tiles,
        dest_take1,
        src_put1,
        count,
        [sources1],
        [half_tiles * EDGE] * 2,
        True,
        [share],
        "backward1",
    )
    shares = whole_call(add_body, [half] * n_plane, mine, swap(other, "core"), name="share1")
    arrived = [offset_send(shares[offset], PLANE_AXES, "z", offset) for offset in range(1, n_plane)]
    grad_x0, piece = whole_call(sum_body, [half, (piece_rows, EDGE)], terms, name="sum0")
    (grad_x,) = whole_call(finish_body, [full], grad_x0, shares[0], *arrived, name="finish")

    pieces = exchange(jnp.broadcast_to(piece[None], (n_row, piece_rows, EDGE)), ROW_AXES)
    scale = (rows * n_row * n_col) ** (-0.5)
    (grad_w,) = whole_call(functools.partial(assemble_body, scale), [full], pieces, name="assemble")
    return hidden, grad_x, grad_w


def solution(mesh):
    chips = Mesh(mesh.devices.reshape(4, 2, 2, 4, 2), ROW_AXES + COL_AXES)
    placed = (
        P(ROW_AXES + COL_AXES, None),
        P(),
        P(COL_AXES, ROW_AXES, None, None, None),
        P(COL_AXES, ROW_AXES, None, None),
        P(COL_AXES, ROW_AXES),
        P(COL_AXES + ROW_AXES, None),
    )
    return jax.shard_map(
        body,
        mesh=chips,
        in_specs=placed,
        out_specs=(P(COL_AXES + ROW_AXES, None), P(ROW_AXES + COL_AXES, None), P()),
        check_vma=False,
    )
```

time: 169 us -> 165 us (0.976)
  starting transfers between devices: 82.6 us -> 76.4 us
  Pallas kernels: 18.9 us -> 23 us
  waiting for transfers between devices: 63.2 us -> 60.4 us
    all_to_all x0 -> x3, starting transfers between devices: none -> 20.5 us  [exchange(): return lax.all_to_all(value, axes, 0, 0, tiled=True)]
    ppermute x21 -> x12, waiting for transfers between devices: 42.3 us -> 24.4 us  [ring_send(): lax.ppermute(value, axis, [(place, (place + step) % size) for place in ra...]
    ppermute x21 -> x12, starting transfers between devices: 39.3 us -> 22.8 us  [ring_send(): lax.ppermute(value, axis, [(place, (place + step) % size) for place in ra...]
    all_to_all x0 -> x3, waiting for transfers between devices: none -> 10.7 us  [exchange(): return lax.all_to_all(value, axes, 0, 0, tiled=True)]
    ppermute x14, waiting for transfers between devices: 4.17 us -> 12.1 us  [offset_send(): return lax.ppermute(value, axes, hops)]
    ppermute x14, starting transfers between devices: 30.7 us -> 24.9 us  [offset_send(): return lax.ppermute(value, axes, hops)]
    ppermute x18 -> x12, starting transfers between devices: 12.5 us -> 8.19 us  [swap(): return lax.ppermute(value, axis, [(0, 1), (1, 0)])]
    ppermute x18 -> x12, waiting for transfers between devices: 16.7 us -> 13.2 us  [swap(): return lax.ppermute(value, axis, [(0, 1), (1, 0)])]
  transfers between devices with their start and end apart: 53 -> 41, of which waited for: 21 -> 22; matrix products, arithmetic and copies ran while one was open for 1% -> 1% of each run, Pallas kernels for 10% -> 11%
where the time goes in v4:
time: 165 us; the launch traced here: 164 us
  starting transfers between devices  76.4 us (46%)
  waiting for transfers between devices  60.4 us (37%)
  Pallas kernels  23 us (14%)
  local copies, waits for them, and re-layouts  2.48 us (2%)
    ppermute x14, starting transfers between devices, offset_send(): return lax.ppermute(value, axes, hops)  24.9 us
    ppermute x12, waiting for transfers between devices, ring_send(): lax.ppermute(value, axis, [(place, (place + step) % size) for place in ra...  24.4 us
    ppermute x12, starting transfers between devices, ring_send(): lax.ppermute(value, axis, [(place, (place + step) % size) for place in ra...  22.8 us
    all_to_all x3, starting transfers between devices, exchange(): return lax.all_to_all(value, axes, 0, 0, tiled=True)  20.5 us
    pallas_call x4, Pallas kernels, spread(): pl.pallas_call(functools.partial(spread_body, flipped, len(sources), len(...  16.4 us
    ppermute x12, waiting for transfers between devices, swap(): return lax.ppermute(value, axis, [(0, 1), (1, 0)])  13.2 us
    ppermute x14, waiting for transfers between devices, offset_send(): return lax.ppermute(value, axes, hops)  12.1 us
    all_to_all x3, waiting for transfers between devices, exchange(): return lax.all_to_all(value, axes, 0, 0, tiled=True)  10.7 us
  transfers between devices with their start and end apart: 41, of which 22 were waited for; matrix products, arithmetic and copies ran while one was open for 1% of the time, Pallas kernels for 11%

profile of v4, /device:TPU:0, one launch (start us, length us, event | category | flops | bytes accessed | tf_op | source)
XLA Modules:
  0.0 163.8 jit_solution(11478393236555695158)
XLA Ops:
  3.3 3.5 %collective-permute-done.other = f32[256,128]{1,0:T(8,128)S(1)} collective-permute-done((f32[256,128]{1,0:T(8,128)S(1)}, f32[256,128]{1,0:T(8,128)S(1)}, u32[]{:S(2)}, u32[]{:S(2)}) %collective-permute-start) | collective-permute-done | bytes 131104 | tf_op jit(solution)/shard_map/ppermute | solution.py:235
  10.5 3.6 %collective-permute-start.2 = (f32[512,128]{1,0:T(8,128)S(1)}, f32[512,128]{1,0:T(8,128)S(1)}, u32[]{:S(2)}, u32[]{:S(2)}) collective-permute-start(f32[512,128]{1,0:T(8,128)S(1)} %pair0.1.refs_0_), channel_id=1, source_target_pairs={{0,4},{2,6},{4,0},{6,2},{1,5},{3,7},{5,1},{7,3},{8,12},{10,14},{12... | collective-permute-start | bytes 786440 | tf_op jit(solution)/shard_map/ppermute | solution.py:240
  15.1 2.4 %collective-permute-done.1.refs_1_.refs_0_ = f32[512,128]{1,0:T(8,128)S(1)} collective-permute-done((f32[512,128]{1,0:T(8,128)S(1)}, f32[512,128]{1,0:T(8,128)S(1)}, u32[]{:S(2)}, u32[]{:S(2)}) %collective-permute-start.1) | collective-permute-done | bytes 262176 | tf_op jit(solution)/shard_map/ppermute | solution.py:240
  19.0 4.4 %collective-permute-done.2.refs_2_.refs_1_ = f32[512,128]{1,0:T(8,128)S(1)} collective-permute-done((f32[512,128]{1,0:T(8,128)S(1)}, f32[512,128]{1,0:T(8,128)S(1)}, u32[]{:S(2)}, u32[]{:S(2)}) %collective-permute-start.2) | collective-permute-done | bytes 262176 | tf_op jit(solution)/shard_map/ppermute | solution.py:240
  25.9 2.4 %collective-permute-start.13 = (f32[512,128]{1,0:T(8,128)S(1)}, f32[512,128]{1,0:T(8,128)S(1)}, u32[]{:S(2)}, u32[]{:S(2)}) collective-permute-start(f32[512,128]{1,0:T(8,128)S(1)} %pair1.1.refs_0_), channel_id=1, source_target_pairs={{0,4},{2,6},{4,0},{6,2},{1,5},{3,7},{5,1},{7,3},{8,12},{10,14},{12... | collective-permute-start | bytes 786440 | tf_op jit(solution)/shard_map/ppermute | solution.py:240
  31.5 3.8 %forward0.1 = (f32[512,128]{1,0:T(8,128)S(1)}, f32[512,128]{1,0:T(8,128)S(1)}, f32[512,128]{1,0:T(8,128)S(1)}, f32[512,128]{1,0:T(8,128)S(1)}) custom-call(s32[256]{0:T(256)S(1)} %get-tuple-element.81.take, s32[256]{0:T(256)S(1)} %add_select_fusion.3.put, s32[1]{0:T(128)} %bitcast.8.count, f32[256,128,128]{2,1,0:T(8,128)} %bitcast.12, ...), custom_call_target="tpu_custom_call" | custom-call | tf_op jit(solution)/shard_map/forward0/pallas_call | solution.py:104
  35.2 4.3 %collective-permute-done.13.refs_2_ = f32[512,128]{1,0:T(8,128)S(1)} collective-permute-done((f32[512,128]{1,0:T(8,128)S(1)}, f32[512,128]{1,0:T(8,128)S(1)}, u32[]{:S(2)}, u32[]{:S(2)}) %collective-permute-start.13) | collective-permute-done | bytes 262176 | tf_op jit(solution)/shard_map/ppermute | solution.py:240
  41.4 2.9 %collective-permute-start.9 = (f32[512,128]{1,0:T(8,128)S(1)}, f32[512,128]{1,0:T(8,128)S(1)}, u32[]{:S(2)}, u32[]{:S(2)}) collective-permute-start(f32[512,128]{1,0:T(8,128)S(1)} %get-tuple-element.39), channel_id=1, source_target_pairs={{0,64},{32,96},{64,0},{96,32},{1,65},{33,97},{65,1},{97,33},{2,66}... | collective-permute-start | bytes 786440 | tf_op jit(solution)/shard_map/ppermute | solution.py:240
  45.7 3.8 %forward1.1 = (f32[256,128]{1,0:T(8,128)S(1)}, f32[256,128]{1,0:T(8,128)S(1)}, f32[256,128]{1,0:T(8,128)S(1)}, f32[256,128]{1,0:T(8,128)S(1)}, f32[256,128]{1,0:...) custom-call(s32[256]{0:T(256)S(1)} %get-tuple-element.81.take, ...), custom_call_target="tpu_custom_call" | custom-call | tf_op jit(solution)/shard_map/forward1/pallas_call | solution.py:104
  49.5 2.8 %collective-permute-start.16 = (f32[256,128]{1,0:T(8,128)S(1)}, f32[256,128]{1,0:T(8,128)S(1)}, u32[]{:S(2)}, u32[]{:S(2)}) collective-permute-start(f32[256,128]{1,0:T(8,128)S(1)} %get-tuple-element.41), channel_id=1, source_target_pairs={{0,16},{16,0},{32,48},{48,32},{64,80},{80,64},{96,112},{112,96},{1... | collective-permute-start | bytes 393224 | tf_op jit(solution)/shard_map/ppermute | solution.py:253
  53.2 3.8 %collective-permute-done.9.refs_2_ = f32[512,128]{1,0:T(8,128)S(1)} collective-permute-done((f32[512,128]{1,0:T(8,128)S(1)}, f32[512,128]{1,0:T(8,128)S(1)}, u32[]{:S(2)}, u32[]{:S(2)}) %collective-permute-start.9) | collective-permute-done | bytes 262176 | tf_op jit(solution)/shard_map/ppermute | solution.py:240
  57.7 5.3 %collective-permute-start.21 = (f32[256,128]{1,0:T(8,128)S(1)}, f32[256,128]{1,0:T(8,128)S(1)}, u32[]{:S(2)}, u32[]{:S(2)}) collective-permute-start(f32[256,128]{1,0:T(8,128)S(1)} %get-tuple-element.48), channel_id=1, source_target_pairs={{0,80},{16,64},{32,112},{48,96},{64,16},{80,0},{96,48},{112,32},{1... | collective-permute-start | bytes 393224 | tf_op jit(solution)/shard_map/ppermute | solution.py:253
  63.1 2.3 %collective-permute-start.23 = (f32[256,128]{1,0:T(8,128)S(1)}, f32[256,128]{1,0:T(8,128)S(1)}, u32[]{:S(2)}, u32[]{:S(2)}) collective-permute-start(f32[256,128]{1,0:T(8,128)S(1)} %get-tuple-element.50), channel_id=1, source_target_pairs={{0,112},{16,96},{32,16},{48,0},{64,48},{80,32},{96,80},{112,64},{1... | collective-permute-start | bytes 393224 | tf_op jit(solution)/shard_map/ppermute | solution.py:253
  67.8 4.4 %collective-permute-done.22.refs_6_ = f32[256,128]{1,0:T(8,128)S(1)} collective-permute-done((f32[256,128]{1,0:T(8,128)S(1)}, f32[256,128]{1,0:T(8,128)S(1)}, u32[]{:S(2)}, u32[]{:S(2)}) %collective-permute-start.22) | collective-permute-done | bytes 131104 | tf_op jit(solution)/shard_map/ppermute | solution.py:253
  73.7 2.4 %collective-permute-start.24 = (f32[256,128]{1,0:T(8,128)S(1)}, f32[256,128]{1,0:T(8,128)S(1)}, u32[]{:S(2)}, u32[]{:S(2)}) collective-permute-start(f32[256,128]{1,0:T(8,128)S(1)} %get-tuple-element.52.mine), channel_id=1, source_target_pairs={{0,16},{16,0},{1,17},{17,1},{2,18},{18,2},{3,19},{19,3},{4,20},{20... | collective-permute-start | bytes 393224 | tf_op jit(solution)/shard_map/ppermute | solution.py:235
  76.1 4.0 %collective-permute-done.24.other = f32[256,128]{1,0:T(8,128)S(1)} collective-permute-done((f32[256,128]{1,0:T(8,128)S(1)}, f32[256,128]{1,0:T(8,128)S(1)}, u32[]{:S(2)}, u32[]{:S(2)}) %collective-permute-start.24) | collective-permute-done | bytes 131104 | tf_op jit(solution)/shard_map/ppermute | solution.py:235
  86.0 4.8 %all-to-all-start = ((f32[8,320,128]{2,1,0:T(8,128)}), f32[8,320,128]{2,1,0:T(8,128)S(1)}, u32[]{:S(2)}, u32[]{:S(2)}) async-start(f32[8,320,128]{2,1,0:T(8,128)} %copies.1.refs_4_), calls=%async_computation | async-start | bytes 2621440 | tf_op jit(solution)/shard_map/all_to_all | solution.py:257
  92.8 3.1 %collective-permute-done.26.refs_2_ = f32[512,128]{1,0:T(8,128)S(1)} collective-permute-done((f32[512,128]{1,0:T(8,128)S(1)}, f32[512,128]{1,0:T(8,128)S(1)}, u32[]{:S(2)}, u32[]{:S(2)}) %collective-permute-start.26) | collective-permute-done | bytes 262176 | tf_op jit(solution)/shard_map/ppermute | solution.py:240
  95.9 3.6 %collective-permute-done.27.refs_3_ = f32[512,128]{1,0:T(8,128)S(1)} collective-permute-done((f32[512,128]{1,0:T(8,128)S(1)}, f32[512,128]{1,0:T(8,128)S(1)}, u32[]{:S(2)}, u32[]{:S(2)}) %collective-permute-start.27) | collective-permute-done | bytes 262176 | tf_op jit(solution)/shard_map/ppermute | solution.py:240
  99.5 4.9 %backward0.1 = (f32[2048,128]{1,0:T(8,128)S(1)}, f32[2048,128]{1,0:T(8,128)}) custom-call(s32[256]{0:T(256)S(1)} %get-tuple-element.86.take, s32[256]{0:T(256)S(1)} %get-tuple-element.80.put, s32[1]{0:T(128)} %bitcast.10.count, f32[256,128,128]{2,1,0:T(8,128)} %bitcast.14, f32[512,128]{1,0:T(8,128)S(1)} %pair2.1.refs_1_.refs_0_, ...), custom_call_target="tpu_custom_call" | custom-call | tf_op jit(solution)/shard_map/backward0/pallas_call | solution.py:104
  104.5 3.6 %all-to-all-done.arrived = f32[8,320,128]{2,1,0:T(8,128)S(1)} async-done(((f32[8,320,128]{2,1,0:T(8,128)}), f32[8,320,128]{2,1,0:T(8,128)S(1)}, u32[]{:S(2)}, u32[]{:S(2)}) %all-to-all-start) | async-done | bytes 1310752 | tf_op jit(solution)/shard_map/all_to_all | solution.py:257
  109.4 2.4 %share0.1.refs_1_ = f32[8,320,128]{2,1,0:T(8,128)} custom-call(f32[2048,128]{1,0:T(8,128)S(1)} %get-tuple-element.55.mine, f32[2048,128]{1,0:T(8,128)} %collective-permute-done.28.other, f32[64,128]{1,0:T(8,128)S(1)} %get-tuple-element.57.piece, f32[64,128]{1,0:T(8,128)S(1)} %collective-permute-done.29.other_piece), custom_call_target="tpu_custom_call" | custom-call | tf_op jit(solution)/shard_map/share0/pallas_call | solution.py:123
  111.9 6.5 %all-to-all-start.1 = ((f32[8,320,128]{2,1,0:T(8,128)}), f32[8,320,128]{2,1,0:T(8,128)S(1)}, u32[]{:S(2)}, u32[]{:S(2)}) async-start(f32[8,320,128]{2,1,0:T(8,128)} %share0.1.refs_1_), calls=%async_computation.1 | async-start | bytes 2621440 | tf_op jit(solution)/shard_map/all_to_all | solution.py:257
  118.3 4.0 %backward1.1 = (f32[2048,128]{1,0:T(8,128)S(1)}, f32[2048,128]{1,0:T(8,128)S(1)}) custom-call(s32[256]{0:T(256)S(1)} %get-tuple-element.85.take, s32[256]{0:T(256)S(1)} %get-tuple-element.71.put, s32[1]{0:T(128)} %bitcast.11.count, f32[256,128,128]{2,1,0:T(8,128)} %bitcast.15, f32[2048,128]{1,0:T(8,128)S(1)} %get-tuple-element.59.refs_0_, ...), custom_call_target="tpu_custom_call" | custom-call | tf_op jit(solution)/shard_map/backward1/pallas_call | solution.py:104
  122.4 2.6 %collective-permute-done.30.other = f32[2048,128]{1,0:T(8,128)S(1)} collective-permute-done((f32[2048,128]{1,0:T(8,128)S(1)}, f32[2048,128]{1,0:T(8,128)S(1)}, u32[]{:S(2)}, u32[]{:S(2)}) %collective-permute-start.30) | collective-permute-done | bytes 1048608 | tf_op jit(solution)/shard_map/ppermute | solution.py:235
  125.2 3.1 %collective-permute-start.31 = (f32[256,128]{1,0:T(8,128)S(1)}, f32[256,128]{1,0:T(8,128)S(1)}, u32[]{:S(2)}, u32[]{:S(2)}) collective-permute-start(f32[256,128]{1,0:T(8,128)S(1)} %get-tuple-element.63), channel_id=1, source_target_pairs={{0,8},{2,10},{4,12},{6,14},{8,0},{10,2},{12,4},{14,6},{1,9},{3,11}... | collective-permute-start | bytes 393224 | tf_op jit(solution)/shard_map/ppermute | solution.py:253
  129.5 7.1 %all-to-all-done.1.terms = f32[8,320,128]{2,1,0:T(8,128)S(1)} async-done(((f32[8,320,128]{2,1,0:T(8,128)}), f32[8,320,128]{2,1,0:T(8,128)S(1)}, u32[]{:S(2)}, u32[]{:S(2)}) %all-to-all-start.1) | async-done | bytes 1310752 | tf_op jit(solution)/shard_map/all_to_all | solution.py:257
  137.4 9.3 %all-to-all-start.2 = ((f32[8,64,128]{2,1,0:T(8,128)}), f32[8,64,128]{2,1,0:T(8,128)S(1)}, u32[]{:S(2)}, u32[]{:S(2)}) async-start(f32[8,64,128]{2,1,0:T(8,128)} %broadcast_in_dim.13), calls=%async_computation.2 | async-start | bytes 524288 | tf_op jit(solution)/shard_map/all_to_all | solution.py:257
  147.5 2.7 %collective-permute-start.34 = (f32[256,128]{1,0:T(8,128)S(1)}, f32[256,128]{1,0:T(8,128)S(1)}, u32[]{:S(2)}, u32[]{:S(2)}) collective-permute-start(f32[256,128]{1,0:T(8,128)S(1)} %get-tuple-element.66), channel_id=1, source_target_pairs={{0,4},{2,6},{4,0},{6,2},{8,12},{10,14},{12,8},{14,10},{1,5},{3,7},... | collective-permute-start | bytes 393224 | tf_op jit(solution)/shard_map/ppermute | solution.py:253
  150.2 2.8 %collective-permute-start.35 = (f32[256,128]{1,0:T(8,128)S(1)}, f32[256,128]{1,0:T(8,128)S(1)}, u32[]{:S(2)}, u32[]{:S(2)}) collective-permute-start(f32[256,128]{1,0:T(8,128)S(1)} %get-tuple-element.67), channel_id=1, source_target_pairs={{0,12},{2,14},{4,8},{6,10},{8,4},{10,6},{12,0},{14,2},{1,13},{3,15... | collective-permute-start | bytes 393224 | tf_op jit(solution)/shard_map/ppermute | solution.py:253
  156.2 3.1 %collective-permute-done.34.refs_4_ = f32[256,128]{1,0:T(8,128)S(1)} collective-permute-done((f32[256,128]{1,0:T(8,128)S(1)}, f32[256,128]{1,0:T(8,128)S(1)}, u32[]{:S(2)}, u32[]{:S(2)}) %collective-permute-start.34) | collective-permute-done | bytes 131104 | tf_op jit(solution)/shard_map/ppermute | solution.py:253
  159.2 3.0 %collective-permute-done.36.refs_6_ = f32[256,128]{1,0:T(8,128)S(1)} collective-permute-done((f32[256,128]{1,0:T(8,128)S(1)}, f32[256,128]{1,0:T(8,128)S(1)}, u32[]{:S(2)}, u32[]{:S(2)}) %collective-permute-start.36) | collective-permute-done | bytes 131104 | tf_op jit(solution)/shard_map/ppermute | solution.py:253
  (77 shorter events, 39.7 us)
Async XLA Ops:
  6.8 10.7 %collective-permute-start.1 = (f32[512,128]{1,0:T(8,128)S(1)}, f32[512,128]{1,0:T(8,128)S(1)}, u32[]{:S(2)}, u32[]{:S(2)}) collective-permute-start(f32[512,128]{1,0:T(8,128)S(1)} %pair0.1.refs_0_), channel_id=1, source_target_pairs={{0,2},{2,4},{4,6},{6,0},{1,3},{3,5},{5,7},{7,1},{8,10},{10,12},{12... | collective-permute-start | bytes 786440 | tf_op jit(solution)/shard_map/ppermute | solution.py:240
  9.0 9.9 %collective-permute-start.11 = (f32[256,128]{1,0:T(8,128)S(1)}, f32[256,128]{1,0:T(8,128)S(1)}, u32[]{:S(2)}, u32[]{:S(2)}) collective-permute-start(f32[256,128]{1,0:T(8,128)S(1)} %get-tuple-element.78.mine), channel_id=1, source_target_pairs={{0,8},{8,0},{1,9},{9,1},{2,10},{10,2},{3,11},{11,3},{4,12},{12,4},... | collective-permute-start | bytes 393224 | tf_op jit(solution)/shard_map/ppermute | solution.py:235
  10.5 12.9 %collective-permute-start.2 = (f32[512,128]{1,0:T(8,128)S(1)}, f32[512,128]{1,0:T(8,128)S(1)}, u32[]{:S(2)}, u32[]{:S(2)}) collective-permute-start(f32[512,128]{1,0:T(8,128)S(1)} %pair0.1.refs_0_), channel_id=1, source_target_pairs={{0,4},{2,6},{4,0},{6,2},{1,5},{3,7},{5,1},{7,3},{8,12},{10,14},{12... | collective-permute-start | bytes 786440 | tf_op jit(solution)/shard_map/ppermute | solution.py:240
  14.1 10.0 %collective-permute-start.3 = (f32[512,128]{1,0:T(8,128)S(1)}, f32[512,128]{1,0:T(8,128)S(1)}, u32[]{:S(2)}, u32[]{:S(2)}) collective-permute-start(f32[512,128]{1,0:T(8,128)S(1)} %pair0.1.refs_0_), channel_id=1, source_target_pairs={{0,6},{2,0},{4,2},{6,4},{1,7},{3,1},{5,3},{7,5},{8,14},{10,8},{12,... | collective-permute-start | bytes 786440 | tf_op jit(solution)/shard_map/ppermute | solution.py:240
  15.1 14.4 %collective-permute-start.4 = (f32[512,128]{1,0:T(8,128)S(1)}, f32[512,128]{1,0:T(8,128)S(1)}, u32[]{:S(2)}, u32[]{:S(2)}) collective-permute-start(f32[512,128]{1,0:T(8,128)S(1)} %pair0.1.refs_0_), channel_id=1, source_target_pairs={{0,1},{1,0},{2,3},{3,2},{4,5},{5,4},{6,7},{7,6},{8,9},{9,8},{10,11... | collective-permute-start | bytes 786440 | tf_op jit(solution)/shard_map/ppermute | solution.py:235
  17.5 12.1 %collective-permute-start.5 = (f32[512,128]{1,0:T(8,128)S(1)}, f32[512,128]{1,0:T(8,128)S(1)}, u32[]{:S(2)}, u32[]{:S(2)}) collective-permute-start(f32[512,128]{1,0:T(8,128)S(1)} %collective-permute-done.1.refs_1_.refs_0_), channel_id=1, source_target_pairs={{0,1},{1,0},{2,3},{3,2},{4,5},{5,4},{6,7},{7,6},{8,9},{9,8},{10,11... | collective-permute-start | bytes 786440 | tf_op jit(solution)/shard_map/ppermute | solution.py:235
  24.1 11.1 %collective-permute-start.12 = (f32[512,128]{1,0:T(8,128)S(1)}, f32[512,128]{1,0:T(8,128)S(1)}, u32[]{:S(2)}, u32[]{:S(2)}) collective-permute-start(f32[512,128]{1,0:T(8,128)S(1)} %pair1.1.refs_0_), channel_id=1, source_target_pairs={{0,2},{2,4},{4,6},{6,0},{1,3},{3,5},{5,7},{7,1},{8,10},{10,12},{12... | collective-permute-start | bytes 786440 | tf_op jit(solution)/shard_map/ppermute | solution.py:240
  25.9 13.7 %collective-permute-start.13 = (f32[512,128]{1,0:T(8,128)S(1)}, f32[512,128]{1,0:T(8,128)S(1)}, u32[]{:S(2)}, u32[]{:S(2)}) collective-permute-start(f32[512,128]{1,0:T(8,128)S(1)} %pair1.1.refs_0_), channel_id=1, source_target_pairs={{0,4},{2,6},{4,0},{6,2},{1,5},{3,7},{5,1},{7,3},{8,12},{10,14},{12... | collective-permute-start | bytes 786440 | tf_op jit(solution)/shard_map/ppermute | solution.py:240
  28.3 11.3 %collective-permute-start.14 = (f32[512,128]{1,0:T(8,128)S(1)}, f32[512,128]{1,0:T(8,128)S(1)}, u32[]{:S(2)}, u32[]{:S(2)}) collective-permute-start(f32[512,128]{1,0:T(8,128)S(1)} %pair1.1.refs_0_), channel_id=1, source_target_pairs={{0,6},{2,0},{4,2},{6,4},{1,7},{3,1},{5,3},{7,5},{8,14},{10,8},{12,... | collective-permute-start | bytes 786440 | tf_op jit(solution)/shard_map/ppermute | solution.py:240
  39.8 13.2 %collective-permute-start.8 = (f32[512,128]{1,0:T(8,128)S(1)}, f32[512,128]{1,0:T(8,128)S(1)}, u32[]{:S(2)}, u32[]{:S(2)}) collective-permute-start(f32[512,128]{1,0:T(8,128)S(1)} %get-tuple-element.38), channel_id=1, source_target_pairs={{0,32},{32,64},{64,96},{96,0},{1,33},{33,65},{65,97},{97,1},{2,34}... | collective-permute-start | bytes 786440 | tf_op jit(solution)/shard_map/ppermute | solution.py:240
  41.4 15.6 %collective-permute-start.9 = (f32[512,128]{1,0:T(8,128)S(1)}, f32[512,128]{1,0:T(8,128)S(1)}, u32[]{:S(2)}, u32[]{:S(2)}) collective-permute-start(f32[512,128]{1,0:T(8,128)S(1)} %get-tuple-element.39), channel_id=1, source_target_pairs={{0,64},{32,96},{64,0},{96,32},{1,65},{33,97},{65,1},{97,33},{2,66}... | collective-permute-start | bytes 786440 | tf_op jit(solution)/shard_map/ppermute | solution.py:240
  44.3 13.4 %collective-permute-start.10 = (f32[512,128]{1,0:T(8,128)S(1)}, f32[512,128]{1,0:T(8,128)S(1)}, u32[]{:S(2)}, u32[]{:S(2)}) collective-permute-start(f32[512,128]{1,0:T(8,128)S(1)} %get-tuple-element.40), channel_id=1, source_target_pairs={{0,96},{32,0},{64,32},{96,64},{1,97},{33,1},{65,33},{97,65},{2,98}... | collective-permute-start | bytes 786440 | tf_op jit(solution)/shard_map/ppermute | solution.py:240
  49.5 13.5 %collective-permute-start.16 = (f32[256,128]{1,0:T(8,128)S(1)}, f32[256,128]{1,0:T(8,128)S(1)}, u32[]{:S(2)}, u32[]{:S(2)}) collective-permute-start(f32[256,128]{1,0:T(8,128)S(1)} %get-tuple-element.41), channel_id=1, source_target_pairs={{0,16},{16,0},{32,48},{48,32},{64,80},{80,64},{96,112},{112,96},{1... | collective-permute-start | bytes 393224 | tf_op jit(solution)/shard_map/ppermute | solution.py:253
  52.3 10.8 %collective-permute-start.18 = (f32[256,128]{1,0:T(8,128)S(1)}, f32[256,128]{1,0:T(8,128)S(1)}, u32[]{:S(2)}, u32[]{:S(2)}) collective-permute-start(f32[256,128]{1,0:T(8,128)S(1)} %get-tuple-element.45), channel_id=1, source_target_pairs={{0,32},{16,48},{32,64},{48,80},{64,96},{80,112},{96,0},{112,16},{1... | collective-permute-start | bytes 393224 | tf_op jit(solution)/shard_map/ppermute | solution.py:253
  52.9 12.5 %collective-permute-start.19 = (f32[256,128]{1,0:T(8,128)S(1)}, f32[256,128]{1,0:T(8,128)S(1)}, u32[]{:S(2)}, u32[]{:S(2)}) collective-permute-start(f32[256,128]{1,0:T(8,128)S(1)} %get-tuple-element.46), channel_id=1, source_target_pairs={{0,48},{16,32},{32,80},{48,64},{64,112},{80,96},{96,16},{112,0},{1... | collective-permute-start | bytes 393224 | tf_op jit(solution)/shard_map/ppermute | solution.py:253
  57.0 10.8 %collective-permute-start.20 = (f32[256,128]{1,0:T(8,128)S(1)}, f32[256,128]{1,0:T(8,128)S(1)}, u32[]{:S(2)}, u32[]{:S(2)}) collective-permute-start(f32[256,128]{1,0:T(8,128)S(1)} %get-tuple-element.47), channel_id=1, source_target_pairs={{0,64},{16,80},{32,96},{48,112},{64,0},{80,16},{96,32},{112,48},{1... | collective-permute-start | bytes 393224 | tf_op jit(solution)/shard_map/ppermute | solution.py:253
  57.7 10.1 %collective-permute-start.21 = (f32[256,128]{1,0:T(8,128)S(1)}, f32[256,128]{1,0:T(8,128)S(1)}, u32[]{:S(2)}, u32[]{:S(2)}) collective-permute-start(f32[256,128]{1,0:T(8,128)S(1)} %get-tuple-element.48), channel_id=1, source_target_pairs={{0,80},{16,64},{32,112},{48,96},{64,16},{80,0},{96,48},{112,32},{1... | collective-permute-start | bytes 393224 | tf_op jit(solution)/shard_map/ppermute | solution.py:253
  63.0 9.2 %collective-permute-start.22 = (f32[256,128]{1,0:T(8,128)S(1)}, f32[256,128]{1,0:T(8,128)S(1)}, u32[]{:S(2)}, u32[]{:S(2)}) collective-permute-start(f32[256,128]{1,0:T(8,128)S(1)} %get-tuple-element.49), channel_id=1, source_target_pairs={{0,96},{16,112},{32,0},{48,16},{64,32},{80,48},{96,64},{112,80},{1... | collective-permute-start | bytes 393224 | tf_op jit(solution)/shard_map/ppermute | solution.py:253
  63.1 9.1 %collective-permute-start.23 = (f32[256,128]{1,0:T(8,128)S(1)}, f32[256,128]{1,0:T(8,128)S(1)}, u32[]{:S(2)}, u32[]{:S(2)}) collective-permute-start(f32[256,128]{1,0:T(8,128)S(1)} %get-tuple-element.50), channel_id=1, source_target_pairs={{0,112},{16,96},{32,16},{48,0},{64,48},{80,32},{96,80},{112,64},{1... | collective-permute-start | bytes 393224 | tf_op jit(solution)/shard_map/ppermute | solution.py:253
  80.2 12.6 %collective-permute-start.25 = (f32[512,128]{1,0:T(8,128)S(1)}, f32[512,128]{1,0:T(8,128)S(1)}, u32[]{:S(2)}, u32[]{:S(2)}) collective-permute-start(f32[512,128]{1,0:T(8,128)S(1)} %pair2.1.refs_1_.refs_0_), channel_id=1, source_target_pairs={{0,32},{32,64},{64,96},{96,0},{1,33},{33,65},{65,97},{97,1},{2,34}... | collective-permute-start | bytes 786440 | tf_op jit(solution)/shard_map/ppermute | solution.py:240
  81.8 14.1 %collective-permute-start.26 = (f32[512,128]{1,0:T(8,128)S(1)}, f32[512,128]{1,0:T(8,128)S(1)}, u32[]{:S(2)}, u32[]{:S(2)}) collective-permute-start(f32[512,128]{1,0:T(8,128)S(1)} %pair2.1.refs_1_.refs_0_), channel_id=1, source_target_pairs={{0,64},{32,96},{64,0},{96,32},{1,65},{33,97},{65,1},{97,33},{2,66}... | collective-permute-start | bytes 786440 | tf_op jit(solution)/shard_map/ppermute | solution.py:240
  83.4 16.2 %collective-permute-start.27 = (f32[512,128]{1,0:T(8,128)S(1)}, f32[512,128]{1,0:T(8,128)S(1)}, u32[]{:S(2)}, u32[]{:S(2)}) collective-permute-start(f32[512,128]{1,0:T(8,128)S(1)} %pair2.1.refs_1_.refs_0_), channel_id=1, source_target_pairs={{0,96},{32,0},{64,32},{96,64},{1,97},{33,1},{65,33},{97,65},{2,98}... | collective-permute-start | bytes 786440 | tf_op jit(solution)/shard_map/ppermute | solution.py:240
  86.0 22.1 %all-to-all-start = ((f32[8,320,128]{2,1,0:T(8,128)}), f32[8,320,128]{2,1,0:T(8,128)S(1)}, u32[]{:S(2)}, u32[]{:S(2)}) async-start(f32[8,320,128]{2,1,0:T(8,128)} %copies.1.refs_4_), calls=%async_computation | async-start | bytes 2621440 | tf_op jit(solution)/shard_map/all_to_all | solution.py:257
  111.9 24.8 %all-to-all-start.1 = ((f32[8,320,128]{2,1,0:T(8,128)}), f32[8,320,128]{2,1,0:T(8,128)S(1)}, u32[]{:S(2)}, u32[]{:S(2)}) async-start(f32[8,320,128]{2,1,0:T(8,128)} %share0.1.refs_1_), calls=%async_computation.1 | async-start | bytes 2621440 | tf_op jit(solution)/shard_map/all_to_all | solution.py:257
  125.2 27.9 %collective-permute-start.31 = (f32[256,128]{1,0:T(8,128)S(1)}, f32[256,128]{1,0:T(8,128)S(1)}, u32[]{:S(2)}, u32[]{:S(2)}) collective-permute-start(f32[256,128]{1,0:T(8,128)S(1)} %get-tuple-element.63), channel_id=1, source_target_pairs={{0,8},{2,10},{4,12},{6,14},{8,0},{10,2},{12,4},{14,6},{1,9},{3,11}... | collective-permute-start | bytes 393224 | tf_op jit(solution)/shard_map/ppermute | solution.py:253
  128.3 26.1 %collective-permute-start.32 = (f32[256,128]{1,0:T(8,128)S(1)}, f32[256,128]{1,0:T(8,128)S(1)}, u32[]{:S(2)}, u32[]{:S(2)}) collective-permute-start(f32[256,128]{1,0:T(8,128)S(1)} %get-tuple-element.64), channel_id=1, source_target_pairs={{0,2},{2,4},{4,6},{6,0},{8,10},{10,12},{12,14},{14,8},{1,3},{3,5},... | collective-permute-start | bytes 393224 | tf_op jit(solution)/shard_map/ppermute | solution.py:253
  137.4 25.6 %all-to-all-start.2 = ((f32[8,64,128]{2,1,0:T(8,128)}), f32[8,64,128]{2,1,0:T(8,128)S(1)}, u32[]{:S(2)}, u32[]{:S(2)}) async-start(f32[8,64,128]{2,1,0:T(8,128)} %broadcast_in_dim.13), calls=%async_computation.2 | async-start | bytes 524288 | tf_op jit(solution)/shard_map/all_to_all | solution.py:257
  146.7 9.5 %collective-permute-start.33 = (f32[256,128]{1,0:T(8,128)S(1)}, f32[256,128]{1,0:T(8,128)S(1)}, u32[]{:S(2)}, u32[]{:S(2)}) collective-permute-start(f32[256,128]{1,0:T(8,128)S(1)} %get-tuple-element.65), channel_id=1, source_target_pairs={{0,10},{2,12},{4,14},{6,8},{8,2},{10,4},{12,6},{14,0},{1,11},{3,13... | collective-permute-start | bytes 393224 | tf_op jit(solution)/shard_map/ppermute | solution.py:253
  147.5 11.7 %collective-permute-start.34 = (f32[256,128]{1,0:T(8,128)S(1)}, f32[256,128]{1,0:T(8,128)S(1)}, u32[]{:S(2)}, u32[]{:S(2)}) collective-permute-start(f32[256,128]{1,0:T(8,128)S(1)} %get-tuple-element.66), channel_id=1, source_target_pairs={{0,4},{2,6},{4,0},{6,2},{8,12},{10,14},{12,8},{14,10},{1,5},{3,7},... | collective-permute-start | bytes 393224 | tf_op jit(solution)/shard_map/ppermute | solution.py:253
  150.2 9.0 %collective-permute-start.35 = (f32[256,128]{1,0:T(8,128)S(1)}, f32[256,128]{1,0:T(8,128)S(1)}, u32[]{:S(2)}, u32[]{:S(2)}) collective-permute-start(f32[256,128]{1,0:T(8,128)S(1)} %get-tuple-element.67), channel_id=1, source_target_pairs={{0,12},{2,14},{4,8},{6,10},{8,4},{10,6},{12,0},{14,2},{1,13},{3,15... | collective-permute-start | bytes 393224 | tf_op jit(solution)/shard_map/ppermute | solution.py:253
  153.0 9.3 %collective-permute-start.36 = (f32[256,128]{1,0:T(8,128)S(1)}, f32[256,128]{1,0:T(8,128)S(1)}, u32[]{:S(2)}, u32[]{:S(2)}) collective-permute-start(f32[256,128]{1,0:T(8,128)S(1)} %get-tuple-element.68), channel_id=1, source_target_pairs={{0,6},{2,0},{4,2},{6,4},{8,14},{10,8},{12,10},{14,12},{1,7},{3,1},... | collective-permute-start | bytes 393224 | tf_op jit(solution)/shard_map/ppermute | solution.py:253
  154.4 7.9 %collective-permute-start.37 = (f32[256,128]{1,0:T(8,128)S(1)}, f32[256,128]{1,0:T(8,128)S(1)}, u32[]{:S(2)}, u32[]{:S(2)}) collective-permute-start(f32[256,128]{1,0:T(8,128)S(1)} %get-tuple-element.69), channel_id=1, source_target_pairs={{0,14},{2,8},{4,10},{6,12},{8,6},{10,0},{12,2},{14,4},{1,15},{3,9}... | collective-permute-start | bytes 393224 | tf_op jit(solution)/shard_map/ppermute | solution.py:253
  (11 other events, 83.7 us)

commit v5 on v4

--- a/solution.py
+++ b/solution.py
@@ -171,10 +171,19 @@
 
 
 def join_body(*refs):
-    blocks, out = refs[:-2], refs[-1]
+    blocks, out = refs[:-1], refs[-1]
     rows = blocks[0].shape[0]
     for place, block in enumerate(blocks):
         out[place * rows : (place + 1) * rows] = block[...]
+
+
+def join_pairs_body(*refs):
+    blocks, out = refs[:-2], refs[-1]
+    rows = blocks[0].shape[0] // 2
+    for place, block in enumerate(blocks):
+        for half in range(2):
+            first = (half * len(blocks) + place) * rows
+            out[first : first + rows] = block[half * rows : (half + 1) * rows]
 
 
 def pair_body(mine, other, *refs):
@@ -193,10 +202,9 @@
         first += out.shape[0]
 
 
-def add_body(mine, other, *outs):
-    rows = mine.shape[0] // len(outs)
-    for step, out in enumerate(outs):
-        here = pl.ds(step * rows, rows)
+def add_body(place, count, mine, other, *refs):
+    for step, out in enumerate(refs[-count:]):
+        here = pl.ds((place + step) * out.shape[0], out.shape[0])
         out[...] = mine[here, :] + other[here, :]
 
 
@@ -257,9 +265,18 @@
     return lax.all_to_all(value, axes, 0, 0, tiled=True)
 
 
-def offset_of(ring_index, pair_index, ring, pair, sign):
-    step = (sign * (lax.axis_index(ring) - ring_index)) % lax.axis_size(ring)
+def gather_place(ring_index, pair_index, ring, pair):
+    size = lax.axis_size(ring)
+    return (pair_index ^ lax.axis_index(pair)) * size + (lax.axis_index(ring) - ring_index) % size
+
+
+def scatter_place(ring_index, pair_index, ring, pair):
+    step = (ring_index - lax.axis_index(ring)) % lax.axis_size(ring)
     return step * 2 + (pair_index ^ lax.axis_index(pair))
+
+
+def around(value, axis):
+    return [value] + [ring_send(value, axis, step) for step in range(1, lax.axis_size(axis))]
 
 
 def body(features, weight, tile_vals, tile_index, tile_count, out_grad):
@@ -281,54 +298,53 @@
 
     plane = src_home // 2
 
-    def src_place(sign):
-        return src_half + per * offset_of(plane % n_z, plane // n_z, "z", "xl", sign)
-
-    def dest_place(sign):
-        return dest_tile + per * offset_of(dest_home // 2, dest_home % 2, "y", "xh", sign)
+    src_at = (plane % n_z, plane // n_z, "z", "xl")
+    dest_at = (dest_home // 2, dest_home % 2, "y", "xh")
 
     live = jnp.arange(tiles.shape[0], dtype=jnp.int32) < count[0]
     src_take, dest_put, dest_take0, dest_take1, src_put0, src_put1 = [
         jnp.where(live, index, 0).astype(jnp.int32)
         for index in (
-            src_place(1),
-            dest_place(-1),
-            dest_place(1),
+            src_half + per * gather_place(*src_at),
+            dest_tile + per * scatter_place(*dest_at),
+            dest_tile + per * gather_place(*dest_at),
             dest,
             src_half + per * plane,
-            src_place(-1),
+            src_half + per * scatter_place(*src_at),
         )
     ]
 
     half = (rows, EDGE)
     full = (rows, width)
-    gathered = []
-    for chunk in range(2):
-        part = features[:, chunk * EDGE : (chunk + 1) * EDGE]
-        after = gathered[0][1:] if chunk else []
-        (both,) = whole_call(
-            pair_body,
-            [(2 * rows, EDGE)],
-            part,
-            swap(part, "xl"),
-            *after,
-            skipped=len(after),
-            name=f"pair{chunk}",
-        )
-        gathered.append([both] + [ring_send(both, "z", step) for step in range(1, n_z)])
+    block = [(n_z * rows, EDGE)]
+    parts = [features[:, :EDGE], features[:, EDGE:]]
+    first = around(parts[0], "z")
+    second = around(swap(parts[0], "xl"), "z")
+    (both,) = whole_call(
+        pair_body,
+        [(2 * rows, EDGE)],
+        parts[1],
+        swap(parts[1], "xl"),
+        *second[1:],
+        skipped=n_z - 1,
+        name="pair1",
+    )
+    gathered = around(both, "z")
+    (first,) = whole_call(join_body, block, *first, name="join0")
+    (second,) = whole_call(join_body, block, *second, name="join1")
     partial0 = spread(
         tiles,
         src_take,
         dest_put,
         count,
-        gathered[0] + [swap(block, "core") for block in gathered[0]],
+        [first, second, swap(first, "core"), swap(second, "core")],
         [2 * rows] * n_y,
         False,
         [],
         "forward0",
     )
     (joined,) = whole_call(
-        join_body, [(half_tiles * EDGE, EDGE)], *gathered[1], partial0[0], skipped=1, name="join"
+        join_pairs_body, [(half_tiles * EDGE, EDGE)], *gathered, partial0[0], skipped=1, name="join2"
     )
     partial1 = spread(
         tiles,
@@ -365,10 +381,10 @@
         name="middle",
     )
 
-    (both,) = whole_call(pair_body, [(2 * rows, EDGE)], grad0, swap(grad0, "xh"), name="pair2")
-    sources0 = [both] + [ring_send(both, "y", step) for step in range(1, n_y)]
+    other = swap(grad0, "xh")
+    sources0 = around(grad0, "y") + around(other, "y")
     (copied,) = whole_call(
-        copies_body, [(n_row, rows + piece_rows, EDGE)], grad1, weight_part, both, skipped=1, name="copies"
+        copies_body, [(n_row, rows + piece_rows, EDGE)], grad1, weight_part, other, skipped=1, name="copies"
     )
     arrived = exchange(copied, ROW_AXES)
     sources1, piece = whole_call(
@@ -406,7 +422,13 @@
         [share],
         "backward1",
     )
-    shares = whole_call(add_body, [half] * n_plane, mine, swap(other, "core"), name="share1")
+    shares = whole_call(
+        functools.partial(add_body, 0, n_plane),
+        [half] * n_plane,
+        mine,
+        swap(other, "core"),
+        name="share1",
+    )
     arrived = [offset_send(shares[offset], PLANE_AXES, "z", offset) for offset in range(1, n_plane)]
     grad_x0, piece = whole_call(sum_body, [half, (piece_rows, EDGE)], terms, name="sum0")
     (grad_x,) = whole_call(finish_body, [full], grad_x0, shares[0], *arrived, name="finish")

time: 165 us -> 158 us (0.958); the launches traced: 164 us -> 160 us
  waiting for transfers between devices: 60.4 us -> 54.8 us
  starting transfers between devices: 76.4 us -> 78.7 us
    ppermute x12 -> x10, waiting for transfers between devices: 13.2 us -> 4.38 us  [swap(): return lax.ppermute(value, axis, [(0, 1), (1, 0)])]
    all_to_all x3, waiting for transfers between devices: 10.7 us -> 19.3 us  [exchange(): return lax.all_to_all(value, axes, 0, 0, tiled=True)]
    ppermute x12 -> x18, starting transfers between devices: 22.8 us -> 28.2 us  [ring_send(): lax.ppermute(value, axis, [(place, (place + step) % size) for place in ra...]
    ppermute x12 -> x18, waiting for transfers between devices: 24.4 us -> 19.3 us  [ring_send(): lax.ppermute(value, axis, [(place, (place + step) % size) for place in ra...]
    all_to_all x3, starting transfers between devices: 20.5 us -> 18 us  [exchange(): return lax.all_to_all(value, axes, 0, 0, tiled=True)]
    ppermute x12 -> x10, starting transfers between devices: 8.19 us -> 7.06 us  [swap(): return lax.ppermute(value, axis, [(0, 1), (1, 0)])]
  transfers between devices with their start and end apart: 41 -> 45, of which waited for: 22 -> 19; matrix products, arithmetic and copies ran while one was open for 1% -> 0% of each run, Pallas kernels for 11% -> 12%
where the time goes in v5:
time: 158 us; the launch traced here: 160 us
  starting transfers between devices  78.7 us (50%)
  waiting for transfers between devices  54.8 us (35%)
  Pallas kernels  23 us (15%)
  local copies, waits for them, and re-layouts  1.73 us (1%)
    ppermute x18, starting transfers between devices, ring_send(): lax.ppermute(value, axis, [(place, (place + step) % size) for place in ra...  28.2 us
    ppermute x14, starting transfers between devices, offset_send(): return lax.ppermute(value, axes, hops)  25.5 us
    all_to_all x3, waiting for transfers between devices, exchange(): return lax.all_to_all(value, axes, 0, 0, tiled=True)  19.3 us
    ppermute x18, waiting for transfers between devices, ring_send(): lax.ppermute(value, axis, [(place, (place + step) % size) for place in ra...  19.3 us
    all_to_all x3, starting transfers between devices, exchange(): return lax.all_to_all(value, axes, 0, 0, tiled=True)  18 us
    pallas_call x4, Pallas kernels, spread(): pl.pallas_call(functools.partial(spread_body, flipped, len(sources), len(...  16.4 us
    ppermute x14, waiting for transfers between devices, offset_send(): return lax.ppermute(value, axes, hops)  11.8 us
    ppermute x10, starting transfers between devices, swap(): return lax.ppermute(value, axis, [(0, 1), (1, 0)])  7.06 us
  transfers between devices with their start and end apart: 45, of which 19 were waited for; matrix products, arithmetic and copies ran while one was open for 0% of the time, Pallas kernels for 12%

profile of v5, /device:TPU:0, one launch (start us, length us, event | category | flops | bytes accessed | tf_op | source)
XLA Modules:
  0.0 159.9 jit_solution(393499027242665924)
XLA Ops:
  3.3 1.9 %collective-permute-start = (f32[256,128]{1,0:T(8,128)S(1)}, f32[256,128]{1,0:T(8,128)S(1)}, u32[]{:S(2)}, u32[]{:S(2)}) collective-permute-start(f32[256,128]{1,0:T(8,128)S(1)} %get-tuple-element.76.refs_0_), channel_id=1, source_target_pairs={{0,2},{2,4},{4,6},{6,0},{1,3},{3,5},{5,7},{7,1},{8,10},{10,12},{12... | collective-permute-start | bytes 393224 | tf_op jit(solution)/shard_map/ppermute | solution.py:248
  5.2 3.6 %collective-permute-start.1 = (f32[256,128]{1,0:T(8,128)S(1)}, f32[256,128]{1,0:T(8,128)S(1)}, u32[]{:S(2)}, u32[]{:S(2)}) collective-permute-start(f32[256,128]{1,0:T(8,128)S(1)} %get-tuple-element.76.refs_0_), channel_id=1, source_target_pairs={{0,4},{2,6},{4,0},{6,2},{1,5},{3,7},{5,1},{7,3},{8,12},{10,14},{12... | collective-permute-start | bytes 393224 | tf_op jit(solution)/shard_map/ppermute | solution.py:248
  13.7 2.3 %collective-permute-done.1.refs_2_ = f32[256,128]{1,0:T(8,128)S(1)} collective-permute-done((f32[256,128]{1,0:T(8,128)S(1)}, f32[256,128]{1,0:T(8,128)S(1)}, u32[]{:S(2)}, u32[]{:S(2)}) %collective-permute-start.1) | collective-permute-done | bytes 131104 | tf_op jit(solution)/shard_map/ppermute | solution.py:248
  17.9 2.2 %collective-permute-done.5.refs_2_.refs_1_ = f32[256,128]{1,0:T(8,128)S(1)} collective-permute-done((f32[256,128]{1,0:T(8,128)S(1)}, f32[256,128]{1,0:T(8,128)S(1)}, u32[]{:S(2)}, u32[]{:S(2)}) %collective-permute-start.5) | collective-permute-done | bytes 131104 | tf_op jit(solution)/shard_map/ppermute | solution.py:248
  22.2 2.4 %collective-permute-start.14 = (f32[512,128]{1,0:T(8,128)S(1)}, f32[512,128]{1,0:T(8,128)S(1)}, u32[]{:S(2)}, u32[]{:S(2)}) collective-permute-start(f32[512,128]{1,0:T(8,128)S(1)} %pair1.1.refs_0_), channel_id=1, source_target_pairs={{0,4},{2,6},{4,0},{6,2},{1,5},{3,7},{5,1},{7,3},{8,12},{10,14},{12... | collective-permute-start | bytes 786440 | tf_op jit(solution)/shard_map/ppermute | solution.py:248
  26.0 3.8 %forward0.1 = (f32[512,128]{1,0:T(8,128)S(1)}, f32[512,128]{1,0:T(8,128)S(1)}, f32[512,128]{1,0:T(8,128)S(1)}, f32[512,128]{1,0:T(8,128)S(1)}) custom-call(s32[256]{0:T(256)S(1)} %get-tuple-element.78.take, s32[256]{0:T(256)S(1)} %get-tuple-element.84.put, s32[1]{0:T(128)} %bitcast.7.count, f32[256,128,128]{2,1,0:T(8,128)} %bitcast.11, ...), custom_call_target="tpu_custom_call" | custom-call | tf_op jit(solution)/shard_map/forward0/pallas_call | solution.py:104
  31.1 5.8 %collective-permute-done.14.refs_2_ = f32[512,128]{1,0:T(8,128)S(1)} collective-permute-done((f32[512,128]{1,0:T(8,128)S(1)}, f32[512,128]{1,0:T(8,128)S(1)}, u32[]{:S(2)}, u32[]{:S(2)}) %collective-permute-start.14) | collective-permute-done | bytes 262176 | tf_op jit(solution)/shard_map/ppermute | solution.py:248
  39.0 2.9 %collective-permute-start.10 = (f32[512,128]{1,0:T(8,128)S(1)}, f32[512,128]{1,0:T(8,128)S(1)}, u32[]{:S(2)}, u32[]{:S(2)}) collective-permute-start(f32[512,128]{1,0:T(8,128)S(1)} %get-tuple-element.39), channel_id=1, source_target_pairs={{0,64},{32,96},{64,0},{96,32},{1,65},{33,97},{65,1},{97,33},{2,66}... | collective-permute-start | bytes 786440 | tf_op jit(solution)/shard_map/ppermute | solution.py:248
  43.3 3.8 %forward1.1 = (f32[256,128]{1,0:T(8,128)S(1)}, f32[256,128]{1,0:T(8,128)S(1)}, f32[256,128]{1,0:T(8,128)S(1)}, f32[256,128]{1,0:T(8,128)S(1)}, f32[256,128]{1,0:...) custom-call(s32[256]{0:T(256)S(1)} %get-tuple-element.78.take, ...), custom_call_target="tpu_custom_call" | custom-call | tf_op jit(solution)/shard_map/forward1/pallas_call | solution.py:104
  47.1 2.8 %collective-permute-start.17 = (f32[256,128]{1,0:T(8,128)S(1)}, f32[256,128]{1,0:T(8,128)S(1)}, u32[]{:S(2)}, u32[]{:S(2)}) collective-permute-start(f32[256,128]{1,0:T(8,128)S(1)} %get-tuple-element.41), channel_id=1, source_target_pairs={{0,16},{16,0},{32,48},{48,32},{64,80},{80,64},{96,112},{112,96},{1... | collective-permute-start | bytes 393224 | tf_op jit(solution)/shard_map/ppermute | solution.py:261
  50.8 3.8 %collective-permute-done.10.refs_2_ = f32[512,128]{1,0:T(8,128)S(1)} collective-permute-done((f32[512,128]{1,0:T(8,128)S(1)}, f32[512,128]{1,0:T(8,128)S(1)}, u32[]{:S(2)}, u32[]{:S(2)}) %collective-permute-start.10) | collective-permute-done | bytes 262176 | tf_op jit(solution)/shard_map/ppermute | solution.py:248
  55.3 5.5 %collective-permute-start.22 = (f32[256,128]{1,0:T(8,128)S(1)}, f32[256,128]{1,0:T(8,128)S(1)}, u32[]{:S(2)}, u32[]{:S(2)}) collective-permute-start(f32[256,128]{1,0:T(8,128)S(1)} %get-tuple-element.48), channel_id=1, source_target_pairs={{0,80},{16,64},{32,112},{48,96},{64,16},{80,0},{96,48},{112,32},{1... | collective-permute-start | bytes 393224 | tf_op jit(solution)/shard_map/ppermute | solution.py:261
  60.9 2.2 %collective-permute-start.24 = (f32[256,128]{1,0:T(8,128)S(1)}, f32[256,128]{1,0:T(8,128)S(1)}, u32[]{:S(2)}, u32[]{:S(2)}) collective-permute-start(f32[256,128]{1,0:T(8,128)S(1)} %get-tuple-element.50), channel_id=1, source_target_pairs={{0,112},{16,96},{32,16},{48,0},{64,48},{80,32},{96,80},{112,64},{1... | collective-permute-start | bytes 393224 | tf_op jit(solution)/shard_map/ppermute | solution.py:261
  63.0 1.7 %collective-permute-start.18 = (f32[256,128]{1,0:T(8,128)S(1)}, f32[256,128]{1,0:T(8,128)S(1)}, u32[]{:S(2)}, u32[]{:S(2)}) collective-permute-start(f32[256,128]{1,0:T(8,128)S(1)} %get-tuple-element.43), channel_id=1, source_target_pairs={{0,16},{16,0},{1,17},{17,1},{2,18},{18,2},{3,19},{19,3},{4,20},{20... | collective-permute-start | bytes 393224 | tf_op jit(solution)/shard_map/ppermute | solution.py:243
  65.4 4.3 %collective-permute-done.23.refs_6_ = f32[256,128]{1,0:T(8,128)S(1)} collective-permute-done((f32[256,128]{1,0:T(8,128)S(1)}, f32[256,128]{1,0:T(8,128)S(1)}, u32[]{:S(2)}, u32[]{:S(2)}) %collective-permute-start.23) | collective-permute-done | bytes 131104 | tf_op jit(solution)/shard_map/ppermute | solution.py:261
  71.3 2.6 %collective-permute-start.28 = (f32[256,128]{1,0:T(8,128)S(1)}, f32[256,128]{1,0:T(8,128)S(1)}, u32[]{:S(2)}, u32[]{:S(2)}) collective-permute-start(f32[256,128]{1,0:T(8,128)S(1)} %get-tuple-element.52.refs_0_), channel_id=1, source_target_pairs={{0,16},{16,0},{1,17},{17,1},{2,18},{18,2},{3,19},{19,3},{4,20},{20... | collective-permute-start | bytes 393224 | tf_op jit(solution)/shard_map/ppermute | solution.py:243
  76.3 1.9 %collective-permute-start.27 = (f32[256,128]{1,0:T(8,128)S(1)}, f32[256,128]{1,0:T(8,128)S(1)}, u32[]{:S(2)}, u32[]{:S(2)}) collective-permute-start(f32[256,128]{1,0:T(8,128)S(1)} %get-tuple-element.52.refs_0_), channel_id=1, source_target_pairs={{0,96},{32,0},{64,32},{96,64},{1,97},{33,1},{65,33},{97,65},{2,98}... | collective-permute-start | bytes 393224 | tf_op jit(solution)/shard_map/ppermute | solution.py:248
  80.8 2.1 %collective-permute-done.25.refs_1_ = f32[256,128]{1,0:T(8,128)S(1)} collective-permute-done((f32[256,128]{1,0:T(8,128)S(1)}, f32[256,128]{1,0:T(8,128)S(1)}, u32[]{:S(2)}, u32[]{:S(2)}) %collective-permute-start.25) | collective-permute-done | bytes 131104 | tf_op jit(solution)/shard_map/ppermute | solution.py:248
  84.1 4.3 %all-to-all-start = ((f32[8,320,128]{2,1,0:T(8,128)}), f32[8,320,128]{2,1,0:T(8,128)S(1)}, u32[]{:S(2)}, u32[]{:S(2)}) async-start(f32[8,320,128]{2,1,0:T(8,128)} %copies.1.refs_8_), calls=%async_computation | async-start | bytes 2621440 | tf_op jit(solution)/shard_map/all_to_all | solution.py:265
  88.6 4.9 %backward0.1 = (f32[2048,128]{1,0:T(8,128)S(1)}, f32[2048,128]{1,0:T(8,128)}) custom-call(s32[256]{0:T(256)S(1)} %get-tuple-element.85.take, s32[256]{0:T(256)S(1)} %get-tuple-element.77.put, s32[1]{0:T(128)} %bitcast.9.count, f32[256,128,128]{2,1,0:T(8,128)} %bitcast.13, f32[256,128]{1,0:T(8,128)S(1)} %get-tuple-element.52.refs_0_, ...), custom_call_target="tpu_custom_call" | custom-call | tf_op jit(solution)/shard_map/backward0/pallas_call | solution.py:104
  93.6 12.1 %all-to-all-done.arrived = f32[8,320,128]{2,1,0:T(8,128)S(1)} async-done(((f32[8,320,128]{2,1,0:T(8,128)}), f32[8,320,128]{2,1,0:T(8,128)S(1)}, u32[]{:S(2)}, u32[]{:S(2)}) %all-to-all-start) | async-done | bytes 1310752 | tf_op jit(solution)/shard_map/all_to_all | solution.py:265
  107.1 2.4 %share0.1.refs_1_ = f32[8,320,128]{2,1,0:T(8,128)} custom-call(f32[2048,128]{1,0:T(8,128)S(1)} %get-tuple-element.55.mine, f32[2048,128]{1,0:T(8,128)} %collective-permute-done.32.other, f32[64,128]{1,0:T(8,128)S(1)} %get-tuple-element.57.piece, f32[64,128]{1,0:T(8,128)S(1)} %collective-permute-done.33.other_piece), custom_call_target="tpu_custom_call" | custom-call | tf_op jit(solution)/shard_map/share0/pallas_call | solution.py:123
  109.6 10.3 %all-to-all-start.1 = ((f32[8,320,128]{2,1,0:T(8,128)}), f32[8,320,128]{2,1,0:T(8,128)S(1)}, u32[]{:S(2)}, u32[]{:S(2)}) async-start(f32[8,320,128]{2,1,0:T(8,128)} %share0.1.refs_1_), calls=%async_computation.1 | async-start | bytes 2621440 | tf_op jit(solution)/shard_map/all_to_all | solution.py:265
  119.9 4.0 %backward1.1 = (f32[2048,128]{1,0:T(8,128)S(1)}, f32[2048,128]{1,0:T(8,128)S(1)}) custom-call(s32[256]{0:T(256)S(1)} %get-tuple-element.86.take, s32[256]{0:T(256)S(1)} %get-tuple-element.71.put, s32[1]{0:T(128)} %bitcast.10.count, f32[256,128,128]{2,1,0:T(8,128)} %bitcast.14, f32[2048,128]{1,0:T(8,128)S(1)} %get-tuple-element.59.refs_0_, ...), custom_call_target="tpu_custom_call" | custom-call | tf_op jit(solution)/shard_map/backward1/pallas_call | solution.py:104
  123.9 2.6 %collective-permute-done.34.other = f32[2048,128]{1,0:T(8,128)S(1)} collective-permute-done((f32[2048,128]{1,0:T(8,128)S(1)}, f32[2048,128]{1,0:T(8,128)S(1)}, u32[]{:S(2)}, u32[]{:S(2)}) %collective-permute-start.34) | collective-permute-done | bytes 1048608 | tf_op jit(solution)/shard_map/ppermute | solution.py:243
  126.7 2.9 %collective-permute-start.35 = (f32[256,128]{1,0:T(8,128)S(1)}, f32[256,128]{1,0:T(8,128)S(1)}, u32[]{:S(2)}, u32[]{:S(2)}) collective-permute-start(f32[256,128]{1,0:T(8,128)S(1)} %get-tuple-element.63), channel_id=1, source_target_pairs={{0,8},{2,10},{4,12},{6,14},{8,0},{10,2},{12,4},{14,6},{1,9},{3,11}... | collective-permute-start | bytes 393224 | tf_op jit(solution)/shard_map/ppermute | solution.py:261
  131.0 7.2 %all-to-all-done.1.terms = f32[8,320,128]{2,1,0:T(8,128)S(1)} async-done(((f32[8,320,128]{2,1,0:T(8,128)}), f32[8,320,128]{2,1,0:T(8,128)S(1)}, u32[]{:S(2)}, u32[]{:S(2)}) %all-to-all-start.1) | async-done | bytes 1310752 | tf_op jit(solution)/shard_map/all_to_all | solution.py:265
  139.0 3.4 %all-to-all-start.2 = ((f32[8,64,128]{2,1,0:T(8,128)}), f32[8,64,128]{2,1,0:T(8,128)S(1)}, u32[]{:S(2)}, u32[]{:S(2)}) async-start(f32[8,64,128]{2,1,0:T(8,128)} %broadcast_in_dim.13), calls=%async_computation.2 | async-start | bytes 524288 | tf_op jit(solution)/shard_map/all_to_all | solution.py:265
  143.8 2.7 %collective-permute-start.38 = (f32[256,128]{1,0:T(8,128)S(1)}, f32[256,128]{1,0:T(8,128)S(1)}, u32[]{:S(2)}, u32[]{:S(2)}) collective-permute-start(f32[256,128]{1,0:T(8,128)S(1)} %get-tuple-element.66), channel_id=1, source_target_pairs={{0,4},{2,6},{4,0},{6,2},{8,12},{10,14},{12,8},{14,10},{1,5},{3,7},... | collective-permute-start | bytes 393224 | tf_op jit(solution)/shard_map/ppermute | solution.py:261
  147.9 2.2 %collective-permute-start.40 = (f32[256,128]{1,0:T(8,128)S(1)}, f32[256,128]{1,0:T(8,128)S(1)}, u32[]{:S(2)}, u32[]{:S(2)}) collective-permute-start(f32[256,128]{1,0:T(8,128)S(1)} %get-tuple-element.68), channel_id=1, source_target_pairs={{0,6},{2,0},{4,2},{6,4},{8,14},{10,8},{12,10},{14,12},{1,7},{3,1},... | collective-permute-start | bytes 393224 | tf_op jit(solution)/shard_map/ppermute | solution.py:261
  152.2 3.4 %collective-permute-done.38.refs_4_ = f32[256,128]{1,0:T(8,128)S(1)} collective-permute-done((f32[256,128]{1,0:T(8,128)S(1)}, f32[256,128]{1,0:T(8,128)S(1)}, u32[]{:S(2)}, u32[]{:S(2)}) %collective-permute-start.38) | collective-permute-done | bytes 131104 | tf_op jit(solution)/shard_map/ppermute | solution.py:261
  155.7 2.7 %collective-permute-done.40.refs_6_ = f32[256,128]{1,0:T(8,128)S(1)} collective-permute-done((f32[256,128]{1,0:T(8,128)S(1)}, f32[256,128]{1,0:T(8,128)S(1)}, u32[]{:S(2)}, u32[]{:S(2)}) %collective-permute-start.40) | collective-permute-done | bytes 131104 | tf_op jit(solution)/shard_map/ppermute | solution.py:261
  (86 shorter events, 37.6 us)
Async XLA Ops:
  3.3 9.2 %collective-permute-start = (f32[256,128]{1,0:T(8,128)S(1)}, f32[256,128]{1,0:T(8,128)S(1)}, u32[]{:S(2)}, u32[]{:S(2)}) collective-permute-start(f32[256,128]{1,0:T(8,128)S(1)} %get-tuple-element.76.refs_0_), channel_id=1, source_target_pairs={{0,2},{2,4},{4,6},{6,0},{1,3},{3,5},{5,7},{7,1},{8,10},{10,12},{12... | collective-permute-start | bytes 393224 | tf_op jit(solution)/shard_map/ppermute | solution.py:248
  5.2 10.8 %collective-permute-start.1 = (f32[256,128]{1,0:T(8,128)S(1)}, f32[256,128]{1,0:T(8,128)S(1)}, u32[]{:S(2)}, u32[]{:S(2)}) collective-permute-start(f32[256,128]{1,0:T(8,128)S(1)} %get-tuple-element.76.refs_0_), channel_id=1, source_target_pairs={{0,4},{2,6},{4,0},{6,2},{1,5},{3,7},{5,1},{7,3},{8,12},{10,14},{12... | collective-permute-start | bytes 393224 | tf_op jit(solution)/shard_map/ppermute | solution.py:248
  10.8 9.3 %collective-permute-start.5 = (f32[256,128]{1,0:T(8,128)S(1)}, f32[256,128]{1,0:T(8,128)S(1)}, u32[]{:S(2)}, u32[]{:S(2)}) collective-permute-start(f32[256,128]{1,0:T(8,128)S(1)} %collective-permute-done.3.refs_0_), channel_id=1, source_target_pairs={{0,4},{2,6},{4,0},{6,2},{1,5},{3,7},{5,1},{7,3},{8,12},{10,14},{12... | collective-permute-start | bytes 393224 | tf_op jit(solution)/shard_map/ppermute | solution.py:248
  16.6 9.4 %collective-permute-start.7 = (f32[1024,128]{1,0:T(8,128)S(1)}, f32[1024,128]{1,0:T(8,128)S(1)}, u32[]{:S(2)}, u32[]{:S(2)}) collective-permute-start(f32[1024,128]{1,0:T(8,128)S(1)} %join0.1.refs_0_), channel_id=1, source_target_pairs={{0,1},{1,0},{2,3},{3,2},{4,5},{5,4},{6,7},{7,6},{8,9},{9,8},{10,11... | collective-permute-start | bytes 1572872 | tf_op jit(solution)/shard_map/ppermute | solution.py:243
  21.0 10.1 %collective-permute-start.13 = (f32[512,128]{1,0:T(8,128)S(1)}, f32[512,128]{1,0:T(8,128)S(1)}, u32[]{:S(2)}, u32[]{:S(2)}) collective-permute-start(f32[512,128]{1,0:T(8,128)S(1)} %pair1.1.refs_0_), channel_id=1, source_target_pairs={{0,2},{2,4},{4,6},{6,0},{1,3},{3,5},{5,7},{7,1},{8,10},{10,12},{12... | collective-permute-start | bytes 786440 | tf_op jit(solution)/shard_map/ppermute | solution.py:248
  22.2 14.7 %collective-permute-start.14 = (f32[512,128]{1,0:T(8,128)S(1)}, f32[512,128]{1,0:T(8,128)S(1)}, u32[]{:S(2)}, u32[]{:S(2)}) collective-permute-start(f32[512,128]{1,0:T(8,128)S(1)} %pair1.1.refs_0_), channel_id=1, source_target_pairs={{0,4},{2,6},{4,0},{6,2},{1,5},{3,7},{5,1},{7,3},{8,12},{10,14},{12... | collective-permute-start | bytes 786440 | tf_op jit(solution)/shard_map/ppermute | solution.py:248
  24.6 12.6 %collective-permute-start.15 = (f32[512,128]{1,0:T(8,128)S(1)}, f32[512,128]{1,0:T(8,128)S(1)}, u32[]{:S(2)}, u32[]{:S(2)}) collective-permute-start(f32[512,128]{1,0:T(8,128)S(1)} %pair1.1.refs_0_), channel_id=1, source_target_pairs={{0,6},{2,0},{4,2},{6,4},{1,7},{3,1},{5,3},{7,5},{8,14},{10,8},{12,... | collective-permute-start | bytes 786440 | tf_op jit(solution)/shard_map/ppermute | solution.py:248
  37.4 13.2 %collective-permute-start.9 = (f32[512,128]{1,0:T(8,128)S(1)}, f32[512,128]{1,0:T(8,128)S(1)}, u32[]{:S(2)}, u32[]{:S(2)}) collective-permute-start(f32[512,128]{1,0:T(8,128)S(1)} %get-tuple-element.38), channel_id=1, source_target_pairs={{0,32},{32,64},{64,96},{96,0},{1,33},{33,65},{65,97},{97,1},{2,34}... | collective-permute-start | bytes 786440 | tf_op jit(solution)/shard_map/ppermute | solution.py:248
  39.0 15.6 %collective-permute-start.10 = (f32[512,128]{1,0:T(8,128)S(1)}, f32[512,128]{1,0:T(8,128)S(1)}, u32[]{:S(2)}, u32[]{:S(2)}) collective-permute-start(f32[512,128]{1,0:T(8,128)S(1)} %get-tuple-element.39), channel_id=1, source_target_pairs={{0,64},{32,96},{64,0},{96,32},{1,65},{33,97},{65,1},{97,33},{2,66}... | collective-permute-start | bytes 786440 | tf_op jit(solution)/shard_map/ppermute | solution.py:248
  41.9 13.4 %collective-permute-start.11 = (f32[512,128]{1,0:T(8,128)S(1)}, f32[512,128]{1,0:T(8,128)S(1)}, u32[]{:S(2)}, u32[]{:S(2)}) collective-permute-start(f32[512,128]{1,0:T(8,128)S(1)} %get-tuple-element.40), channel_id=1, source_target_pairs={{0,96},{32,0},{64,32},{96,64},{1,97},{33,1},{65,33},{97,65},{2,98}... | collective-permute-start | bytes 786440 | tf_op jit(solution)/shard_map/ppermute | solution.py:248
  47.1 13.7 %collective-permute-start.17 = (f32[256,128]{1,0:T(8,128)S(1)}, f32[256,128]{1,0:T(8,128)S(1)}, u32[]{:S(2)}, u32[]{:S(2)}) collective-permute-start(f32[256,128]{1,0:T(8,128)S(1)} %get-tuple-element.41), channel_id=1, source_target_pairs={{0,16},{16,0},{32,48},{48,32},{64,80},{80,64},{96,112},{112,96},{1... | collective-permute-start | bytes 393224 | tf_op jit(solution)/shard_map/ppermute | solution.py:261
  49.9 11.0 %collective-permute-start.19 = (f32[256,128]{1,0:T(8,128)S(1)}, f32[256,128]{1,0:T(8,128)S(1)}, u32[]{:S(2)}, u32[]{:S(2)}) collective-permute-start(f32[256,128]{1,0:T(8,128)S(1)} %get-tuple-element.45), channel_id=1, source_target_pairs={{0,32},{16,48},{32,64},{48,80},{64,96},{80,112},{96,0},{112,16},{1... | collective-permute-start | bytes 393224 | tf_op jit(solution)/shard_map/ppermute | solution.py:261
  50.6 12.5 %collective-permute-start.20 = (f32[256,128]{1,0:T(8,128)S(1)}, f32[256,128]{1,0:T(8,128)S(1)}, u32[]{:S(2)}, u32[]{:S(2)}) collective-permute-start(f32[256,128]{1,0:T(8,128)S(1)} %get-tuple-element.46), channel_id=1, source_target_pairs={{0,48},{16,32},{32,80},{48,64},{64,112},{80,96},{96,16},{112,0},{1... | collective-permute-start | bytes 393224 | tf_op jit(solution)/shard_map/ppermute | solution.py:261
  54.6 10.8 %collective-permute-start.21 = (f32[256,128]{1,0:T(8,128)S(1)}, f32[256,128]{1,0:T(8,128)S(1)}, u32[]{:S(2)}, u32[]{:S(2)}) collective-permute-start(f32[256,128]{1,0:T(8,128)S(1)} %get-tuple-element.47), channel_id=1, source_target_pairs={{0,64},{16,80},{32,96},{48,112},{64,0},{80,16},{96,32},{112,48},{1... | collective-permute-start | bytes 393224 | tf_op jit(solution)/shard_map/ppermute | solution.py:261
  55.3 10.1 %collective-permute-start.22 = (f32[256,128]{1,0:T(8,128)S(1)}, f32[256,128]{1,0:T(8,128)S(1)}, u32[]{:S(2)}, u32[]{:S(2)}) collective-permute-start(f32[256,128]{1,0:T(8,128)S(1)} %get-tuple-element.48), channel_id=1, source_target_pairs={{0,80},{16,64},{32,112},{48,96},{64,16},{80,0},{96,48},{112,32},{1... | collective-permute-start | bytes 393224 | tf_op jit(solution)/shard_map/ppermute | solution.py:261
  60.8 8.9 %collective-permute-start.23 = (f32[256,128]{1,0:T(8,128)S(1)}, f32[256,128]{1,0:T(8,128)S(1)}, u32[]{:S(2)}, u32[]{:S(2)}) collective-permute-start(f32[256,128]{1,0:T(8,128)S(1)} %get-tuple-element.49), channel_id=1, source_target_pairs={{0,96},{16,112},{32,0},{48,16},{64,32},{80,48},{96,64},{112,80},{1... | collective-permute-start | bytes 393224 | tf_op jit(solution)/shard_map/ppermute | solution.py:261
  60.9 8.9 %collective-permute-start.24 = (f32[256,128]{1,0:T(8,128)S(1)}, f32[256,128]{1,0:T(8,128)S(1)}, u32[]{:S(2)}, u32[]{:S(2)}) collective-permute-start(f32[256,128]{1,0:T(8,128)S(1)} %get-tuple-element.50), channel_id=1, source_target_pairs={{0,112},{16,96},{32,16},{48,0},{64,48},{80,32},{96,80},{112,64},{1... | collective-permute-start | bytes 393224 | tf_op jit(solution)/shard_map/ppermute | solution.py:261
  73.9 9.0 %collective-permute-start.25 = (f32[256,128]{1,0:T(8,128)S(1)}, f32[256,128]{1,0:T(8,128)S(1)}, u32[]{:S(2)}, u32[]{:S(2)}) collective-permute-start(f32[256,128]{1,0:T(8,128)S(1)} %get-tuple-element.52.refs_0_), channel_id=1, source_target_pairs={{0,32},{32,64},{64,96},{96,0},{1,33},{33,65},{65,97},{97,1},{2,34}... | collective-permute-start | bytes 393224 | tf_op jit(solution)/shard_map/ppermute | solution.py:248
  75.1 13.3 %collective-permute-start.26 = (f32[256,128]{1,0:T(8,128)S(1)}, f32[256,128]{1,0:T(8,128)S(1)}, u32[]{:S(2)}, u32[]{:S(2)}) collective-permute-start(f32[256,128]{1,0:T(8,128)S(1)} %get-tuple-element.52.refs_0_), channel_id=1, source_target_pairs={{0,64},{32,96},{64,0},{96,32},{1,65},{33,97},{65,1},{97,33},{2,66}... | collective-permute-start | bytes 393224 | tf_op jit(solution)/shard_map/ppermute | solution.py:248
  76.3 12.2 %collective-permute-start.27 = (f32[256,128]{1,0:T(8,128)S(1)}, f32[256,128]{1,0:T(8,128)S(1)}, u32[]{:S(2)}, u32[]{:S(2)}) collective-permute-start(f32[256,128]{1,0:T(8,128)S(1)} %get-tuple-element.52.refs_0_), channel_id=1, source_target_pairs={{0,96},{32,0},{64,32},{96,64},{1,97},{33,1},{65,33},{97,65},{2,98}... | collective-permute-start | bytes 393224 | tf_op jit(solution)/shard_map/ppermute | solution.py:248
  78.1 10.3 %collective-permute-start.29 = (f32[256,128]{1,0:T(8,128)S(1)}, f32[256,128]{1,0:T(8,128)S(1)}, u32[]{:S(2)}, u32[]{:S(2)}) collective-permute-start(f32[256,128]{1,0:T(8,128)S(1)} %collective-permute-done.28.refs_1_.refs_4_), channel_id=1, source_target_pairs={{0,32},{32,64},{64,96},{96,0},{1,33},{33,65},{65,97},{97,1},{2,34}... | collective-permute-start | bytes 393224 | tf_op jit(solution)/shard_map/ppermute | solution.py:248
  79.3 9.2 %collective-permute-start.30 = (f32[256,128]{1,0:T(8,128)S(1)}, f32[256,128]{1,0:T(8,128)S(1)}, u32[]{:S(2)}, u32[]{:S(2)}) collective-permute-start(f32[256,128]{1,0:T(8,128)S(1)} %collective-permute-done.28.refs_1_.refs_4_), channel_id=1, source_target_pairs={{0,64},{32,96},{64,0},{96,32},{1,65},{33,97},{65,1},{97,33},{2,66}... | collective-permute-start | bytes 393224 | tf_op jit(solution)/shard_map/ppermute | solution.py:248
  84.1 21.6 %all-to-all-start = ((f32[8,320,128]{2,1,0:T(8,128)}), f32[8,320,128]{2,1,0:T(8,128)S(1)}, u32[]{:S(2)}, u32[]{:S(2)}) async-start(f32[8,320,128]{2,1,0:T(8,128)} %copies.1.refs_8_), calls=%async_computation | async-start | bytes 2621440 | tf_op jit(solution)/shard_map/all_to_all | solution.py:265
  93.5 12.4 %collective-permute-start.32 = (f32[2048,128]{1,0:T(8,128)}, f32[2048,128]{1,0:T(8,128)}, u32[]{:S(2)}, u32[]{:S(2)}) collective-permute-start(f32[2048,128]{1,0:T(8,128)} %get-tuple-element.56), channel_id=1, source_target_pairs={{0,1},{1,0},{2,3},{3,2},{4,5},{5,4},{6,7},{7,6},{8,9},{9,8},{10,11... | collective-permute-start | bytes 3145736 | tf_op jit(solution)/shard_map/ppermute | solution.py:243
  109.6 28.6 %all-to-all-start.1 = ((f32[8,320,128]{2,1,0:T(8,128)}), f32[8,320,128]{2,1,0:T(8,128)S(1)}, u32[]{:S(2)}, u32[]{:S(2)}) async-start(f32[8,320,128]{2,1,0:T(8,128)} %share0.1.refs_1_), calls=%async_computation.1 | async-start | bytes 2621440 | tf_op jit(solution)/shard_map/all_to_all | solution.py:265
  126.7 21.3 %collective-permute-start.35 = (f32[256,128]{1,0:T(8,128)S(1)}, f32[256,128]{1,0:T(8,128)S(1)}, u32[]{:S(2)}, u32[]{:S(2)}) collective-permute-start(f32[256,128]{1,0:T(8,128)S(1)} %get-tuple-element.63), channel_id=1, source_target_pairs={{0,8},{2,10},{4,12},{6,14},{8,0},{10,2},{12,4},{14,6},{1,9},{3,11}... | collective-permute-start | bytes 393224 | tf_op jit(solution)/shard_map/ppermute | solution.py:261
  129.6 20.6 %collective-permute-start.36 = (f32[256,128]{1,0:T(8,128)S(1)}, f32[256,128]{1,0:T(8,128)S(1)}, u32[]{:S(2)}, u32[]{:S(2)}) collective-permute-start(f32[256,128]{1,0:T(8,128)S(1)} %get-tuple-element.64), channel_id=1, source_target_pairs={{0,2},{2,4},{4,6},{6,0},{8,10},{10,12},{12,14},{14,8},{1,3},{3,5},... | collective-permute-start | bytes 393224 | tf_op jit(solution)/shard_map/ppermute | solution.py:261
  139.0 20.2 %all-to-all-start.2 = ((f32[8,64,128]{2,1,0:T(8,128)}), f32[8,64,128]{2,1,0:T(8,128)S(1)}, u32[]{:S(2)}, u32[]{:S(2)}) async-start(f32[8,64,128]{2,1,0:T(8,128)} %broadcast_in_dim.13), calls=%async_computation.2 | async-start | bytes 524288 | tf_op jit(solution)/shard_map/all_to_all | solution.py:265
  142.4 9.8 %collective-permute-start.37 = (f32[256,128]{1,0:T(8,128)S(1)}, f32[256,128]{1,0:T(8,128)S(1)}, u32[]{:S(2)}, u32[]{:S(2)}) collective-permute-start(f32[256,128]{1,0:T(8,128)S(1)} %get-tuple-element.65), channel_id=1, source_target_pairs={{0,10},{2,12},{4,14},{6,8},{8,2},{10,4},{12,6},{14,0},{1,11},{3,13... | collective-permute-start | bytes 393224 | tf_op jit(solution)/shard_map/ppermute | solution.py:261
  143.8 11.9 %collective-permute-start.38 = (f32[256,128]{1,0:T(8,128)S(1)}, f32[256,128]{1,0:T(8,128)S(1)}, u32[]{:S(2)}, u32[]{:S(2)}) collective-permute-start(f32[256,128]{1,0:T(8,128)S(1)} %get-tuple-element.66), channel_id=1, source_target_pairs={{0,4},{2,6},{4,0},{6,2},{8,12},{10,14},{12,8},{14,10},{1,5},{3,7},... | collective-permute-start | bytes 393224 | tf_op jit(solution)/shard_map/ppermute | solution.py:261
  146.5 9.2 %collective-permute-start.39 = (f32[256,128]{1,0:T(8,128)S(1)}, f32[256,128]{1,0:T(8,128)S(1)}, u32[]{:S(2)}, u32[]{:S(2)}) collective-permute-start(f32[256,128]{1,0:T(8,128)S(1)} %get-tuple-element.67), channel_id=1, source_target_pairs={{0,12},{2,14},{4,8},{6,10},{8,4},{10,6},{12,0},{14,2},{1,13},{3,15... | collective-permute-start | bytes 393224 | tf_op jit(solution)/shard_map/ppermute | solution.py:261
  147.9 10.4 %collective-permute-start.40 = (f32[256,128]{1,0:T(8,128)S(1)}, f32[256,128]{1,0:T(8,128)S(1)}, u32[]{:S(2)}, u32[]{:S(2)}) collective-permute-start(f32[256,128]{1,0:T(8,128)S(1)} %get-tuple-element.68), channel_id=1, source_target_pairs={{0,6},{2,0},{4,2},{6,4},{8,14},{10,8},{12,10},{14,12},{1,7},{3,1},... | collective-permute-start | bytes 393224 | tf_op jit(solution)/shard_map/ppermute | solution.py:261
  (16 other events, 146.5 us)

commit v6 on v5

--- a/solution.py
+++ b/solution.py
@@ -160,7 +160,7 @@
     for place in range(out.shape[0]):
         out[place, :rows] = value[...]
         if out.shape[1] > rows:
-            out[place, rows:] = refs[0][place]
+            out[place, rows:] = refs[0][place] + refs[1][place]
 
 
 def unpack_body(arrived, rows_out, piece):
@@ -202,19 +202,18 @@
         first += out.shape[0]
 
 
-def add_body(place, count, mine, other, *refs):
-    for step, out in enumerate(refs[-count:]):
-        here = pl.ds((place + step) * out.shape[0], out.shape[0])
-        out[...] = mine[here, :] + other[here, :]
-
-
-def share_body(mine, other, piece, other_piece, out):
+def add_body(count, mine, *refs):
+    others, outs = refs[:count], refs[count:]
+    for step, (other, out) in enumerate(zip(others, outs)):
+        out[...] = mine[pl.ds(step * out.shape[0], out.shape[0]), :] + other[...]
+
+
+def share_body(mine, other, piece, out):
     rows = out.shape[1] - piece.shape[0]
-    both = piece[...] + other_piece[...]
     for place in range(out.shape[0]):
         here = pl.ds(place * rows, rows)
         out[place, :rows] = mine[here, :] + other[here, :]
-        out[place, rows:] = both
+        out[place, rows:] = piece[...]
 
 
 def sum_body(terms, grad, piece):
@@ -384,7 +383,14 @@
     other = swap(grad0, "xh")
     sources0 = around(grad0, "y") + around(other, "y")
     (copied,) = whole_call(
-        copies_body, [(n_row, rows + piece_rows, EDGE)], grad1, weight_part, other, skipped=1, name="copies"
+        copies_body,
+        [(n_row, rows + piece_rows, EDGE)],
+        grad1,
+        weight_part,
+        swap(weight_part, "core"),
+        other,
+        skipped=1,
+        name="copies",
     )
     arrived = exchange(copied, ROW_AXES)
     sources1, piece = whole_call(
@@ -407,31 +413,33 @@
         mine,
         swap(other, "core"),
         piece,
-        swap(piece, "core"),
         name="share0",
     )
     terms = exchange(share, PLANE_AXES)
-    mine, other = spread(
+    mine, *others = spread(
         tiles,
         dest_take1,
         src_put1,
         count,
         [sources1],
-        [half_tiles * EDGE] * 2,
+        [half_tiles * EDGE] + [2 * rows] * n_z,
         True,
         [share],
         "backward1",
     )
     shares = whole_call(
-        functools.partial(add_body, 0, n_plane),
-        [half] * n_plane,
+        functools.partial(add_body, n_z),
+        [(2 * rows, EDGE)] * n_z,
         mine,
-        swap(other, "core"),
+        *[swap(other, "core") for other in others],
         name="share1",
     )
-    arrived = [offset_send(shares[offset], PLANE_AXES, "z", offset) for offset in range(1, n_plane)]
+    arrived = [ring_send(shares[step], "z", step) for step in range(1, n_z)]
+    own, other = whole_call(
+        functools.partial(fold_body, n_z), [half, half], shares[0], *arrived, mine, skipped=1, name="fold1"
+    )
     grad_x0, piece = whole_call(sum_body, [half, (piece_rows, EDGE)], terms, name="sum0")
-    (grad_x,) = whole_call(finish_body, [full], grad_x0, shares[0], *arrived, name="finish")
+    (grad_x,) = whole_call(finish_body, [full], grad_x0, own, swap(other, "xl"), name="finish")
 
     pieces = exchange(jnp.broadcast_to(piece[None], (n_row, piece_rows, EDGE)), ROW_AXES)
     scale = (rows * n_row * n_col) ** (-0.5)

time: 158 us -> 151 us (0.956)
  waiting for transfers between devices: 54.8 us -> 49.3 us
  starting transfers between devices: 78.7 us -> 76.7 us
    ppermute x14 -> x7, starting transfers between devices: 25.5 us -> 12 us  [offset_send(): return lax.ppermute(value, axes, hops)]
    ppermute x14 -> x7, waiting for transfers between devices: 11.8 us -> 4.97 us  [offset_send(): return lax.ppermute(value, axes, hops)]
    all_to_all x3, waiting for transfers between devices: 19.3 us -> 12.8 us  [exchange(): return lax.all_to_all(value, axes, 0, 0, tiled=True)]
    ppermute x18 -> x21, waiting for transfers between devices: 19.3 us -> 25.5 us  [ring_send(): lax.ppermute(value, axis, [(place, (place + step) % size) for place in ra...]
    ppermute x18 -> x21, starting transfers between devices: 28.2 us -> 33.9 us  [ring_send(): lax.ppermute(value, axis, [(place, (place + step) % size) for place in ra...]
    ppermute x10 -> x14, starting transfers between devices: 7.06 us -> 12.4 us  [swap(): return lax.ppermute(value, axis, [(0, 1), (1, 0)])]
    ppermute x10 -> x14, waiting for transfers between devices: 4.38 us -> 6.03 us  [swap(): return lax.ppermute(value, axis, [(0, 1), (1, 0)])]
    pallas_call x13 -> x14, Pallas kernels: 6.63 us -> 7.5 us  [whole_call(): pl.pallas_call(kernel, in_specs=[here] * (len(args) - skipped) + [there]...]
  transfers between devices with their start and end apart: 45 -> 45, of which waited for: 19 -> 19; matrix products, arithmetic and copies ran while one was open for 0% -> 1% of each run, Pallas kernels for 12% -> 13%
where the time goes in v6:
time: 151 us; the launch traced here: 153 us
  starting transfers between devices  76.7 us (51%)
  waiting for transfers between devices  49.3 us (33%)
  Pallas kernels  23.9 us (16%)
  local copies, waits for them, and re-layouts  1.74 us (1%)
  between operations  1.56 us (1%)
    ppermute x21, starting transfers between devices, ring_send(): lax.ppermute(value, axis, [(place, (place + step) % size) for place in ra...  33.9 us
    ppermute x21, waiting for transfers between devices, ring_send(): lax.ppermute(value, axis, [(place, (place + step) % size) for place in ra...  25.5 us
    all_to_all x3, starting transfers between devices, exchange(): return lax.all_to_all(value, axes, 0, 0, tiled=True)  18.4 us
    pallas_call x4, Pallas kernels, spread(): pl.pallas_call(functools.partial(spread_body, flipped, len(sources), len(...  16.4 us
    all_to_all x3, waiting for transfers between devices, exchange(): return lax.all_to_all(value, axes, 0, 0, tiled=True)  12.8 us
    ppermute x14, starting transfers between devices, swap(): return lax.ppermute(value, axis, [(0, 1), (1, 0)])  12.4 us
    ppermute x7, starting transfers between devices, offset_send(): return lax.ppermute(value, axes, hops)  12 us
    pallas_call x14, Pallas kernels, whole_call(): pl.pallas_call(kernel, in_specs=[here] * (len(args) - skipped) + [there]...  7.5 us
  transfers between devices with their start and end apart: 45, of which 19 were waited for; matrix products, arithmetic and copies ran while one was open for 1% of the time, Pallas kernels for 13%

profile of v6, /device:TPU:0, one launch (start us, length us, event | category | flops | bytes accessed | tf_op | source)
XLA Modules:
  0.0 153.3 jit_solution(15822422435833196247)
XLA Ops:
  1.6 1.7 %collective-permute-start.3 = (f32[256,128]{1,0:T(8,128)S(1)}, f32[256,128]{1,0:T(8,128)S(1)}, u32[]{:S(2)}, u32[]{:S(2)}) collective-permute-start(f32[256,128]{1,0:T(8,128)S(1)} %get-tuple-element.78.refs_0_), channel_id=1, source_target_pairs={{0,8},{8,0},{1,9},{9,1},{2,10},{10,2},{3,11},{11,3},{4,12},{12,4},... | collective-permute-start | bytes 393224 | tf_op jit(solution)/shard_map/ppermute | solution.py:242
  3.3 1.9 %collective-permute-start = (f32[256,128]{1,0:T(8,128)S(1)}, f32[256,128]{1,0:T(8,128)S(1)}, u32[]{:S(2)}, u32[]{:S(2)}) collective-permute-start(f32[256,128]{1,0:T(8,128)S(1)} %get-tuple-element.78.refs_0_), channel_id=1, source_target_pairs={{0,2},{2,4},{4,6},{6,0},{1,3},{3,5},{5,7},{7,1},{8,10},{10,12},{12... | collective-permute-start | bytes 393224 | tf_op jit(solution)/shard_map/ppermute | solution.py:247
  5.2 3.6 %collective-permute-start.1 = (f32[256,128]{1,0:T(8,128)S(1)}, f32[256,128]{1,0:T(8,128)S(1)}, u32[]{:S(2)}, u32[]{:S(2)}) collective-permute-start(f32[256,128]{1,0:T(8,128)S(1)} %get-tuple-element.78.refs_0_), channel_id=1, source_target_pairs={{0,4},{2,6},{4,0},{6,2},{1,5},{3,7},{5,1},{7,3},{8,12},{10,14},{12... | collective-permute-start | bytes 393224 | tf_op jit(solution)/shard_map/ppermute | solution.py:247
  10.8 1.7 %collective-permute-start.5 = (f32[256,128]{1,0:T(8,128)S(1)}, f32[256,128]{1,0:T(8,128)S(1)}, u32[]{:S(2)}, u32[]{:S(2)}) collective-permute-start(f32[256,128]{1,0:T(8,128)S(1)} %collective-permute-done.3.refs_0_), channel_id=1, source_target_pairs={{0,4},{2,6},{4,0},{6,2},{1,5},{3,7},{5,1},{7,3},{8,12},{10,14},{12... | collective-permute-start | bytes 393224 | tf_op jit(solution)/shard_map/ppermute | solution.py:247
  13.7 2.3 %collective-permute-done.1.refs_2_ = f32[256,128]{1,0:T(8,128)S(1)} collective-permute-done((f32[256,128]{1,0:T(8,128)S(1)}, f32[256,128]{1,0:T(8,128)S(1)}, u32[]{:S(2)}, u32[]{:S(2)}) %collective-permute-start.1) | collective-permute-done | bytes 131104 | tf_op jit(solution)/shard_map/ppermute | solution.py:247
  17.9 2.2 %collective-permute-done.5.refs_2_.refs_1_ = f32[256,128]{1,0:T(8,128)S(1)} collective-permute-done((f32[256,128]{1,0:T(8,128)S(1)}, f32[256,128]{1,0:T(8,128)S(1)}, u32[]{:S(2)}, u32[]{:S(2)}) %collective-permute-start.5) | collective-permute-done | bytes 131104 | tf_op jit(solution)/shard_map/ppermute | solution.py:247
  22.2 2.4 %collective-permute-start.14 = (f32[512,128]{1,0:T(8,128)S(1)}, f32[512,128]{1,0:T(8,128)S(1)}, u32[]{:S(2)}, u32[]{:S(2)}) collective-permute-start(f32[512,128]{1,0:T(8,128)S(1)} %pair1.1.refs_0_), channel_id=1, source_target_pairs={{0,4},{2,6},{4,0},{6,2},{1,5},{3,7},{5,1},{7,3},{8,12},{10,14},{12... | collective-permute-start | bytes 786440 | tf_op jit(solution)/shard_map/ppermute | solution.py:247
  26.0 3.8 %forward0.1 = (f32[512,128]{1,0:T(8,128)S(1)}, f32[512,128]{1,0:T(8,128)S(1)}, f32[512,128]{1,0:T(8,128)S(1)}, f32[512,128]{1,0:T(8,128)S(1)}) custom-call(s32[256]{0:T(256)S(1)} %get-tuple-element.80.take, s32[256]{0:T(256)S(1)} %get-tuple-element.86.put, s32[1]{0:T(128)} %bitcast.7.count, f32[256,128,128]{2,1,0:T(8,128)} %bitcast.11, ...), custom_call_target="tpu_custom_call" | custom-call | tf_op jit(solution)/shard_map/forward0/pallas_call | solution.py:104
  31.1 5.8 %collective-permute-done.14.refs_2_ = f32[512,128]{1,0:T(8,128)S(1)} collective-permute-done((f32[512,128]{1,0:T(8,128)S(1)}, f32[512,128]{1,0:T(8,128)S(1)}, u32[]{:S(2)}, u32[]{:S(2)}) %collective-permute-start.14) | collective-permute-done | bytes 262176 | tf_op jit(solution)/shard_map/ppermute | solution.py:247
  39.0 2.9 %collective-permute-start.10 = (f32[512,128]{1,0:T(8,128)S(1)}, f32[512,128]{1,0:T(8,128)S(1)}, u32[]{:S(2)}, u32[]{:S(2)}) collective-permute-start(f32[512,128]{1,0:T(8,128)S(1)} %get-tuple-element.40), channel_id=1, source_target_pairs={{0,64},{32,96},{64,0},{96,32},{1,65},{33,97},{65,1},{97,33},{2,66}... | collective-permute-start | bytes 786440 | tf_op jit(solution)/shard_map/ppermute | solution.py:247
  43.3 3.8 %forward1.1 = (f32[256,128]{1,0:T(8,128)S(1)}, f32[256,128]{1,0:T(8,128)S(1)}, f32[256,128]{1,0:T(8,128)S(1)}, f32[256,128]{1,0:T(8,128)S(1)}, f32[256,128]{1,0:...) custom-call(s32[256]{0:T(256)S(1)} %get-tuple-element.80.take, ...), custom_call_target="tpu_custom_call" | custom-call | tf_op jit(solution)/shard_map/forward1/pallas_call | solution.py:104
  47.1 2.8 %collective-permute-start.17 = (f32[256,128]{1,0:T(8,128)S(1)}, f32[256,128]{1,0:T(8,128)S(1)}, u32[]{:S(2)}, u32[]{:S(2)}) collective-permute-start(f32[256,128]{1,0:T(8,128)S(1)} %get-tuple-element.42), channel_id=1, source_target_pairs={{0,16},{16,0},{32,48},{48,32},{64,80},{80,64},{96,112},{112,96},{1... | collective-permute-start | bytes 393224 | tf_op jit(solution)/shard_map/ppermute | solution.py:260
  50.8 3.8 %collective-permute-done.10.refs_2_ = f32[512,128]{1,0:T(8,128)S(1)} collective-permute-done((f32[512,128]{1,0:T(8,128)S(1)}, f32[512,128]{1,0:T(8,128)S(1)}, u32[]{:S(2)}, u32[]{:S(2)}) %collective-permute-start.10) | collective-permute-done | bytes 262176 | tf_op jit(solution)/shard_map/ppermute | solution.py:247
  55.3 5.5 %collective-permute-start.22 = (f32[256,128]{1,0:T(8,128)S(1)}, f32[256,128]{1,0:T(8,128)S(1)}, u32[]{:S(2)}, u32[]{:S(2)}) collective-permute-start(f32[256,128]{1,0:T(8,128)S(1)} %get-tuple-element.49), channel_id=1, source_target_pairs={{0,80},{16,64},{32,112},{48,96},{64,16},{80,0},{96,48},{112,32},{1... | collective-permute-start | bytes 393224 | tf_op jit(solution)/shard_map/ppermute | solution.py:260
  60.9 2.2 %collective-permute-start.24 = (f32[256,128]{1,0:T(8,128)S(1)}, f32[256,128]{1,0:T(8,128)S(1)}, u32[]{:S(2)}, u32[]{:S(2)}) collective-permute-start(f32[256,128]{1,0:T(8,128)S(1)} %get-tuple-element.51), channel_id=1, source_target_pairs={{0,112},{16,96},{32,16},{48,0},{64,48},{80,32},{96,80},{112,64},{1... | collective-permute-start | bytes 393224 | tf_op jit(solution)/shard_map/ppermute | solution.py:260
  63.0 1.7 %collective-permute-start.18 = (f32[256,128]{1,0:T(8,128)S(1)}, f32[256,128]{1,0:T(8,128)S(1)}, u32[]{:S(2)}, u32[]{:S(2)}) collective-permute-start(f32[256,128]{1,0:T(8,128)S(1)} %get-tuple-element.44), channel_id=1, source_target_pairs={{0,16},{16,0},{1,17},{17,1},{2,18},{18,2},{3,19},{19,3},{4,20},{20... | collective-permute-start | bytes 393224 | tf_op jit(solution)/shard_map/ppermute | solution.py:242
  65.4 4.3 %collective-permute-done.23.refs_6_ = f32[256,128]{1,0:T(8,128)S(1)} collective-permute-done((f32[256,128]{1,0:T(8,128)S(1)}, f32[256,128]{1,0:T(8,128)S(1)}, u32[]{:S(2)}, u32[]{:S(2)}) %collective-permute-start.23) | collective-permute-done | bytes 131104 | tf_op jit(solution)/shard_map/ppermute | solution.py:260
  71.3 2.6 %collective-permute-start.28 = (f32[256,128]{1,0:T(8,128)S(1)}, f32[256,128]{1,0:T(8,128)S(1)}, u32[]{:S(2)}, u32[]{:S(2)}) collective-permute-start(f32[256,128]{1,0:T(8,128)S(1)} %get-tuple-element.53.refs_0_), channel_id=1, source_target_pairs={{0,16},{16,0},{1,17},{17,1},{2,18},{18,2},{3,19},{19,3},{4,20},{20... | collective-permute-start | bytes 393224 | tf_op jit(solution)/shard_map/ppermute | solution.py:242
  76.3 1.9 %collective-permute-start.27 = (f32[256,128]{1,0:T(8,128)S(1)}, f32[256,128]{1,0:T(8,128)S(1)}, u32[]{:S(2)}, u32[]{:S(2)}) collective-permute-start(f32[256,128]{1,0:T(8,128)S(1)} %get-tuple-element.53.refs_0_), channel_id=1, source_target_pairs={{0,96},{32,0},{64,32},{96,64},{1,97},{33,1},{65,33},{97,65},{2,98}... | collective-permute-start | bytes 393224 | tf_op jit(solution)/shard_map/ppermute | solution.py:247
  80.2 4.1 %collective-permute-done.25.refs_1_ = f32[256,128]{1,0:T(8,128)S(1)} collective-permute-done((f32[256,128]{1,0:T(8,128)S(1)}, f32[256,128]{1,0:T(8,128)S(1)}, u32[]{:S(2)}, u32[]{:S(2)}) %collective-permute-start.25) | collective-permute-done | bytes 131104 | tf_op jit(solution)/shard_map/ppermute | solution.py:247
  85.5 5.4 %all-to-all-start = ((f32[8,320,128]{2,1,0:T(8,128)}), f32[8,320,128]{2,1,0:T(8,128)S(1)}, u32[]{:S(2)}, u32[]{:S(2)}) async-start(f32[8,320,128]{2,1,0:T(8,128)} %copies.1.refs_8_), calls=%async_computation | async-start | bytes 2621440 | tf_op jit(solution)/shard_map/all_to_all | solution.py:264
  90.9 4.9 %backward0.1 = (f32[2048,128]{1,0:T(8,128)S(1)}, f32[2048,128]{1,0:T(8,128)}) custom-call(s32[256]{0:T(256)S(1)} %get-tuple-element.87.take, s32[256]{0:T(256)S(1)} %get-tuple-element.79.put, s32[1]{0:T(128)} %bitcast.9.count, f32[256,128,128]{2,1,0:T(8,128)} %bitcast.13, f32[256,128]{1,0:T(8,128)S(1)} %get-tuple-element.53.refs_0_, ...), custom_call_target="tpu_custom_call" | custom-call | tf_op jit(solution)/shard_map/backward0/pallas_call | solution.py:104
  95.9 12.8 %all-to-all-done.arrived = f32[8,320,128]{2,1,0:T(8,128)S(1)} async-done(((f32[8,320,128]{2,1,0:T(8,128)}), f32[8,320,128]{2,1,0:T(8,128)S(1)}, u32[]{:S(2)}, u32[]{:S(2)}) %all-to-all-start) | async-done | bytes 1310752 | tf_op jit(solution)/shard_map/all_to_all | solution.py:264
  108.7 2.4 %share0.1.refs_1_ = f32[8,320,128]{2,1,0:T(8,128)} custom-call(f32[2048,128]{1,0:T(8,128)S(1)} %get-tuple-element.56.mine, f32[2048,128]{1,0:T(8,128)} %collective-permute-done.33.other, f32[64,128]{1,0:T(8,128)S(1)} %get-tuple-element.58.piece), custom_call_target="tpu_custom_call" | custom-call | tf_op jit(solution)/shard_map/share0/pallas_call | solution.py:123
  111.2 7.4 %all-to-all-start.1 = ((f32[8,320,128]{2,1,0:T(8,128)}), f32[8,320,128]{2,1,0:T(8,128)S(1)}, u32[]{:S(2)}, u32[]{:S(2)}) async-start(f32[8,320,128]{2,1,0:T(8,128)} %share0.1.refs_1_), calls=%async_computation.1 | async-start | bytes 2621440 | tf_op jit(solution)/shard_map/all_to_all | solution.py:264
  118.6 4.0 %backward1.1 = (f32[2048,128]{1,0:T(8,128)S(1)}, f32[512,128]{1,0:T(8,128)S(1)}, f32[512,128]{1,0:T(8,128)S(1)}, f32[512,128]{1,0:T(8,128)S(1)}, f32[512,128]{1,0:T(8,128)S(1)}) custom-call(s32[256]{0:T(256)S(1)} %get-tuple-element.88.take, s32[256]{0:T(256)S(1)} %get-tuple-element.73.put, s32[1]{0:T(128)} %bitcast.10.count, f32[256,128,128]{2,1,0:T(8,128)} %bitcast.14, ...), custom_call_target="tpu_custom_call" | custom-call | tf_op jit(solution)/shard_map/backward1/pallas_call | solution.py:104
  126.2 2.0 %collective-permute-start.38 = (f32[512,128]{1,0:T(8,128)}, f32[512,128]{1,0:T(8,128)S(1)}, u32[]{:S(2)}, u32[]{:S(2)}) collective-permute-start(f32[512,128]{1,0:T(8,128)} %get-tuple-element.67), channel_id=1, source_target_pairs={{0,2},{2,4},{4,6},{6,0},{1,3},{3,5},{5,7},{7,1},{8,10},{10,12},{12... | collective-permute-start | bytes 786440 | tf_op jit(solution)/shard_map/ppermute | solution.py:247
  128.2 3.5 %collective-permute-start.39 = (f32[512,128]{1,0:T(8,128)}, f32[512,128]{1,0:T(8,128)S(1)}, u32[]{:S(2)}, u32[]{:S(2)}) collective-permute-start(f32[512,128]{1,0:T(8,128)} %get-tuple-element.68), channel_id=1, source_target_pairs={{0,4},{2,6},{4,0},{6,2},{1,5},{3,7},{5,1},{7,3},{8,12},{10,14},{12... | collective-permute-start | bytes 786440 | tf_op jit(solution)/shard_map/ppermute | solution.py:247
  134.0 5.7 %all-to-all-start.2 = ((f32[8,64,128]{2,1,0:T(8,128)}), f32[8,64,128]{2,1,0:T(8,128)S(1)}, u32[]{:S(2)}, u32[]{:S(2)}) async-start(f32[8,64,128]{2,1,0:T(8,128)} %broadcast_in_dim.13), calls=%async_computation.2 | async-start | bytes 524288 | tf_op jit(solution)/shard_map/all_to_all | solution.py:264
  139.6 4.5 %collective-permute-done.39.refs_2_ = f32[512,128]{1,0:T(8,128)S(1)} collective-permute-done((f32[512,128]{1,0:T(8,128)}, f32[512,128]{1,0:T(8,128)S(1)}, u32[]{:S(2)}, u32[]{:S(2)}) %collective-permute-start.39) | collective-permute-done | bytes 262176 | tf_op jit(solution)/shard_map/ppermute | solution.py:247
  144.1 4.4 %collective-permute-start.41 = (f32[256,128]{1,0:T(8,128)S(1)}, f32[256,128]{1,0:T(8,128)S(1)}, u32[]{:S(2)}, u32[]{:S(2)}) collective-permute-start(f32[256,128]{1,0:T(8,128)S(1)} %get-tuple-element.71), channel_id=1, source_target_pairs={{0,8},{8,0},{1,9},{9,1},{2,10},{10,2},{3,11},{11,3},{4,12},{12,4},... | collective-permute-start | bytes 393224 | tf_op jit(solution)/shard_map/ppermute | solution.py:242
  148.5 3.3 %collective-permute-done.41.refs_1_ = f32[256,128]{1,0:T(8,128)S(1)} collective-permute-done((f32[256,128]{1,0:T(8,128)S(1)}, f32[256,128]{1,0:T(8,128)S(1)}, u32[]{:S(2)}, u32[]{:S(2)}) %collective-permute-start.41) | collective-permute-done | bytes 131104 | tf_op jit(solution)/shard_map/ppermute | solution.py:242
  (87 shorter events, 30.8 us)
Async XLA Ops:
  1.6 8.2 %collective-permute-start.3 = (f32[256,128]{1,0:T(8,128)S(1)}, f32[256,128]{1,0:T(8,128)S(1)}, u32[]{:S(2)}, u32[]{:S(2)}) collective-permute-start(f32[256,128]{1,0:T(8,128)S(1)} %get-tuple-element.78.refs_0_), channel_id=1, source_target_pairs={{0,8},{8,0},{1,9},{9,1},{2,10},{10,2},{3,11},{11,3},{4,12},{12,4},... | collective-permute-start | bytes 393224 | tf_op jit(solution)/shard_map/ppermute | solution.py:242
  3.3 9.2 %collective-permute-start = (f32[256,128]{1,0:T(8,128)S(1)}, f32[256,128]{1,0:T(8,128)S(1)}, u32[]{:S(2)}, u32[]{:S(2)}) collective-permute-start(f32[256,128]{1,0:T(8,128)S(1)} %get-tuple-element.78.refs_0_), channel_id=1, source_target_pairs={{0,2},{2,4},{4,6},{6,0},{1,3},{3,5},{5,7},{7,1},{8,10},{10,12},{12... | collective-permute-start | bytes 393224 | tf_op jit(solution)/shard_map/ppermute | solution.py:247
  5.2 10.8 %collective-permute-start.1 = (f32[256,128]{1,0:T(8,128)S(1)}, f32[256,128]{1,0:T(8,128)S(1)}, u32[]{:S(2)}, u32[]{:S(2)}) collective-permute-start(f32[256,128]{1,0:T(8,128)S(1)} %get-tuple-element.78.refs_0_), channel_id=1, source_target_pairs={{0,4},{2,6},{4,0},{6,2},{1,5},{3,7},{5,1},{7,3},{8,12},{10,14},{12... | collective-permute-start | bytes 393224 | tf_op jit(solution)/shard_map/ppermute | solution.py:247
  8.8 7.8 %collective-permute-start.2 = (f32[256,128]{1,0:T(8,128)S(1)}, f32[256,128]{1,0:T(8,128)S(1)}, u32[]{:S(2)}, u32[]{:S(2)}) collective-permute-start(f32[256,128]{1,0:T(8,128)S(1)} %get-tuple-element.78.refs_0_), channel_id=1, source_target_pairs={{0,6},{2,0},{4,2},{6,4},{1,7},{3,1},{5,3},{7,5},{8,14},{10,8},{12,... | collective-permute-start | bytes 393224 | tf_op jit(solution)/shard_map/ppermute | solution.py:247
  9.8 8.1 %collective-permute-start.4 = (f32[256,128]{1,0:T(8,128)S(1)}, f32[256,128]{1,0:T(8,128)S(1)}, u32[]{:S(2)}, u32[]{:S(2)}) collective-permute-start(f32[256,128]{1,0:T(8,128)S(1)} %collective-permute-done.3.refs_0_), channel_id=1, source_target_pairs={{0,2},{2,4},{4,6},{6,0},{1,3},{3,5},{5,7},{7,1},{8,10},{10,12},{12... | collective-permute-start | bytes 393224 | tf_op jit(solution)/shard_map/ppermute | solution.py:247
  10.8 9.3 %collective-permute-start.5 = (f32[256,128]{1,0:T(8,128)S(1)}, f32[256,128]{1,0:T(8,128)S(1)}, u32[]{:S(2)}, u32[]{:S(2)}) collective-permute-start(f32[256,128]{1,0:T(8,128)S(1)} %collective-permute-done.3.refs_0_), channel_id=1, source_target_pairs={{0,4},{2,6},{4,0},{6,2},{1,5},{3,7},{5,1},{7,3},{8,12},{10,14},{12... | collective-permute-start | bytes 393224 | tf_op jit(solution)/shard_map/ppermute | solution.py:247
  16.6 9.4 %collective-permute-start.7 = (f32[1024,128]{1,0:T(8,128)S(1)}, f32[1024,128]{1,0:T(8,128)S(1)}, u32[]{:S(2)}, u32[]{:S(2)}) collective-permute-start(f32[1024,128]{1,0:T(8,128)S(1)} %join0.1.refs_0_), channel_id=1, source_target_pairs={{0,1},{1,0},{2,3},{3,2},{4,5},{5,4},{6,7},{7,6},{8,9},{9,8},{10,11... | collective-permute-start | bytes 1572872 | tf_op jit(solution)/shard_map/ppermute | solution.py:242
  21.0 10.1 %collective-permute-start.13 = (f32[512,128]{1,0:T(8,128)S(1)}, f32[512,128]{1,0:T(8,128)S(1)}, u32[]{:S(2)}, u32[]{:S(2)}) collective-permute-start(f32[512,128]{1,0:T(8,128)S(1)} %pair1.1.refs_0_), channel_id=1, source_target_pairs={{0,2},{2,4},{4,6},{6,0},{1,3},{3,5},{5,7},{7,1},{8,10},{10,12},{12... | collective-permute-start | bytes 786440 | tf_op jit(solution)/shard_map/ppermute | solution.py:247
  22.2 14.7 %collective-permute-start.14 = (f32[512,128]{1,0:T(8,128)S(1)}, f32[512,128]{1,0:T(8,128)S(1)}, u32[]{:S(2)}, u32[]{:S(2)}) collective-permute-start(f32[512,128]{1,0:T(8,128)S(1)} %pair1.1.refs_0_), channel_id=1, source_target_pairs={{0,4},{2,6},{4,0},{6,2},{1,5},{3,7},{5,1},{7,3},{8,12},{10,14},{12... | collective-permute-start | bytes 786440 | tf_op jit(solution)/shard_map/ppermute | solution.py:247
  24.6 12.6 %collective-permute-start.15 = (f32[512,128]{1,0:T(8,128)S(1)}, f32[512,128]{1,0:T(8,128)S(1)}, u32[]{:S(2)}, u32[]{:S(2)}) collective-permute-start(f32[512,128]{1,0:T(8,128)S(1)} %pair1.1.refs_0_), channel_id=1, source_target_pairs={{0,6},{2,0},{4,2},{6,4},{1,7},{3,1},{5,3},{7,5},{8,14},{10,8},{12,... | collective-permute-start | bytes 786440 | tf_op jit(solution)/shard_map/ppermute | solution.py:247
  37.4 13.2 %collective-permute-start.9 = (f32[512,128]{1,0:T(8,128)S(1)}, f32[512,128]{1,0:T(8,128)S(1)}, u32[]{:S(2)}, u32[]{:S(2)}) collective-permute-start(f32[512,128]{1,0:T(8,128)S(1)} %get-tuple-element.39), channel_id=1, source_target_pairs={{0,32},{32,64},{64,96},{96,0},{1,33},{33,65},{65,97},{97,1},{2,34}... | collective-permute-start | bytes 786440 | tf_op jit(solution)/shard_map/ppermute | solution.py:247
  39.0 15.6 %collective-permute-start.10 = (f32[512,128]{1,0:T(8,128)S(1)}, f32[512,128]{1,0:T(8,128)S(1)}, u32[]{:S(2)}, u32[]{:S(2)}) collective-permute-start(f32[512,128]{1,0:T(8,128)S(1)} %get-tuple-element.40), channel_id=1, source_target_pairs={{0,64},{32,96},{64,0},{96,32},{1,65},{33,97},{65,1},{97,33},{2,66}... | collective-permute-start | bytes 786440 | tf_op jit(solution)/shard_map/ppermute | solution.py:247
  41.9 13.4 %collective-permute-start.11 = (f32[512,128]{1,0:T(8,128)S(1)}, f32[512,128]{1,0:T(8,128)S(1)}, u32[]{:S(2)}, u32[]{:S(2)}) collective-permute-start(f32[512,128]{1,0:T(8,128)S(1)} %get-tuple-element.41), channel_id=1, source_target_pairs={{0,96},{32,0},{64,32},{96,64},{1,97},{33,1},{65,33},{97,65},{2,98}... | collective-permute-start | bytes 786440 | tf_op jit(solution)/shard_map/ppermute | solution.py:247
  47.1 13.7 %collective-permute-start.17 = (f32[256,128]{1,0:T(8,128)S(1)}, f32[256,128]{1,0:T(8,128)S(1)}, u32[]{:S(2)}, u32[]{:S(2)}) collective-permute-start(f32[256,128]{1,0:T(8,128)S(1)} %get-tuple-element.42), channel_id=1, source_target_pairs={{0,16},{16,0},{32,48},{48,32},{64,80},{80,64},{96,112},{112,96},{1... | collective-permute-start | bytes 393224 | tf_op jit(solution)/shard_map/ppermute | solution.py:260
  49.9 11.0 %collective-permute-start.19 = (f32[256,128]{1,0:T(8,128)S(1)}, f32[256,128]{1,0:T(8,128)S(1)}, u32[]{:S(2)}, u32[]{:S(2)}) collective-permute-start(f32[256,128]{1,0:T(8,128)S(1)} %get-tuple-element.46), channel_id=1, source_target_pairs={{0,32},{16,48},{32,64},{48,80},{64,96},{80,112},{96,0},{112,16},{1... | collective-permute-start | bytes 393224 | tf_op jit(solution)/shard_map/ppermute | solution.py:260
  50.6 12.5 %collective-permute-start.20 = (f32[256,128]{1,0:T(8,128)S(1)}, f32[256,128]{1,0:T(8,128)S(1)}, u32[]{:S(2)}, u32[]{:S(2)}) collective-permute-start(f32[256,128]{1,0:T(8,128)S(1)} %get-tuple-element.47), channel_id=1, source_target_pairs={{0,48},{16,32},{32,80},{48,64},{64,112},{80,96},{96,16},{112,0},{1... | collective-permute-start | bytes 393224 | tf_op jit(solution)/shard_map/ppermute | solution.py:260
  54.6 10.8 %collective-permute-start.21 = (f32[256,128]{1,0:T(8,128)S(1)}, f32[256,128]{1,0:T(8,128)S(1)}, u32[]{:S(2)}, u32[]{:S(2)}) collective-permute-start(f32[256,128]{1,0:T(8,128)S(1)} %get-tuple-element.48), channel_id=1, source_target_pairs={{0,64},{16,80},{32,96},{48,112},{64,0},{80,16},{96,32},{112,48},{1... | collective-permute-start | bytes 393224 | tf_op jit(solution)/shard_map/ppermute | solution.py:260
  55.3 10.1 %collective-permute-start.22 = (f32[256,128]{1,0:T(8,128)S(1)}, f32[256,128]{1,0:T(8,128)S(1)}, u32[]{:S(2)}, u32[]{:S(2)}) collective-permute-start(f32[256,128]{1,0:T(8,128)S(1)} %get-tuple-element.49), channel_id=1, source_target_pairs={{0,80},{16,64},{32,112},{48,96},{64,16},{80,0},{96,48},{112,32},{1... | collective-permute-start | bytes 393224 | tf_op jit(solution)/shard_map/ppermute | solution.py:260
  60.8 8.9 %collective-permute-start.23 = (f32[256,128]{1,0:T(8,128)S(1)}, f32[256,128]{1,0:T(8,128)S(1)}, u32[]{:S(2)}, u32[]{:S(2)}) collective-permute-start(f32[256,128]{1,0:T(8,128)S(1)} %get-tuple-element.50), channel_id=1, source_target_pairs={{0,96},{16,112},{32,0},{48,16},{64,32},{80,48},{96,64},{112,80},{1... | collective-permute-start | bytes 393224 | tf_op jit(solution)/shard_map/ppermute | solution.py:260
  60.9 8.9 %collective-permute-start.24 = (f32[256,128]{1,0:T(8,128)S(1)}, f32[256,128]{1,0:T(8,128)S(1)}, u32[]{:S(2)}, u32[]{:S(2)}) collective-permute-start(f32[256,128]{1,0:T(8,128)S(1)} %get-tuple-element.51), channel_id=1, source_target_pairs={{0,112},{16,96},{32,16},{48,0},{64,48},{80,32},{96,80},{112,64},{1... | collective-permute-start | bytes 393224 | tf_op jit(solution)/shard_map/ppermute | solution.py:260
  71.3 13.0 %collective-permute-start.32 = (f32[8,64,128]{2,1,0:T(8,128)S(1)}, f32[8,64,128]{2,1,0:T(8,128)S(1)}, u32[]{:S(2)}, u32[]{:S(2)}) collective-permute-start(f32[8,64,128]{2,1,0:T(8,128)S(1)} %get-tuple-element.55.refs_0_), channel_id=1, source_target_pairs={{0,1},{1,0},{2,3},{3,2},{4,5},{5,4},{6,7},{7,6},{8,9},{9,8},{10,11... | collective-permute-start | bytes 786440 | tf_op jit(solution)/shard_map/ppermute | solution.py:242
  73.9 10.4 %collective-permute-start.25 = (f32[256,128]{1,0:T(8,128)S(1)}, f32[256,128]{1,0:T(8,128)S(1)}, u32[]{:S(2)}, u32[]{:S(2)}) collective-permute-start(f32[256,128]{1,0:T(8,128)S(1)} %get-tuple-element.53.refs_0_), channel_id=1, source_target_pairs={{0,32},{32,64},{64,96},{96,0},{1,33},{33,65},{65,97},{97,1},{2,34}... | collective-permute-start | bytes 393224 | tf_op jit(solution)/shard_map/ppermute | solution.py:247
  75.1 15.7 %collective-permute-start.26 = (f32[256,128]{1,0:T(8,128)S(1)}, f32[256,128]{1,0:T(8,128)S(1)}, u32[]{:S(2)}, u32[]{:S(2)}) collective-permute-start(f32[256,128]{1,0:T(8,128)S(1)} %get-tuple-element.53.refs_0_), channel_id=1, source_target_pairs={{0,64},{32,96},{64,0},{96,32},{1,65},{33,97},{65,1},{97,33},{2,66}... | collective-permute-start | bytes 393224 | tf_op jit(solution)/shard_map/ppermute | solution.py:247
  76.3 14.6 %collective-permute-start.27 = (f32[256,128]{1,0:T(8,128)S(1)}, f32[256,128]{1,0:T(8,128)S(1)}, u32[]{:S(2)}, u32[]{:S(2)}) collective-permute-start(f32[256,128]{1,0:T(8,128)S(1)} %get-tuple-element.53.refs_0_), channel_id=1, source_target_pairs={{0,96},{32,0},{64,32},{96,64},{1,97},{33,1},{65,33},{97,65},{2,98}... | collective-permute-start | bytes 393224 | tf_op jit(solution)/shard_map/ppermute | solution.py:247
  78.7 12.1 %collective-permute-start.29 = (f32[256,128]{1,0:T(8,128)S(1)}, f32[256,128]{1,0:T(8,128)S(1)}, u32[]{:S(2)}, u32[]{:S(2)}) collective-permute-start(f32[256,128]{1,0:T(8,128)S(1)} %collective-permute-done.28.refs_2_.refs_4_), channel_id=1, source_target_pairs={{0,32},{32,64},{64,96},{96,0},{1,33},{33,65},{65,97},{97,1},{2,34}... | collective-permute-start | bytes 393224 | tf_op jit(solution)/shard_map/ppermute | solution.py:247
  85.5 23.2 %all-to-all-start = ((f32[8,320,128]{2,1,0:T(8,128)}), f32[8,320,128]{2,1,0:T(8,128)S(1)}, u32[]{:S(2)}, u32[]{:S(2)}) async-start(f32[8,320,128]{2,1,0:T(8,128)} %copies.1.refs_8_), calls=%async_computation | async-start | bytes 2621440 | tf_op jit(solution)/shard_map/all_to_all | solution.py:264
  95.8 12.9 %collective-permute-start.33 = (f32[2048,128]{1,0:T(8,128)}, f32[2048,128]{1,0:T(8,128)}, u32[]{:S(2)}, u32[]{:S(2)}) collective-permute-start(f32[2048,128]{1,0:T(8,128)} %get-tuple-element.57), channel_id=1, source_target_pairs={{0,1},{1,0},{2,3},{3,2},{4,5},{5,4},{6,7},{7,6},{8,9},{9,8},{10,11... | collective-permute-start | bytes 3145736 | tf_op jit(solution)/shard_map/ppermute | solution.py:242
  111.2 22.0 %all-to-all-start.1 = ((f32[8,320,128]{2,1,0:T(8,128)}), f32[8,320,128]{2,1,0:T(8,128)S(1)}, u32[]{:S(2)}, u32[]{:S(2)}) async-start(f32[8,320,128]{2,1,0:T(8,128)} %share0.1.refs_1_), calls=%async_computation.1 | async-start | bytes 2621440 | tf_op jit(solution)/shard_map/all_to_all | solution.py:264
  126.2 13.4 %collective-permute-start.38 = (f32[512,128]{1,0:T(8,128)}, f32[512,128]{1,0:T(8,128)S(1)}, u32[]{:S(2)}, u32[]{:S(2)}) collective-permute-start(f32[512,128]{1,0:T(8,128)} %get-tuple-element.67), channel_id=1, source_target_pairs={{0,2},{2,4},{4,6},{6,0},{1,3},{3,5},{5,7},{7,1},{8,10},{10,12},{12... | collective-permute-start | bytes 786440 | tf_op jit(solution)/shard_map/ppermute | solution.py:247
  128.2 15.8 %collective-permute-start.39 = (f32[512,128]{1,0:T(8,128)}, f32[512,128]{1,0:T(8,128)S(1)}, u32[]{:S(2)}, u32[]{:S(2)}) collective-permute-start(f32[512,128]{1,0:T(8,128)} %get-tuple-element.68), channel_id=1, source_target_pairs={{0,4},{2,6},{4,0},{6,2},{1,5},{3,7},{5,1},{7,3},{8,12},{10,14},{12... | collective-permute-start | bytes 786440 | tf_op jit(solution)/shard_map/ppermute | solution.py:247
  131.7 12.4 %collective-permute-start.40 = (f32[512,128]{1,0:T(8,128)}, f32[512,128]{1,0:T(8,128)S(1)}, u32[]{:S(2)}, u32[]{:S(2)}) collective-permute-start(f32[512,128]{1,0:T(8,128)} %get-tuple-element.69), channel_id=1, source_target_pairs={{0,6},{2,0},{4,2},{6,4},{1,7},{3,1},{5,3},{7,5},{8,14},{10,8},{12,... | collective-permute-start | bytes 786440 | tf_op jit(solution)/shard_map/ppermute | solution.py:247
  134.0 18.6 %all-to-all-start.2 = ((f32[8,64,128]{2,1,0:T(8,128)}), f32[8,64,128]{2,1,0:T(8,128)S(1)}, u32[]{:S(2)}, u32[]{:S(2)}) async-start(f32[8,64,128]{2,1,0:T(8,128)} %broadcast_in_dim.13), calls=%async_computation.2 | async-start | bytes 524288 | tf_op jit(solution)/shard_map/all_to_all | solution.py:264
  (16 other events, 133.3 us)

commit v7 on v6

--- a/solution.py
+++ b/solution.py
@@ -62,32 +62,22 @@
         lax.fori_loop(0, rows, pair, 0)
         first += rows
 
-    def block(index, masked):
+    def block(index, carry):
+        fetch(index).wait()
         for offset in range(BLOCK):
             slot = index * BLOCK + offset
-            tile = held[slot]
-            if masked:
-                tile = jnp.where(slot < count[0], tile, 0.0)
-            high, low = split(tile.T if flipped else tile)
+            high, low = split(held[slot].T if flipped else held[slot])
+            high = jnp.where(slot < count[0], high, jnp.zeros_like(high))
+            low = jnp.where(slot < count[0], low, jnp.zeros_like(low))
             both = jnp.dot(
                 jnp.concatenate([high, low], axis=1),
                 paired[take[slot]],
                 preferred_element_type=jnp.float32,
             )
             total[put[slot]] += both[:, :EDGE] + both[:, EDGE:]
-
-    def whole_block(index, carry):
-        fetch(index).wait()
-        block(index, False)
         return carry
 
-    blocks = count[0] // BLOCK
-    lax.fori_loop(0, blocks, whole_block, 0)
-
-    @pl.when(blocks * BLOCK < count[0])
-    def _():
-        fetch(blocks).wait()
-        block(blocks, True)
+    lax.fori_loop(0, pl.cdiv(count[0], BLOCK), block, 0)
 
     place = 0
     for out in outs:
@@ -388,8 +378,6 @@
         grad1,
         weight_part,
         swap(weight_part, "core"),
-        other,
-        skipped=1,
         name="copies",
     )
     arrived = exchange(copied, ROW_AXES)

time: 151 us -> 149 us (0.987); the launches traced: 153 us -> 148 us
  starting transfers between devices: 76.7 us -> 68.5 us
  waiting for transfers between devices: 49.3 us -> 52.4 us
    all_to_all x3, starting transfers between devices: 18.4 us -> 13.9 us  [exchange(): return lax.all_to_all(value, axes, 0, 0, tiled=True)]
    ppermute x14, starting transfers between devices: 12.4 us -> 9.53 us  [swap(): return lax.ppermute(value, axis, [(0, 1), (1, 0)])]
    all_to_all x3, waiting for transfers between devices: 12.8 us -> 15.2 us  [exchange(): return lax.all_to_all(value, axes, 0, 0, tiled=True)]
  transfers between devices with their start and end apart: 45 -> 45, of which waited for: 19 -> 20; matrix products, arithmetic and copies ran while one was open for 1% -> 1% of each run, Pallas kernels for 13% -> 13%
where the time goes in v7:
time: 149 us; the launch traced here: 148 us
  starting transfers between devices  68.5 us (46%)
  waiting for transfers between devices  52.4 us (35%)
  Pallas kernels  23.9 us (16%)
  local copies, waits for them, and re-layouts  1.74 us (1%)
  between operations  1.57 us (1%)
    ppermute x21, starting transfers between devices, ring_send(): lax.ppermute(value, axis, [(place, (place + step) % size) for place in ra...  33.1 us
    ppermute x21, waiting for transfers between devices, ring_send(): lax.ppermute(value, axis, [(place, (place + step) % size) for place in ra...  26 us
    pallas_call x4, Pallas kernels, spread(): pl.pallas_call(functools.partial(spread_body, flipped, len(sources), len(...  16.4 us
    all_to_all x3, waiting for transfers between devices, exchange(): return lax.all_to_all(value, axes, 0, 0, tiled=True)  15.2 us
    all_to_all x3, starting transfers between devices, exchange(): return lax.all_to_all(value, axes, 0, 0, tiled=True)  13.9 us
    ppermute x7, starting transfers between devices, offset_send(): return lax.ppermute(value, axes, hops)  12 us
    ppermute x14, starting transfers between devices, swap(): return lax.ppermute(value, axis, [(0, 1), (1, 0)])  9.53 us
    pallas_call x14, Pallas kernels, whole_call(): pl.pallas_call(kernel, in_specs=[here] * (len(args) - skipped) + [there]...  7.5 us
  transfers between devices with their start and end apart: 45, of which 20 were waited for; matrix products, arithmetic and copies ran while one was open for 1% of the time, Pallas kernels for 13%

profile of v7, /device:TPU:0, one launch (start us, length us, event | category | flops | bytes accessed | tf_op | source)
XLA Modules:
  0.0 148.2 jit_solution(16114136670132637839)
XLA Ops:
  1.6 1.7 %collective-permute-start.3 = (f32[256,128]{1,0:T(8,128)S(1)}, f32[256,128]{1,0:T(8,128)S(1)}, u32[]{:S(2)}, u32[]{:S(2)}) collective-permute-start(f32[256,128]{1,0:T(8,128)S(1)} %get-tuple-element.78.refs_0_), channel_id=1, source_target_pairs={{0,8},{8,0},{1,9},{9,1},{2,10},{10,2},{3,11},{11,3},{4,12},{12,4},... | collective-permute-start | bytes 393224 | tf_op jit(solution)/shard_map/ppermute | solution.py:232
  3.3 1.9 %collective-permute-start = (f32[256,128]{1,0:T(8,128)S(1)}, f32[256,128]{1,0:T(8,128)S(1)}, u32[]{:S(2)}, u32[]{:S(2)}) collective-permute-start(f32[256,128]{1,0:T(8,128)S(1)} %get-tuple-element.78.refs_0_), channel_id=1, source_target_pairs={{0,2},{2,4},{4,6},{6,0},{1,3},{3,5},{5,7},{7,1},{8,10},{10,12},{12... | collective-permute-start | bytes 393224 | tf_op jit(solution)/shard_map/ppermute | solution.py:237
  5.2 3.6 %collective-permute-start.1 = (f32[256,128]{1,0:T(8,128)S(1)}, f32[256,128]{1,0:T(8,128)S(1)}, u32[]{:S(2)}, u32[]{:S(2)}) collective-permute-start(f32[256,128]{1,0:T(8,128)S(1)} %get-tuple-element.78.refs_0_), channel_id=1, source_target_pairs={{0,4},{2,6},{4,0},{6,2},{1,5},{3,7},{5,1},{7,3},{8,12},{10,14},{12... | collective-permute-start | bytes 393224 | tf_op jit(solution)/shard_map/ppermute | solution.py:237
  10.8 1.7 %collective-permute-start.5 = (f32[256,128]{1,0:T(8,128)S(1)}, f32[256,128]{1,0:T(8,128)S(1)}, u32[]{:S(2)}, u32[]{:S(2)}) collective-permute-start(f32[256,128]{1,0:T(8,128)S(1)} %collective-permute-done.3.refs_0_), channel_id=1, source_target_pairs={{0,4},{2,6},{4,0},{6,2},{1,5},{3,7},{5,1},{7,3},{8,12},{10,14},{12... | collective-permute-start | bytes 393224 | tf_op jit(solution)/shard_map/ppermute | solution.py:237
  13.7 2.3 %collective-permute-done.1.refs_2_ = f32[256,128]{1,0:T(8,128)S(1)} collective-permute-done((f32[256,128]{1,0:T(8,128)S(1)}, f32[256,128]{1,0:T(8,128)S(1)}, u32[]{:S(2)}, u32[]{:S(2)}) %collective-permute-start.1) | collective-permute-done | bytes 131104 | tf_op jit(solution)/shard_map/ppermute | solution.py:237
  17.9 2.2 %collective-permute-done.5.refs_2_.refs_1_ = f32[256,128]{1,0:T(8,128)S(1)} collective-permute-done((f32[256,128]{1,0:T(8,128)S(1)}, f32[256,128]{1,0:T(8,128)S(1)}, u32[]{:S(2)}, u32[]{:S(2)}) %collective-permute-start.5) | collective-permute-done | bytes 131104 | tf_op jit(solution)/shard_map/ppermute | solution.py:237
  22.2 2.4 %collective-permute-start.14 = (f32[512,128]{1,0:T(8,128)S(1)}, f32[512,128]{1,0:T(8,128)S(1)}, u32[]{:S(2)}, u32[]{:S(2)}) collective-permute-start(f32[512,128]{1,0:T(8,128)S(1)} %pair1.1.refs_0_), channel_id=1, source_target_pairs={{0,4},{2,6},{4,0},{6,2},{1,5},{3,7},{5,1},{7,3},{8,12},{10,14},{12... | collective-permute-start | bytes 786440 | tf_op jit(solution)/shard_map/ppermute | solution.py:237
  26.0 3.8 %forward0.1 = (f32[512,128]{1,0:T(8,128)S(1)}, f32[512,128]{1,0:T(8,128)S(1)}, f32[512,128]{1,0:T(8,128)S(1)}, f32[512,128]{1,0:T(8,128)S(1)}) custom-call(s32[256]{0:T(256)S(1)} %get-tuple-element.80.take, s32[256]{0:T(256)S(1)} %get-tuple-element.86.put, s32[1]{0:T(128)} %bitcast.7.count, f32[256,128,128]{2,1,0:T(8,128)} %bitcast.11, ...), custom_call_target="tpu_custom_call" | custom-call | tf_op jit(solution)/shard_map/forward0/pallas_call | solution.py:94
  31.1 5.8 %collective-permute-done.14.refs_2_ = f32[512,128]{1,0:T(8,128)S(1)} collective-permute-done((f32[512,128]{1,0:T(8,128)S(1)}, f32[512,128]{1,0:T(8,128)S(1)}, u32[]{:S(2)}, u32[]{:S(2)}) %collective-permute-start.14) | collective-permute-done | bytes 262176 | tf_op jit(solution)/shard_map/ppermute | solution.py:237
  39.0 2.9 %collective-permute-start.10 = (f32[512,128]{1,0:T(8,128)S(1)}, f32[512,128]{1,0:T(8,128)S(1)}, u32[]{:S(2)}, u32[]{:S(2)}) collective-permute-start(f32[512,128]{1,0:T(8,128)S(1)} %get-tuple-element.40), channel_id=1, source_target_pairs={{0,64},{32,96},{64,0},{96,32},{1,65},{33,97},{65,1},{97,33},{2,66}... | collective-permute-start | bytes 786440 | tf_op jit(solution)/shard_map/ppermute | solution.py:237
  43.3 3.8 %forward1.1 = (f32[256,128]{1,0:T(8,128)S(1)}, f32[256,128]{1,0:T(8,128)S(1)}, f32[256,128]{1,0:T(8,128)S(1)}, f32[256,128]{1,0:T(8,128)S(1)}, f32[256,128]{1,0:...) custom-call(s32[256]{0:T(256)S(1)} %get-tuple-element.80.take, ...), custom_call_target="tpu_custom_call" | custom-call | tf_op jit(solution)/shard_map/forward1/pallas_call | solution.py:94
  47.1 2.8 %collective-permute-start.17 = (f32[256,128]{1,0:T(8,128)S(1)}, f32[256,128]{1,0:T(8,128)S(1)}, u32[]{:S(2)}, u32[]{:S(2)}) collective-permute-start(f32[256,128]{1,0:T(8,128)S(1)} %get-tuple-element.42), channel_id=1, source_target_pairs={{0,16},{16,0},{32,48},{48,32},{64,80},{80,64},{96,112},{112,96},{1... | collective-permute-start | bytes 393224 | tf_op jit(solution)/shard_map/ppermute | solution.py:250
  50.8 3.8 %collective-permute-done.10.refs_2_ = f32[512,128]{1,0:T(8,128)S(1)} collective-permute-done((f32[512,128]{1,0:T(8,128)S(1)}, f32[512,128]{1,0:T(8,128)S(1)}, u32[]{:S(2)}, u32[]{:S(2)}) %collective-permute-start.10) | collective-permute-done | bytes 262176 | tf_op jit(solution)/shard_map/ppermute | solution.py:237
  55.3 5.5 %collective-permute-start.22 = (f32[256,128]{1,0:T(8,128)S(1)}, f32[256,128]{1,0:T(8,128)S(1)}, u32[]{:S(2)}, u32[]{:S(2)}) collective-permute-start(f32[256,128]{1,0:T(8,128)S(1)} %get-tuple-element.49), channel_id=1, source_target_pairs={{0,80},{16,64},{32,112},{48,96},{64,16},{80,0},{96,48},{112,32},{1... | collective-permute-start | bytes 393224 | tf_op jit(solution)/shard_map/ppermute | solution.py:250
  60.9 2.2 %collective-permute-start.24 = (f32[256,128]{1,0:T(8,128)S(1)}, f32[256,128]{1,0:T(8,128)S(1)}, u32[]{:S(2)}, u32[]{:S(2)}) collective-permute-start(f32[256,128]{1,0:T(8,128)S(1)} %get-tuple-element.51), channel_id=1, source_target_pairs={{0,112},{16,96},{32,16},{48,0},{64,48},{80,32},{96,80},{112,64},{1... | collective-permute-start | bytes 393224 | tf_op jit(solution)/shard_map/ppermute | solution.py:250
  63.0 1.7 %collective-permute-start.18 = (f32[256,128]{1,0:T(8,128)S(1)}, f32[256,128]{1,0:T(8,128)S(1)}, u32[]{:S(2)}, u32[]{:S(2)}) collective-permute-start(f32[256,128]{1,0:T(8,128)S(1)} %get-tuple-element.44), channel_id=1, source_target_pairs={{0,16},{16,0},{1,17},{17,1},{2,18},{18,2},{3,19},{19,3},{4,20},{20... | collective-permute-start | bytes 393224 | tf_op jit(solution)/shard_map/ppermute | solution.py:232
  65.4 4.3 %collective-permute-done.23.refs_6_ = f32[256,128]{1,0:T(8,128)S(1)} collective-permute-done((f32[256,128]{1,0:T(8,128)S(1)}, f32[256,128]{1,0:T(8,128)S(1)}, u32[]{:S(2)}, u32[]{:S(2)}) %collective-permute-start.23) | collective-permute-done | bytes 131104 | tf_op jit(solution)/shard_map/ppermute | solution.py:250
  71.3 2.6 %collective-permute-start.28 = (f32[256,128]{1,0:T(8,128)S(1)}, f32[256,128]{1,0:T(8,128)S(1)}, u32[]{:S(2)}, u32[]{:S(2)}) collective-permute-start(f32[256,128]{1,0:T(8,128)S(1)} %get-tuple-element.53.refs_0_), channel_id=1, source_target_pairs={{0,16},{16,0},{1,17},{17,1},{2,18},{18,2},{3,19},{19,3},{4,20},{20... | collective-permute-start | bytes 393224 | tf_op jit(solution)/shard_map/ppermute | solution.py:232
  76.3 1.9 %collective-permute-start.27 = (f32[256,128]{1,0:T(8,128)S(1)}, f32[256,128]{1,0:T(8,128)S(1)}, u32[]{:S(2)}, u32[]{:S(2)}) collective-permute-start(f32[256,128]{1,0:T(8,128)S(1)} %get-tuple-element.53.refs_0_), channel_id=1, source_target_pairs={{0,96},{32,0},{64,32},{96,64},{1,97},{33,1},{65,33},{97,65},{2,98}... | collective-permute-start | bytes 393224 | tf_op jit(solution)/shard_map/ppermute | solution.py:237
  80.2 4.1 %collective-permute-done.25.refs_1_ = f32[256,128]{1,0:T(8,128)S(1)} collective-permute-done((f32[256,128]{1,0:T(8,128)S(1)}, f32[256,128]{1,0:T(8,128)S(1)}, u32[]{:S(2)}, u32[]{:S(2)}) %collective-permute-start.25) | collective-permute-done | bytes 131104 | tf_op jit(solution)/shard_map/ppermute | solution.py:237
  85.5 5.4 %all-to-all-start = ((f32[8,320,128]{2,1,0:T(8,128)}), f32[8,320,128]{2,1,0:T(8,128)S(1)}, u32[]{:S(2)}, u32[]{:S(2)}) async-start(f32[8,320,128]{2,1,0:T(8,128)} %copies.1.refs_8_), calls=%async_computation | async-start | bytes 2621440 | tf_op jit(solution)/shard_map/all_to_all | solution.py:254
  90.9 4.9 %backward0.1 = (f32[2048,128]{1,0:T(8,128)S(1)}, f32[2048,128]{1,0:T(8,128)}) custom-call(s32[256]{0:T(256)S(1)} %get-tuple-element.87.take, s32[256]{0:T(256)S(1)} %get-tuple-element.79.put, s32[1]{0:T(128)} %bitcast.9.count, f32[256,128,128]{2,1,0:T(8,128)} %bitcast.13, f32[256,128]{1,0:T(8,128)S(1)} %get-tuple-element.53.refs_0_, ...), custom_call_target="tpu_custom_call" | custom-call | tf_op jit(solution)/shard_map/backward0/pallas_call | solution.py:94
  95.9 12.8 %all-to-all-done.arrived = f32[8,320,128]{2,1,0:T(8,128)S(1)} async-done(((f32[8,320,128]{2,1,0:T(8,128)}), f32[8,320,128]{2,1,0:T(8,128)S(1)}, u32[]{:S(2)}, u32[]{:S(2)}) %all-to-all-start) | async-done | bytes 1310752 | tf_op jit(solution)/shard_map/all_to_all | solution.py:254
  108.7 2.4 %share0.1.refs_1_ = f32[8,320,128]{2,1,0:T(8,128)} custom-call(f32[2048,128]{1,0:T(8,128)S(1)} %get-tuple-element.56.mine, f32[2048,128]{1,0:T(8,128)} %collective-permute-done.33.other, f32[64,128]{1,0:T(8,128)S(1)} %get-tuple-element.58.piece), custom_call_target="tpu_custom_call" | custom-call | tf_op jit(solution)/shard_map/share0/pallas_call | solution.py:113
  111.2 3.6 %all-to-all-start.1 = ((f32[8,320,128]{2,1,0:T(8,128)}), f32[8,320,128]{2,1,0:T(8,128)S(1)}, u32[]{:S(2)}, u32[]{:S(2)}) async-start(f32[8,320,128]{2,1,0:T(8,128)} %share0.1.refs_1_), calls=%async_computation.1 | async-start | bytes 2621440 | tf_op jit(solution)/shard_map/all_to_all | solution.py:254
  114.7 4.0 %backward1.1 = (f32[2048,128]{1,0:T(8,128)S(1)}, f32[512,128]{1,0:T(8,128)S(1)}, f32[512,128]{1,0:T(8,128)S(1)}, f32[512,128]{1,0:T(8,128)S(1)}, f32[512,128]{1,0:T(8,128)S(1)}) custom-call(s32[256]{0:T(256)S(1)} %get-tuple-element.88.take, s32[256]{0:T(256)S(1)} %get-tuple-element.73.put, s32[1]{0:T(128)} %bitcast.10.count, f32[256,128,128]{2,1,0:T(8,128)} %bitcast.14, ...), custom_call_target="tpu_custom_call" | custom-call | tf_op jit(solution)/shard_map/backward1/pallas_call | solution.py:94
  122.4 1.9 %collective-permute-start.38 = (f32[512,128]{1,0:T(8,128)}, f32[512,128]{1,0:T(8,128)S(1)}, u32[]{:S(2)}, u32[]{:S(2)}) collective-permute-start(f32[512,128]{1,0:T(8,128)} %get-tuple-element.67), channel_id=1, source_target_pairs={{0,2},{2,4},{4,6},{6,0},{1,3},{3,5},{5,7},{7,1},{8,10},{10,12},{12... | collective-permute-start | bytes 786440 | tf_op jit(solution)/shard_map/ppermute | solution.py:237
  124.3 2.7 %collective-permute-start.39 = (f32[512,128]{1,0:T(8,128)}, f32[512,128]{1,0:T(8,128)S(1)}, u32[]{:S(2)}, u32[]{:S(2)}) collective-permute-start(f32[512,128]{1,0:T(8,128)} %get-tuple-element.68), channel_id=1, source_target_pairs={{0,4},{2,6},{4,0},{6,2},{1,5},{3,7},{5,1},{7,3},{8,12},{10,14},{12... | collective-permute-start | bytes 786440 | tf_op jit(solution)/shard_map/ppermute | solution.py:237
  128.5 2.5 %all-to-all-done.1.terms = f32[8,320,128]{2,1,0:T(8,128)S(1)} async-done(((f32[8,320,128]{2,1,0:T(8,128)}), f32[8,320,128]{2,1,0:T(8,128)S(1)}, u32[]{:S(2)}, u32[]{:S(2)}) %all-to-all-start.1) | async-done | bytes 1310752 | tf_op jit(solution)/shard_map/all_to_all | solution.py:254
  131.7 5.0 %all-to-all-start.2 = ((f32[8,64,128]{2,1,0:T(8,128)}), f32[8,64,128]{2,1,0:T(8,128)S(1)}, u32[]{:S(2)}, u32[]{:S(2)}) async-start(f32[8,64,128]{2,1,0:T(8,128)} %broadcast_in_dim.13), calls=%async_computation.2 | async-start | bytes 524288 | tf_op jit(solution)/shard_map/all_to_all | solution.py:254
  136.7 4.9 %collective-permute-done.39.refs_2_ = f32[512,128]{1,0:T(8,128)S(1)} collective-permute-done((f32[512,128]{1,0:T(8,128)}, f32[512,128]{1,0:T(8,128)S(1)}, u32[]{:S(2)}, u32[]{:S(2)}) %collective-permute-start.39) | collective-permute-done | bytes 262176 | tf_op jit(solution)/shard_map/ppermute | solution.py:237
  143.2 3.5 %collective-permute-done.41.refs_1_ = f32[256,128]{1,0:T(8,128)S(1)} collective-permute-done((f32[256,128]{1,0:T(8,128)S(1)}, f32[256,128]{1,0:T(8,128)S(1)}, u32[]{:S(2)}, u32[]{:S(2)}) %collective-permute-start.41) | collective-permute-done | bytes 131104 | tf_op jit(solution)/shard_map/ppermute | solution.py:232
  (87 shorter events, 32.3 us)
Async XLA Ops:
  1.6 8.2 %collective-permute-start.3 = (f32[256,128]{1,0:T(8,128)S(1)}, f32[256,128]{1,0:T(8,128)S(1)}, u32[]{:S(2)}, u32[]{:S(2)}) collective-permute-start(f32[256,128]{1,0:T(8,128)S(1)} %get-tuple-element.78.refs_0_), channel_id=1, source_target_pairs={{0,8},{8,0},{1,9},{9,1},{2,10},{10,2},{3,11},{11,3},{4,12},{12,4},... | collective-permute-start | bytes 393224 | tf_op jit(solution)/shard_map/ppermute | solution.py:232
  3.3 9.2 %collective-permute-start = (f32[256,128]{1,0:T(8,128)S(1)}, f32[256,128]{1,0:T(8,128)S(1)}, u32[]{:S(2)}, u32[]{:S(2)}) collective-permute-start(f32[256,128]{1,0:T(8,128)S(1)} %get-tuple-element.78.refs_0_), channel_id=1, source_target_pairs={{0,2},{2,4},{4,6},{6,0},{1,3},{3,5},{5,7},{7,1},{8,10},{10,12},{12... | collective-permute-start | bytes 393224 | tf_op jit(solution)/shard_map/ppermute | solution.py:237
  5.2 10.8 %collective-permute-start.1 = (f32[256,128]{1,0:T(8,128)S(1)}, f32[256,128]{1,0:T(8,128)S(1)}, u32[]{:S(2)}, u32[]{:S(2)}) collective-permute-start(f32[256,128]{1,0:T(8,128)S(1)} %get-tuple-element.78.refs_0_), channel_id=1, source_target_pairs={{0,4},{2,6},{4,0},{6,2},{1,5},{3,7},{5,1},{7,3},{8,12},{10,14},{12... | collective-permute-start | bytes 393224 | tf_op jit(solution)/shard_map/ppermute | solution.py:237
  8.8 7.8 %collective-permute-start.2 = (f32[256,128]{1,0:T(8,128)S(1)}, f32[256,128]{1,0:T(8,128)S(1)}, u32[]{:S(2)}, u32[]{:S(2)}) collective-permute-start(f32[256,128]{1,0:T(8,128)S(1)} %get-tuple-element.78.refs_0_), channel_id=1, source_target_pairs={{0,6},{2,0},{4,2},{6,4},{1,7},{3,1},{5,3},{7,5},{8,14},{10,8},{12,... | collective-permute-start | bytes 393224 | tf_op jit(solution)/shard_map/ppermute | solution.py:237
  9.8 8.1 %collective-permute-start.4 = (f32[256,128]{1,0:T(8,128)S(1)}, f32[256,128]{1,0:T(8,128)S(1)}, u32[]{:S(2)}, u32[]{:S(2)}) collective-permute-start(f32[256,128]{1,0:T(8,128)S(1)} %collective-permute-done.3.refs_0_), channel_id=1, source_target_pairs={{0,2},{2,4},{4,6},{6,0},{1,3},{3,5},{5,7},{7,1},{8,10},{10,12},{12... | collective-permute-start | bytes 393224 | tf_op jit(solution)/shard_map/ppermute | solution.py:237
  10.8 9.3 %collective-permute-start.5 = (f32[256,128]{1,0:T(8,128)S(1)}, f32[256,128]{1,0:T(8,128)S(1)}, u32[]{:S(2)}, u32[]{:S(2)}) collective-permute-start(f32[256,128]{1,0:T(8,128)S(1)} %collective-permute-done.3.refs_0_), channel_id=1, source_target_pairs={{0,4},{2,6},{4,0},{6,2},{1,5},{3,7},{5,1},{7,3},{8,12},{10,14},{12... | collective-permute-start | bytes 393224 | tf_op jit(solution)/shard_map/ppermute | solution.py:237
  16.6 9.4 %collective-permute-start.7 = (f32[1024,128]{1,0:T(8,128)S(1)}, f32[1024,128]{1,0:T(8,128)S(1)}, u32[]{:S(2)}, u32[]{:S(2)}) collective-permute-start(f32[1024,128]{1,0:T(8,128)S(1)} %join0.1.refs_0_), channel_id=1, source_target_pairs={{0,1},{1,0},{2,3},{3,2},{4,5},{5,4},{6,7},{7,6},{8,9},{9,8},{10,11... | collective-permute-start | bytes 1572872 | tf_op jit(solution)/shard_map/ppermute | solution.py:232
  21.0 10.1 %collective-permute-start.13 = (f32[512,128]{1,0:T(8,128)S(1)}, f32[512,128]{1,0:T(8,128)S(1)}, u32[]{:S(2)}, u32[]{:S(2)}) collective-permute-start(f32[512,128]{1,0:T(8,128)S(1)} %pair1.1.refs_0_), channel_id=1, source_target_pairs={{0,2},{2,4},{4,6},{6,0},{1,3},{3,5},{5,7},{7,1},{8,10},{10,12},{12... | collective-permute-start | bytes 786440 | tf_op jit(solution)/shard_map/ppermute | solution.py:237
  22.2 14.7 %collective-permute-start.14 = (f32[512,128]{1,0:T(8,128)S(1)}, f32[512,128]{1,0:T(8,128)S(1)}, u32[]{:S(2)}, u32[]{:S(2)}) collective-permute-start(f32[512,128]{1,0:T(8,128)S(1)} %pair1.1.refs_0_), channel_id=1, source_target_pairs={{0,4},{2,6},{4,0},{6,2},{1,5},{3,7},{5,1},{7,3},{8,12},{10,14},{12... | collective-permute-start | bytes 786440 | tf_op jit(solution)/shard_map/ppermute | solution.py:237
  24.6 12.6 %collective-permute-start.15 = (f32[512,128]{1,0:T(8,128)S(1)}, f32[512,128]{1,0:T(8,128)S(1)}, u32[]{:S(2)}, u32[]{:S(2)}) collective-permute-start(f32[512,128]{1,0:T(8,128)S(1)} %pair1.1.refs_0_), channel_id=1, source_target_pairs={{0,6},{2,0},{4,2},{6,4},{1,7},{3,1},{5,3},{7,5},{8,14},{10,8},{12,... | collective-permute-start | bytes 786440 | tf_op jit(solution)/shard_map/ppermute | solution.py:237
  37.4 13.2 %collective-permute-start.9 = (f32[512,128]{1,0:T(8,128)S(1)}, f32[512,128]{1,0:T(8,128)S(1)}, u32[]{:S(2)}, u32[]{:S(2)}) collective-permute-start(f32[512,128]{1,0:T(8,128)S(1)} %get-tuple-element.39), channel_id=1, source_target_pairs={{0,32},{32,64},{64,96},{96,0},{1,33},{33,65},{65,97},{97,1},{2,34}... | collective-permute-start | bytes 786440 | tf_op jit(solution)/shard_map/ppermute | solution.py:237
  39.0 15.6 %collective-permute-start.10 = (f32[512,128]{1,0:T(8,128)S(1)}, f32[512,128]{1,0:T(8,128)S(1)}, u32[]{:S(2)}, u32[]{:S(2)}) collective-permute-start(f32[512,128]{1,0:T(8,128)S(1)} %get-tuple-element.40), channel_id=1, source_target_pairs={{0,64},{32,96},{64,0},{96,32},{1,65},{33,97},{65,1},{97,33},{2,66}... | collective-permute-start | bytes 786440 | tf_op jit(solution)/shard_map/ppermute | solution.py:237
  41.9 13.4 %collective-permute-start.11 = (f32[512,128]{1,0:T(8,128)S(1)}, f32[512,128]{1,0:T(8,128)S(1)}, u32[]{:S(2)}, u32[]{:S(2)}) collective-permute-start(f32[512,128]{1,0:T(8,128)S(1)} %get-tuple-element.41), channel_id=1, source_target_pairs={{0,96},{32,0},{64,32},{96,64},{1,97},{33,1},{65,33},{97,65},{2,98}... | collective-permute-start | bytes 786440 | tf_op jit(solution)/shard_map/ppermute | solution.py:237
  47.1 13.7 %collective-permute-start.17 = (f32[256,128]{1,0:T(8,128)S(1)}, f32[256,128]{1,0:T(8,128)S(1)}, u32[]{:S(2)}, u32[]{:S(2)}) collective-permute-start(f32[256,128]{1,0:T(8,128)S(1)} %get-tuple-element.42), channel_id=1, source_target_pairs={{0,16},{16,0},{32,48},{48,32},{64,80},{80,64},{96,112},{112,96},{1... | collective-permute-start | bytes 393224 | tf_op jit(solution)/shard_map/ppermute | solution.py:250
  49.9 11.0 %collective-permute-start.19 = (f32[256,128]{1,0:T(8,128)S(1)}, f32[256,128]{1,0:T(8,128)S(1)}, u32[]{:S(2)}, u32[]{:S(2)}) collective-permute-start(f32[256,128]{1,0:T(8,128)S(1)} %get-tuple-element.46), channel_id=1, source_target_pairs={{0,32},{16,48},{32,64},{48,80},{64,96},{80,112},{96,0},{112,16},{1... | collective-permute-start | bytes 393224 | tf_op jit(solution)/shard_map/ppermute | solution.py:250
  50.6 12.5 %collective-permute-start.20 = (f32[256,128]{1,0:T(8,128)S(1)}, f32[256,128]{1,0:T(8,128)S(1)}, u32[]{:S(2)}, u32[]{:S(2)}) collective-permute-start(f32[256,128]{1,0:T(8,128)S(1)} %get-tuple-element.47), channel_id=1, source_target_pairs={{0,48},{16,32},{32,80},{48,64},{64,112},{80,96},{96,16},{112,0},{1... | collective-permute-start | bytes 393224 | tf_op jit(solution)/shard_map/ppermute | solution.py:250
  54.6 10.8 %collective-permute-start.21 = (f32[256,128]{1,0:T(8,128)S(1)}, f32[256,128]{1,0:T(8,128)S(1)}, u32[]{:S(2)}, u32[]{:S(2)}) collective-permute-start(f32[256,128]{1,0:T(8,128)S(1)} %get-tuple-element.48), channel_id=1, source_target_pairs={{0,64},{16,80},{32,96},{48,112},{64,0},{80,16},{96,32},{112,48},{1... | collective-permute-start | bytes 393224 | tf_op jit(solution)/shard_map/ppermute | solution.py:250
  55.3 10.1 %collective-permute-start.22 = (f32[256,128]{1,0:T(8,128)S(1)}, f32[256,128]{1,0:T(8,128)S(1)}, u32[]{:S(2)}, u32[]{:S(2)}) collective-permute-start(f32[256,128]{1,0:T(8,128)S(1)} %get-tuple-element.49), channel_id=1, source_target_pairs={{0,80},{16,64},{32,112},{48,96},{64,16},{80,0},{96,48},{112,32},{1... | collective-permute-start | bytes 393224 | tf_op jit(solution)/shard_map/ppermute | solution.py:250
  60.8 8.9 %collective-permute-start.23 = (f32[256,128]{1,0:T(8,128)S(1)}, f32[256,128]{1,0:T(8,128)S(1)}, u32[]{:S(2)}, u32[]{:S(2)}) collective-permute-start(f32[256,128]{1,0:T(8,128)S(1)} %get-tuple-element.50), channel_id=1, source_target_pairs={{0,96},{16,112},{32,0},{48,16},{64,32},{80,48},{96,64},{112,80},{1... | collective-permute-start | bytes 393224 | tf_op jit(solution)/shard_map/ppermute | solution.py:250
  60.9 8.9 %collective-permute-start.24 = (f32[256,128]{1,0:T(8,128)S(1)}, f32[256,128]{1,0:T(8,128)S(1)}, u32[]{:S(2)}, u32[]{:S(2)}) collective-permute-start(f32[256,128]{1,0:T(8,128)S(1)} %get-tuple-element.51), channel_id=1, source_target_pairs={{0,112},{16,96},{32,16},{48,0},{64,48},{80,32},{96,80},{112,64},{1... | collective-permute-start | bytes 393224 | tf_op jit(solution)/shard_map/ppermute | solution.py:250
  71.3 13.0 %collective-permute-start.32 = (f32[8,64,128]{2,1,0:T(8,128)S(1)}, f32[8,64,128]{2,1,0:T(8,128)S(1)}, u32[]{:S(2)}, u32[]{:S(2)}) collective-permute-start(f32[8,64,128]{2,1,0:T(8,128)S(1)} %get-tuple-element.55.refs_0_), channel_id=1, source_target_pairs={{0,1},{1,0},{2,3},{3,2},{4,5},{5,4},{6,7},{7,6},{8,9},{9,8},{10,11... | collective-permute-start | bytes 786440 | tf_op jit(solution)/shard_map/ppermute | solution.py:232
  73.9 10.4 %collective-permute-start.25 = (f32[256,128]{1,0:T(8,128)S(1)}, f32[256,128]{1,0:T(8,128)S(1)}, u32[]{:S(2)}, u32[]{:S(2)}) collective-permute-start(f32[256,128]{1,0:T(8,128)S(1)} %get-tuple-element.53.refs_0_), channel_id=1, source_target_pairs={{0,32},{32,64},{64,96},{96,0},{1,33},{33,65},{65,97},{97,1},{2,34}... | collective-permute-start | bytes 393224 | tf_op jit(solution)/shard_map/ppermute | solution.py:237
  75.1 15.7 %collective-permute-start.26 = (f32[256,128]{1,0:T(8,128)S(1)}, f32[256,128]{1,0:T(8,128)S(1)}, u32[]{:S(2)}, u32[]{:S(2)}) collective-permute-start(f32[256,128]{1,0:T(8,128)S(1)} %get-tuple-element.53.refs_0_), channel_id=1, source_target_pairs={{0,64},{32,96},{64,0},{96,32},{1,65},{33,97},{65,1},{97,33},{2,66}... | collective-permute-start | bytes 393224 | tf_op jit(solution)/shard_map/ppermute | solution.py:237
  76.3 14.6 %collective-permute-start.27 = (f32[256,128]{1,0:T(8,128)S(1)}, f32[256,128]{1,0:T(8,128)S(1)}, u32[]{:S(2)}, u32[]{:S(2)}) collective-permute-start(f32[256,128]{1,0:T(8,128)S(1)} %get-tuple-element.53.refs_0_), channel_id=1, source_target_pairs={{0,96},{32,0},{64,32},{96,64},{1,97},{33,1},{65,33},{97,65},{2,98}... | collective-permute-start | bytes 393224 | tf_op jit(solution)/shard_map/ppermute | solution.py:237
  78.7 12.1 %collective-permute-start.29 = (f32[256,128]{1,0:T(8,128)S(1)}, f32[256,128]{1,0:T(8,128)S(1)}, u32[]{:S(2)}, u32[]{:S(2)}) collective-permute-start(f32[256,128]{1,0:T(8,128)S(1)} %collective-permute-done.28.refs_4_), channel_id=1, source_target_pairs={{0,32},{32,64},{64,96},{96,0},{1,33},{33,65},{65,97},{97,1},{2,34}... | collective-permute-start | bytes 393224 | tf_op jit(solution)/shard_map/ppermute | solution.py:237
  85.5 23.2 %all-to-all-start = ((f32[8,320,128]{2,1,0:T(8,128)}), f32[8,320,128]{2,1,0:T(8,128)S(1)}, u32[]{:S(2)}, u32[]{:S(2)}) async-start(f32[8,320,128]{2,1,0:T(8,128)} %copies.1.refs_8_), calls=%async_computation | async-start | bytes 2621440 | tf_op jit(solution)/shard_map/all_to_all | solution.py:254
  95.8 12.9 %collective-permute-start.33 = (f32[2048,128]{1,0:T(8,128)}, f32[2048,128]{1,0:T(8,128)}, u32[]{:S(2)}, u32[]{:S(2)}) collective-permute-start(f32[2048,128]{1,0:T(8,128)} %get-tuple-element.57), channel_id=1, source_target_pairs={{0,1},{1,0},{2,3},{3,2},{4,5},{5,4},{6,7},{7,6},{8,9},{9,8},{10,11... | collective-permute-start | bytes 3145736 | tf_op jit(solution)/shard_map/ppermute | solution.py:232
  111.2 19.8 %all-to-all-start.1 = ((f32[8,320,128]{2,1,0:T(8,128)}), f32[8,320,128]{2,1,0:T(8,128)S(1)}, u32[]{:S(2)}, u32[]{:S(2)}) async-start(f32[8,320,128]{2,1,0:T(8,128)} %share0.1.refs_1_), calls=%async_computation.1 | async-start | bytes 2621440 | tf_op jit(solution)/shard_map/all_to_all | solution.py:254
  122.4 14.3 %collective-permute-start.38 = (f32[512,128]{1,0:T(8,128)}, f32[512,128]{1,0:T(8,128)S(1)}, u32[]{:S(2)}, u32[]{:S(2)}) collective-permute-start(f32[512,128]{1,0:T(8,128)} %get-tuple-element.67), channel_id=1, source_target_pairs={{0,2},{2,4},{4,6},{6,0},{1,3},{3,5},{5,7},{7,1},{8,10},{10,12},{12... | collective-permute-start | bytes 786440 | tf_op jit(solution)/shard_map/ppermute | solution.py:237
  124.3 17.3 %collective-permute-start.39 = (f32[512,128]{1,0:T(8,128)}, f32[512,128]{1,0:T(8,128)S(1)}, u32[]{:S(2)}, u32[]{:S(2)}) collective-permute-start(f32[512,128]{1,0:T(8,128)} %get-tuple-element.68), channel_id=1, source_target_pairs={{0,4},{2,6},{4,0},{6,2},{1,5},{3,7},{5,1},{7,3},{8,12},{10,14},{12... | collective-permute-start | bytes 786440 | tf_op jit(solution)/shard_map/ppermute | solution.py:237
  127.0 14.6 %collective-permute-start.40 = (f32[512,128]{1,0:T(8,128)}, f32[512,128]{1,0:T(8,128)S(1)}, u32[]{:S(2)}, u32[]{:S(2)}) collective-permute-start(f32[512,128]{1,0:T(8,128)} %get-tuple-element.69), channel_id=1, source_target_pairs={{0,6},{2,0},{4,2},{6,4},{1,7},{3,1},{5,3},{7,5},{8,14},{10,8},{12,... | collective-permute-start | bytes 786440 | tf_op jit(solution)/shard_map/ppermute | solution.py:237
  131.7 15.7 %all-to-all-start.2 = ((f32[8,64,128]{2,1,0:T(8,128)}), f32[8,64,128]{2,1,0:T(8,128)S(1)}, u32[]{:S(2)}, u32[]{:S(2)}) async-start(f32[8,64,128]{2,1,0:T(8,128)} %broadcast_in_dim.13), calls=%async_computation.2 | async-start | bytes 524288 | tf_op jit(solution)/shard_map/all_to_all | solution.py:254
  (16 other events, 130.6 us)
